TPU v7x, 256 devices: a whole 4x4x8 slice. The times are simulated.
256 devices in a mesh: eig: 64 (over y_hi, x, z), site: 4 (over y_lo, core).
Axes of the slice: x: 4, y: 4 (y_hi: 2, y_lo: 2; y = y_hi * 2 + y_lo), z: 8, core: 2. Of those that a mesh axis runs over, the one named last changes fastest.
Arguments:
- vectors: bfloat16 [2048, 102400], P('eig', 'site'), may hold values from -6 to 6
- rotation: bfloat16 [2048, 2048], P(('eig', 'site')), may hold values from -0.1875 to 0.1875
- locked: int32 [16], replicated, may hold values from 0 to 128
Outputs:
- rotated: bfloat16 [2048, 102400], P('eig', 'site')
All inputs are finite; a program needn't handle non-finite values.
Results may differ from a plain program's by a relative error of at most 0.001.
Values may be sent and summed in bfloat16 or wider, within the bound.
No kernel may reach another device: no remote copies, remote signals or barrier semaphores. Data moves between devices by JAX's collectives and lax.ppermute only.
A program may use at most 128 MiB of HBM per device.

v0:
```python
import jax
import jax.numpy as jnp
from jax import lax
from jax.sharding import PartitionSpec as P

BLOCK = 128


def effective_rows(panel, locked, block):
    count = panel.shape[0]
    width = panel.shape[1]
    rows = jnp.arange(count, dtype=jnp.int32)[:, None]
    cols = jnp.arange(width, dtype=jnp.int32)
    col_block = cols // block
    blocks = jnp.arange(locked.shape[0], dtype=jnp.int32)
    lock_cols = jnp.sum(
        jnp.where(col_block[:, None] == blocks[None, :], locked[None, :], 0), axis=1
    )
    is_locked = cols % block < lock_cols
    identity = jnp.where(rows == cols[None, :], 1.0, 0.0).astype(panel.dtype)
    lower = jnp.where(rows // block >= col_block[None, :], panel, jnp.zeros_like(panel))
    return jnp.where(is_locked[None, :], identity, lower)


def body(vectors, rotation, locked):
    columns = lax.all_to_all(vectors, "eig", split_axis=1, concat_axis=0, tiled=True)
    masked = effective_rows(
        lax.all_gather(rotation, ("eig", "site"), axis=0, tiled=True), locked, BLOCK
    )
    product = lax.dot_general(
        masked, columns, (((0,), (0,)), ((), ())), preferred_element_type=jnp.float32
    )
    rounded = product.astype(jnp.bfloat16)
    return lax.all_to_all(rounded, "eig", split_axis=0, concat_axis=1, tiled=True)


def solution(mesh):
    in_specs = (P("eig", "site"), P(("eig", "site"), None), P())
    out_specs = P("eig", "site")
    return jax.shard_map(body, mesh=mesh, in_specs=in_specs, out_specs=out_specs, check_vma=False)
```

profile of v0, /device:TPU:16, one launch (start us, length us, event | category | flops | bytes accessed | tf_op | source)
XLA Modules:
  0.0 521.1 jit_solution(10885002493717691680)
XLA Ops:
  6.5 0.0 all-gather.2.cloned.1.call-start
  6.5 0.7 all-gather.2.cloned.1.call-update
  7.3 5.7 %all_to_all.28 = bf16[32,64,400]{2,1,0:T(8,128)(2,1)S(1)} reshape(bf16[32,25600]{1,0:T(8,128)(2,1)} %param.3) | data formatting | bytes 3276800 | tf_op jit(solution)/shard_map/all_to_all | solution.py:26
  13.0 0.0 copy-start
  13.0 2.5 copy.10
  15.5 14.5 %all-to-all-start = ((bf16[32,64,400]{2,0,1:T(8,128)(2,1)}), bf16[32,64,400]{2,0,1:T(8,128)(2,1)S(1)}, u32[]{:S(2)}, u32[]{:S(2)}) async-start(bf16[32,64,400]{2,0,1:T(8,128)(2,1)} %copy.10), calls=%async_computation | async-start | bytes 4194304 | tf_op jit(solution)/shard_map/all_to_all | solution.py:26
  30.1 0.0 copy-done
  30.1 0.1 select_reduce_fusion
  30.2 55.3 %all-to-all-done = bf16[32,64,400]{2,0,1:T(8,128)(2,1)S(1)} async-done(((bf16[32,64,400]{2,0,1:T(8,128)(2,1)}), bf16[32,64,400]{2,0,1:T(8,128)(2,1)S(1)}, u32[]{:S(2)}, u32[]{:S(2)}) %all-to-all-start) | async-done | bytes 1638432 | tf_op jit(solution)/shard_map/all_to_all | solution.py:26
  85.5 350.0 %all-gather.2.cloned.1.call-done = bf16[2048,2048]{1,0:T(8,128)(2,1)} async-done(((bf16[8,2048]{1,0:T(8,128)(2,1)}), bf16[2048,2048]{1,0:T(8,128)(2,1)}) %all-gather.2.cloned.1.call-update) | async-done | bytes 8388624 | tf_op jit(solution)/shard_map/all_gather | solution.py:28
  435.5 8.7 %fusion.9 = bf16[2048,400]{0,1:T(8,128)(2,1)} fusion(bf16[2048,400]{1,0:T(8,128)(2,1)S(1)} %bitcast.8, bf16[2048,2048]{1,0:T(8,128)(2,1)} %all-gather.2.cloned.1.call-done, s32[2048]{0:T(1024)S(1)} %add_select_fusion, pred[2048]{0:T(1024)(128)(4,1)S(1)} %fusion.12), kind=kOutput, calls=%fused_computation.11 | convolution fusion | flops 3381428224 | bytes 11675648 | tf_op jit(solution)/shard_map/dot_general | solution.py:30
  444.2 2.8 copy.11
  447.0 62.6 %all_to_all.38 = bf16[64,32,400]{2,1,0:T(8,128)(2,1)S(1)} all-to-all(bf16[64,32,400]{2,1,0:T(8,128)(2,1)S(1)} %bitcast.6), channel_id=1, replica_groups=mesh['eig'=64,'site'=4] {'eig'}, dimensions={0} | all-to-all | bytes 3276800 | tf_op jit(solution)/shard_map/all_to_all | solution.py:34
  509.6 1.2 copy.12
  510.7 3.5 all_to_all.35
  (2 shorter events, 0.0 us)
Async XLA Ops:
  6.5 428.9 %all-gather.2.cloned.1.call-start = ((), (), s32[]{:S(2)}) async-start(), calls=%async_computation.2 | async-start | bytes 8421376 | tf_op jit(solution)/shard_map/all_gather | solution.py:28
  13.0 17.1 %copy-start = (s32[16]{0:T(128)S(1)}, s32[16]{0:T(128)}, u32[]{:S(2)}) copy-start(s32[16]{0:T(128)} %param.5) | copy-start | bytes 196
  15.5 69.9 %all-to-all-start = ((bf16[32,64,400]{2,0,1:T(8,128)(2,1)}), bf16[32,64,400]{2,0,1:T(8,128)(2,1)S(1)}, u32[]{:S(2)}, u32[]{:S(2)}) async-start(bf16[32,64,400]{2,0,1:T(8,128)(2,1)} %copy.10), calls=%async_computation | async-start | bytes 4194304 | tf_op jit(solution)/shard_map/all_to_all | solution.py:26
Sparse Core Ops, SparseCore 0:
  9.2 426.1 all-gather.1
where the time goes:
time: 523 us; the launch traced here: 521 us
  waiting for transfers between devices  406 us (78%)
  blocking collectives  62.6 us (12%)
  local copies, waits for them, and re-layouts  15.7 us (3%)
  starting transfers between devices  14.5 us (3%)
  between operations  13.5 us (3%)
  matrix products  8.74 us (2%)
    all_gather x1, waiting for transfers between devices, body(): lax.all_gather(rotation, ('eig', 'site'), axis=0, tiled=True)  350 us
    all_to_all x1, blocking collectives, body(): lax.all_to_all(rounded, 'eig', split_axis=0, concat_axis=1, tiled=True)  62.6 us
    all_to_all x1, waiting for transfers between devices, body(): lax.all_to_all(vectors, 'eig', split_axis=1, concat_axis=0, tiled=True)  55.3 us
    all_to_all x1, starting transfers between devices, body(): lax.all_to_all(vectors, 'eig', split_axis=1, concat_axis=0, tiled=True)  14.5 us
  transfers between devices with their start and end apart: 2, of which 2 were waited for; matrix products, arithmetic and copies ran while one was open for 1% of the time, Pallas kernels for 0%

commit v1 on v0

v1 whole, which is shorter than its diff:
```python
import jax
import jax.numpy as jnp
from jax import lax
from jax.experimental import pallas as pl
from jax.experimental.pallas import tpu as pltpu
from jax.sharding import Mesh, PartitionSpec as P

AXES = ("yh", "x", "z", "yl", "c")
EIG = ("yh", "x", "z")
SITE = ("yl", "c")
PEERS = 64
ROWS = 32
TILES = 3
CHUNK = 104
KEEP = 1152
WIDTH = 512
HALF = 1024
F32 = jnp.float32
BF16 = jnp.bfloat16


def lane_group():
    return lax.broadcasted_iota(jnp.int32, (8, 128), 1) // 16


def low_half():
    return lax.broadcasted_iota(jnp.int32, (8, 128), 0) < 4


def regroup(tile):
    low = low_half()
    groups = []
    for k in range(4):
        straight = tile[8 * k : 8 * k + 8]
        turned = pltpu.roll(straight, 4, 0)
        groups.append(jnp.where(low, straight, turned))
        groups.append(jnp.where(low, turned, straight))
    return groups


def gather_lanes(groups, place):
    lanes = lane_group()
    total = jnp.zeros((8, 128), F32)
    for h in range(8):
        total = jnp.where(lanes == h, pltpu.roll(groups[h], (16 * (h - place)) % 128, 1), total)
    return total


def pack_kernel(main_ref, left_ref, out_ref):
    def reorder(tile):
        tile = tile.astype(F32)
        return jnp.concatenate([tile[0:8], tile[16:24], tile[8:16], tile[24:32]], axis=0)

    for part in range(2):
        groups = regroup(reorder(left_ref[:, 128 * part : 128 * part + 128]))
        for m in range(8):
            peer = 8 * part + m
            for t in range(TILES):
                column = (TILES * peer + t) * 128
                out_ref[peer, 32 * t : 32 * t + 32, :] = reorder(main_ref[:, column : column + 128]).astype(BF16)
            out_ref[peer, 96:104, :] = gather_lanes(groups, m).astype(BF16)


def pack(vectors):
    return pl.pallas_call(
        pack_kernel,
        grid=(4,),
        in_specs=[
            pl.BlockSpec((ROWS, 6144), lambda t: (0, t)),
            pl.BlockSpec((ROWS, 256), lambda t: (0, 96 + t)),
        ],
        out_specs=pl.BlockSpec((16, CHUNK, 128), lambda t: (t, 0, 0)),
        out_shape=jax.ShapeDtypeStruct((PEERS, CHUNK, 128), BF16),
    )(vectors, vectors)


def unpack_kernel(in_ref, main_ref, left_ref):
    lanes, low = lane_group(), low_half()
    lefts = []
    for m in range(8):
        for t in range(TILES):
            column = (TILES * m + t) * 128
            main_ref[:, column : column + 128] = in_ref[m, 32 * t : 32 * t + 32, :]
        lefts.append(in_ref[m, 96:104, :].astype(F32))
    pieces = []
    for k in range(4):
        total = jnp.zeros((8, 128), F32)
        for m in range(8):
            piece = jnp.where(
                low,
                pltpu.roll(lefts[m], (16 * (m - 2 * k)) % 128, 1),
                pltpu.roll(lefts[m], (16 * (m - 2 * k - 1)) % 128, 1),
            )
            total = jnp.where(lanes == m, piece, total)
        pieces.append(total)
    left_ref[...] = jnp.concatenate(pieces, axis=0).astype(BF16)


def unpack_body(in_ref, out_ref):
    for t in range(8):
        unpack_kernel(
            in_ref.at[pl.ds(8 * t, 8)],
            out_ref.at[:, pl.ds(3072 * t, 3072)],
            out_ref.at[:, pl.ds(24576 + 128 * t, 128)],
        )


def unpack(received):
    return pl.pallas_call(
        unpack_body,
        out_shape=jax.ShapeDtypeStruct((ROWS, 25600), BF16),
        compiler_params=pltpu.CompilerParams(vmem_limit_bytes=32 * 1024 * 1024),
    )(received)


def place_kernel(place_ref, *refs):
    panels, out_ref = refs[:12], refs[12]
    core, yh, x, z = (place_ref[i] for i in range(4))
    for side in range(2):
        half = core if side == 0 else 1 - core
        for first in range(2):
            for dx in range(4):
                group = (yh ^ first) * 4 + (x ^ dx)
                for step in range(8):
                    source, at = (panels[6 * side + first], dx) if step < 4 else (panels[6 * side + 2 + dx], first)
                    row = 16 * (step % 4)
                    out_ref[half, group * 8 + (z ^ step)] = source[at, row : row + 16, :]
    for group in range(8):
        slot, column = (group, 256 * group + 128) if group < 4 else (7 - group, 256 * (8 - group) + 128 * (2 * group - 8))
        for half in range(2):
            out_ref[half, 8 * slot : 8 * slot + 4, :, column : column + 128] = jnp.zeros((4, 16, 128), BF16)


def place_panels(place, panels):
    vmem = pl.BlockSpec(memory_space=pltpu.VMEM)
    return pl.pallas_call(
        place_kernel,
        in_specs=[pl.BlockSpec(memory_space=pltpu.SMEM)] + [vmem] * 12,
        out_specs=vmem,
        out_shape=jax.ShapeDtypeStruct((2, PEERS, 16, KEEP), BF16),
        compiler_params=pltpu.CompilerParams(vmem_limit_bytes=16 * 1024 * 1024),
    )(place, *panels)


def rotate_kernel(locked_ref, in_ref, source_ref, out_ref, held, matrix_ref, sems):
    copies = []
    for index, width in enumerate((256, 256, 256, 256, 128)):
        columns = (slice(None), slice(None), slice(None), pl.ds(256 * index, width))
        copies.append(pltpu.make_async_copy(source_ref.at[columns], matrix_ref.at[columns], sems.at[index]))
        copies[-1].start()
    low64 = lax.broadcasted_iota(jnp.int32, (64, 128), 0) % 8 < 4
    for group in range(8):
        rows = slice(128 * group, 128 * group + 128)
        left = in_ref[:, group, 96:104, :].astype(F32).reshape(64, 128)
        for half in range(2):
            parts = []
            for k in (2 * half, 2 * half + 1):
                a = pltpu.roll(left, (-32 * k) % 128, 1)
                b = pltpu.roll(left, (-32 * k - 16) % 128, 1)
                parts.append(jnp.where(low64, a, b).reshape(8, 8, 128))
            held[half, rows, 384:512] = jnp.stack(parts, axis=1).reshape(128, 128).astype(BF16)
            for t in range(TILES):
                part = in_ref[:, group, 32 * t + 16 * half : 32 * t + 16 * half + 16, :]
                held[half, rows, 128 * t : 128 * t + 128] = part.reshape(128, 128)

    def product(lhs, rhs):
        return lax.dot_general(lhs, rhs, (((0,), (0,)), ((), ())), preferred_element_type=F32)

    def natural(first, second):
        pair = [v.astype(F32).reshape(8, 2, 1, 8, 128) for v in (first, second)]
        return jnp.concatenate(pair, axis=2).reshape(256, 128)

    for block in range(8):
        for copy in copies[block : block + 1]:
            copy.wait()
        total = None
        for half in range(2):

            def panel(group, column, width, groups=1):
                return matrix_ref[half, 8 * group : 8 * (group + groups), :, column : column + width].reshape(128 * groups, width)

            terms = []
            if block < 4:
                terms.append((panel(block, 256 * block, 256, 8 - block), held[half, 128 * block : HALF, :]))
            for peer in range(block, 8) if block >= 4 else ():
                at = 256 * (8 - peer) + 128 * (2 * block - 9)
                if block == 4:
                    lhs = jnp.concatenate([panel(peer, 1024, 128), panel(7 - peer, at + 128, 128)], axis=1)
                else:
                    lhs = panel(7 - peer, at, 256)
                terms.append((lhs, held[half, 128 * peer : 128 * peer + 128, :]))
            for lhs, rhs in terms:
                term = product(lhs, rhs)
                total = term if total is None else total + term
        rows = lax.broadcasted_iota(jnp.int32, (256, 1), 0)
        limit = jnp.where(rows < 128, locked_ref[2 * block], locked_ref[2 * block + 1])
        kept = rows % 128 < limit
        peers = slice(8 * block, 8 * block + 8)
        for t in range(TILES):
            mine = natural(*(in_ref[:, block, 32 * t + at : 32 * t + at + 16, :] for at in (0, 16)))
            result = jnp.where(kept, mine, total[:, 128 * t : 128 * t + 128]).astype(BF16)
            out_ref[peers, 32 * t : 32 * t + 32, :] = result.reshape(8, 32, 128)
        mine = natural(held[0, 128 * block : 128 * block + 128, 384:512], held[1, 128 * block : 128 * block + 128, 384:512])
        result = jnp.where(kept, mine, total[:, 384:512]).astype(BF16).astype(F32)
        for m in range(8):
            groups = regroup(result[32 * m : 32 * m + 32])
            out_ref[8 * block + m, 96:104, :] = gather_lanes(groups, 0).astype(BF16)


def rotate(locked, received, matrix):
    vmem = pl.BlockSpec(memory_space=pltpu.VMEM)
    return pl.pallas_call(
        rotate_kernel,
        in_specs=[pl.BlockSpec(memory_space=pltpu.SMEM), vmem, pl.BlockSpec(memory_space=pl.ANY)],
        out_specs=vmem,
        out_shape=jax.ShapeDtypeStruct((PEERS, CHUNK, 128), BF16),
        scratch_shapes=[
            pltpu.VMEM((2, HALF, WIDTH), BF16),
            pltpu.VMEM((2, PEERS, 16, KEEP), BF16),
            pltpu.SemaphoreType.DMA((5,)),
        ],
        compiler_params=pltpu.CompilerParams(vmem_limit_bytes=56 * 1024 * 1024),
    )(locked, received, matrix)


def exchange(value, axis, size, mask):
    return lax.ppermute(value, axis, [(i, i ^ mask) for i in range(size)])


def gather_near(rotation):
    rows = rotation[None]
    rows = jnp.concatenate([rows] + [exchange(rows, "z", 8, step) for step in (1, 2, 3)])
    late = [i for i in range(PEERS) if i >= 32]
    spare = rows[:, :, KEEP:]
    guests = [lax.ppermute(spare, EIG, [(i, (7 - i // 8) * 8 + (i % 8 ^ far)) for i in late]) for far in (0, 4)]
    return rows[:, :, :KEEP], exchange(rows[:, :, :KEEP], "z", 8, 4), *guests


def gather_panels(near, far, *guests):
    eig, yl = lax.axis_index(EIG), lax.axis_index("yl")
    group = eig // 8
    rows = jnp.concatenate([near, far])
    place = 256 * (group + 1)
    guest = jnp.concatenate([jnp.concatenate(guests), jnp.zeros((8, 8, KEEP), BF16)], axis=2)
    guest = lax.dynamic_update_slice(jnp.zeros((8, 8, 4096), BF16), guest, (0, 0, place))[:, :, :KEEP]
    cols = lax.broadcasted_iota(jnp.int32, (1, 1, KEEP), 2)
    rows = jnp.where((group >= 4) | (cols < place), rows, guest)
    other = exchange(rows, "yl", 2, 1)
    rows = jnp.where(yl == 0, jnp.stack([rows, other], axis=1), jnp.stack([other, rows], axis=1))

    a, b = rows[:4].reshape(1, 64, KEEP), rows[4:].reshape(1, 64, KEEP)
    b = jnp.concatenate([b, exchange(b, "yh", 2, 1)])
    a = jnp.concatenate([a] + [exchange(a, "x", 4, dx) for dx in (1, 2, 3)])
    far_a = exchange(a, "yh", 2, 1)
    far_b = [exchange(b, "x", 4, dx) for dx in (1, 2, 3)]
    a, b, far_a = lax.optimization_barrier((a, b, far_a))
    own = [a, far_a, b] + far_b
    return own + [exchange(panel, "c", 2, 1) for panel in own]


def body(vectors, rotation, locked):
    packed = pack(vectors).reshape(8, 8, CHUNK, 128)
    halfway = lax.all_to_all(packed, ("yh", "x"), split_axis=0, concat_axis=0, tiled=True)
    near, far, *guests = gather_near(rotation)
    halfway, near, far = lax.optimization_barrier((halfway, near, far))
    place = jnp.stack([lax.axis_index(name) for name in ("c", "yh", "x", "z")]).astype(jnp.int32)
    matrix = place_panels(place, gather_panels(near, far, *guests))
    received = lax.all_to_all(halfway.transpose(1, 0, 2, 3), "z", split_axis=0, concat_axis=0, tiled=True)
    back = lax.all_to_all(rotate(locked, received, matrix), EIG, split_axis=0, concat_axis=0, tiled=True)
    return unpack(back)


def solution(mesh):
    fine = Mesh(mesh.devices.reshape(2, 4, 8, 2, 2), AXES)
    in_specs = (P(EIG, SITE), P(EIG + SITE, None), P())
    return jax.shard_map(body, mesh=fine, in_specs=in_specs, out_specs=P(EIG, SITE), check_vma=False)
```

time: 523 us -> 151 us (0.29)
  waiting for transfers between devices: 406 us -> 31 us
  starting transfers between devices: 14.5 us -> 43.3 us
  Pallas kernels: 0 us -> 15.7 us
  between operations: 13.5 us -> 0.16 us
  local copies, waits for them, and re-layouts: 15.7 us -> 5.27 us
  blocking collectives: 62.6 us -> 53.7 us
  matrix products: 8.74 us -> 0 us
    all_gather x1 -> x0, waiting for transfers between devices: 350 us -> none  [body(): lax.all_gather(rotation, ('eig', 'site'), axis=0, tiled=True)]
    all_to_all x1 -> x2, waiting for transfers between devices: 55.3 us -> 1.5 us  [the longest x1 1.49 us: body(): lax.all_to_all(halfway.transpose(1, 0, 2, 3), 'z', split_axis=0, concat_a...]
    ppermute x0 -> x21, starting transfers between devices: none -> 31.6 us  [the longest x19 21.7 us: exchange(): return lax.ppermute(value, axis, [(i, i ^ mask) for i in range(size)])]
    ppermute x0 -> x21, waiting for transfers between devices: none -> 29.5 us  [the longest x19 29.5 us: exchange(): return lax.ppermute(value, axis, [(i, i ^ mask) for i in range(size)])]
    pallas_call x0 -> x4, Pallas kernels: none -> 15.7 us  [the longest x1 8.57 us: rotate(): pl.pallas_call(rotate_kernel, in_specs=[pl.BlockSpec(memory_space=pltpu.S...]
    all_to_all x4 -> x0, local copies, waits for them, and re-layouts: 12.9 us -> none  [the longest x2 8.25 us: body(): lax.all_to_all(vectors, 'eig', split_axis=1, concat_axis=0, tiled=True)]
    all_to_all x1, blocking collectives: 62.6 us -> 53.7 us  [body(): lax.all_to_all(rotate(locked, received, matrix), EIG, split_axis=0, conca...]
    dot_general x1 -> x0, matrix products: 8.74 us -> none  [body(): lax.dot_general(masked, columns, (((0,), (0,)), ((), ())), preferred_elem...]
  transfers between devices with their start and end apart: 2 -> 23, of which waited for: 2 -> 13; matrix products, arithmetic and copies ran while one was open for 1% -> 1% of each run, Pallas kernels for 0% -> 1%
where the time goes in v1:
time: 151 us; the launch traced here: 149 us
  blocking collectives  53.7 us (36%)
  starting transfers between devices  43.3 us (29%)
  waiting for transfers between devices  31 us (21%)
  Pallas kernels  15.7 us (10%)
  local copies, waits for them, and re-layouts  5.27 us (3%)
    all_to_all x1, blocking collectives, body(): lax.all_to_all(rotate(locked, received, matrix), EIG, split_axis=0, conca...  53.7 us
    ppermute x19, waiting for transfers between devices, exchange(): return lax.ppermute(value, axis, [(i, i ^ mask) for i in range(size)])  29.5 us
    ppermute x19, starting transfers between devices, exchange(): return lax.ppermute(value, axis, [(i, i ^ mask) for i in range(size)])  21.7 us
    ppermute x2, starting transfers between devices, gather_near(): lax.ppermute(spare, EIG, [(i, (7 - i // 8) * 8 + (i % 8 ^ far)) for i in...  9.82 us
    pallas_call x1, Pallas kernels, rotate(): pl.pallas_call(rotate_kernel, in_specs=[pl.BlockSpec(memory_space=pltpu.S...  8.57 us
    all_to_all x1, starting transfers between devices, body(): lax.all_to_all(packed, ('yh', 'x'), split_axis=0, concat_axis=0, tiled=True)  7.39 us
    all_to_all x1, starting transfers between devices, body(): lax.all_to_all(halfway.transpose(1, 0, 2, 3), 'z', split_axis=0, concat_a...  4.31 us
    pallas_call x1, Pallas kernels, pack(): pl.pallas_call(pack_kernel, grid=(4,), in_specs=[pl.BlockSpec((ROWS, 6144...  3.82 us
  transfers between devices with their start and end apart: 23, of which 13 were waited for; matrix products, arithmetic and copies ran while one was open for 1% of the time, Pallas kernels for 1%

profile of v1, /device:TPU:16, one launch (start us, length us, event | category | flops | bytes accessed | tf_op | source)
XLA Modules:
  0.0 149.4 jit_solution(5676910315616280807)
XLA Ops:
  0.0 3.8 %shard_map.37 = bf16[64,104,128]{2,1,0:T(8,128)(2,1)} custom-call(bf16[32,25600]{1,0:T(8,128)(2,1)} %left_ref.1, bf16[32,25600]{1,0:T(8,128)(2,1)} %left_ref.1), custom_call_target="tpu_custom_call" | custom-call | tf_op jit(solution)/shard_map/pallas_call | solution.py:65
  3.8 0.0 copy-start.3
  3.8 7.4 %all-to-all-start = ((bf16[8,8,104,128]{3,2,1,0:T(8,128)(2,1)}), bf16[8,8,104,128]{3,2,1,0:T(8,128)(2,1)S(1)}, u32[]{:S(2)}, u32[]{:S(2)}) async-start(bf16[8,8,104,128]{3,2,1,0:T(8,128)(2,1)} %bitcast.13), calls=%async_computation | async-start | bytes 3407872 | tf_op jit(solution)/shard_map/all_to_all | solution.py:263
  11.2 0.0 copy-done.3
  11.2 4.6 %collective-permute-start.2 = (bf16[1,8,2048]{2,1,0:T(8,128)(2,1)S(1)}, bf16[1,8,2048]{2,1,0:T(8,128)(2,1)S(1)}, u32[]{:S(2)}, u32[]{:S(2)}) collective-permute-start(bf16[1,8,2048]{2,1,0:T(8,128)(2,1)S(1)} %bitcast.22), channel_id=1, source_target_pairs={{0,12},{4,8},{8,4},{12,0},{16,28},{20,24},{24,20},{28,16},{1,13},{... | collective-permute-start | bytes 98312 | tf_op jit(solution)/shard_map/ppermute | solution.py:227
  15.8 0.0 collective-permute-start.1
  15.8 0.7 collective-permute-start
  16.5 1.3 collective-permute-done.2
  17.8 2.9 %collective-permute-done.1 = bf16[1,8,2048]{2,1,0:T(8,128)(2,1)S(1)} collective-permute-done((bf16[1,8,2048]{2,1,0:T(8,128)(2,1)S(1)}, bf16[1,8,2048]{2,1,0:T(8,128)(2,1)S(1)}, u32[]{:S(2)}, u32[]{:S(2)}) %collective-permute-start.1) | collective-permute-done | bytes 32800 | tf_op jit(solution)/shard_map/ppermute | solution.py:227
  20.7 0.0 collective-permute-done
  20.7 8.5 %collective-permute-start.5 = (bf16[4,8,896]{2,1,0:T(8,128)(2,1)S(1)}, bf16[4,8,896]{2,1,0:T(8,128)(2,1)S(1)}, u32[]{:S(2)}, u32[]{:S(2)}) collective-permute-start(bf16[4,8,896]{2,1,0:T(8,128)(2,1)S(1)} %pad_maximum_fusion.3), channel_id=1, source_target_pairs={{128,112},{132,116},{136,120},{140,124},{144,96},{148,100},{152,10... | collective-permute-start | bytes 172040 | tf_op jit(solution)/shard_map/ppermute | solution.py:235
  29.2 1.3 collective-permute-start.4
  30.6 1.5 %collective-permute-start.3 = (bf16[4,8,1152]{2,1,0:T(8,128)(2,1)S(1)}, bf16[4,8,1152]{2,1,0:T(8,128)(2,1)S(1)}, u32[]{:S(2)}, u32[]{:S(2)}) collective-permute-start(bf16[4,8,1152]{2,1,0:T(8,128)(2,1)S(1)} %slice.21), channel_id=1, source_target_pairs={{0,16},{4,20},{8,24},{12,28},{16,0},{20,4},{24,8},{28,12},{1,17},{... | collective-permute-start | bytes 221192 | tf_op jit(solution)/shard_map/ppermute | solution.py:227
  32.1 7.3 %collective-permute-done.3 = bf16[4,8,1152]{2,1,0:T(8,128)(2,1)S(1)} collective-permute-done((bf16[4,8,1152]{2,1,0:T(8,128)(2,1)S(1)}, bf16[4,8,1152]{2,1,0:T(8,128)(2,1)S(1)}, u32[]{:S(2)}, u32[]{:S(2)}) %collective-permute-start.3) | collective-permute-done | bytes 73760 | tf_op jit(solution)/shard_map/ppermute | solution.py:227
  39.4 0.0 all-to-all-done
  39.4 1.4 copy.13
  40.7 4.3 %all-to-all-start.1 = ((bf16[8,8,104,128]{3,2,1,0:T(8,128)(2,1)}), bf16[8,8,104,128]{3,2,1,0:T(8,128)(2,1)}, u32[]{:S(2)}, u32[]{:S(2)}) async-start(bf16[8,8,104,128]{3,2,1,0:T(8,128)(2,1)} %bitcast.12), calls=%async_computation.1 | async-start | bytes 3407872 | tf_op jit(solution)/shard_map/all_to_all | solution.py:268
  45.0 0.0 collective-permute-done.5
  45.1 0.0 collective-permute-done.4
  45.2 1.4 collective-permute-start.6
  46.5 3.9 %collective-permute-done.6 = bf16[8,8,1152]{2,1,0:T(8,128)(2,1)S(1)} collective-permute-done((bf16[8,8,1152]{2,1,0:T(8,128)(2,1)S(1)}, bf16[8,8,1152]{2,1,0:T(8,128)(2,1)S(1)}, u32[]{:S(2)}, u32[]{:S(2)}) %collective-permute-start.6) | collective-permute-done | bytes 147488 | tf_op jit(solution)/shard_map/ppermute | solution.py:227
  50.5 1.1 collective-permute-start.9
  51.6 1.3 collective-permute-start.8
  52.9 1.8 %collective-permute-start.7 = (bf16[1,64,1152]{2,1,0:T(8,128)(2,1)S(1)}, bf16[1,64,1152]{2,1,0:T(8,128)(2,1)S(1)}, u32[]{:S(2)}, u32[]{:S(2)}) collective-permute-start(bf16[1,64,1152]{2,1,0:T(8,128)(2,1)S(1)} %bitcast.16), channel_id=1, source_target_pairs={{0,32},{32,0},{64,96},{96,64},{1,33},{33,1},{65,97},{97,65},{2,34}... | collective-permute-start | bytes 442376 | tf_op jit(solution)/shard_map/ppermute | solution.py:227
  54.7 2.0 %collective-permute-start.10 = (bf16[1,64,1152]{2,1,0:T(8,128)(2,1)S(1)}, bf16[1,64,1152]{2,1,0:T(8,128)(2,1)S(1)}, u32[]{:S(2)}, u32[]{:S(2)}) collective-permute-start(bf16[1,64,1152]{2,1,0:T(8,128)(2,1)S(1)} %bitcast.19), channel_id=1, source_target_pairs={{0,128},{128,0},{1,129},{129,1},{2,130},{130,2},{3,131},{131,3},{4... | collective-permute-start | bytes 442376 | tf_op jit(solution)/shard_map/ppermute | solution.py:227
  56.7 1.8 %collective-permute-done.9 = bf16[1,64,1152]{2,1,0:T(8,128)(2,1)S(1)} collective-permute-done((bf16[1,64,1152]{2,1,0:T(8,128)(2,1)S(1)}, bf16[1,64,1152]{2,1,0:T(8,128)(2,1)S(1)}, u32[]{:S(2)}, u32[]{:S(2)}) %collective-permute-start.9) | collective-permute-done | bytes 147488 | tf_op jit(solution)/shard_map/ppermute | solution.py:227
  58.5 0.0 collective-permute-done.8
  58.5 0.9 collective-permute-done.7
  59.4 0.1 pad_maximum_fusion.refs_0_
  59.5 2.0 %collective-permute-start.11 = (bf16[4,64,1152]{2,1,0:T(8,128)(2,1)S(1)}, bf16[4,64,1152]{2,1,0:T(8,128)(2,1)S(1)}, u32[]{:S(2)}, u32[]{:S(2)}) collective-permute-start(bf16[4,64,1152]{2,1,0:T(8,128)(2,1)S(1)} %pad_maximum_fusion.refs_0_), channel_id=1, source_target_pairs={{0,128},{128,0},{1,129},{129,1},{2,130},{130,2},{3,131},{131,3},{4... | collective-permute-start | bytes 1769480 | tf_op jit(solution)/shard_map/ppermute | solution.py:227
  61.5 1.5 %collective-permute-done.10 = bf16[1,64,1152]{2,1,0:T(8,128)(2,1)S(1)} collective-permute-done((bf16[1,64,1152]{2,1,0:T(8,128)(2,1)S(1)}, bf16[1,64,1152]{2,1,0:T(8,128)(2,1)S(1)}, u32[]{:S(2)}, u32[]{:S(2)}) %collective-permute-start.10) | collective-permute-done | bytes 147488 | tf_op jit(solution)/shard_map/ppermute | solution.py:227
  63.0 0.3 collective-permute-start.14
  63.3 2.1 %collective-permute-start.13 = (bf16[2,64,1152]{2,1,0:T(8,128)(2,1)S(1)}, bf16[2,64,1152]{2,1,0:T(8,128)(2,1)S(1)}, u32[]{:S(2)}, u32[]{:S(2)}) collective-permute-start(bf16[2,64,1152]{2,1,0:T(8,128)(2,1)S(1)} %pad_maximum_fusion.1.refs_2_), channel_id=1, source_target_pairs={{0,64},{32,96},{64,0},{96,32},{1,65},{33,97},{65,1},{97,33},{2,66}... | collective-permute-start | bytes 884744 | tf_op jit(solution)/shard_map/ppermute | solution.py:227
  65.4 1.8 %collective-permute-start.12 = (bf16[2,64,1152]{2,1,0:T(8,128)(2,1)S(1)}, bf16[2,64,1152]{2,1,0:T(8,128)(2,1)S(1)}, u32[]{:S(2)}, u32[]{:S(2)}) collective-permute-start(bf16[2,64,1152]{2,1,0:T(8,128)(2,1)S(1)} %pad_maximum_fusion.1.refs_2_), channel_id=1, source_target_pairs={{0,32},{32,0},{64,96},{96,64},{1,33},{33,1},{65,97},{97,65},{2,34}... | collective-permute-start | bytes 884744 | tf_op jit(solution)/shard_map/ppermute | solution.py:227
  67.2 7.4 %collective-permute-done.14.refs_5_ = bf16[2,64,1152]{2,1,0:T(8,128)(2,1)S(1)} collective-permute-done((bf16[2,64,1152]{2,1,0:T(8,128)(2,1)S(1)}, bf16[2,64,1152]{2,1,0:T(8,128)(2,1)S(1)}, u32[]{:S(2)}, u32[]{:S(2)}) %collective-permute-start.14) | collective-permute-done | bytes 294944 | tf_op jit(solution)/shard_map/ppermute | solution.py:227
  74.6 0.0 collective-permute-start.20
  74.6 0.0 collective-permute-done.11.refs_1_
  74.6 0.5 collective-permute-start.15
  75.1 0.0 collective-permute-start.16
  75.1 0.0 collective-permute-done.13.refs_4_
  75.1 0.5 collective-permute-start.19
  75.6 0.0 collective-permute-done.12.refs_3_
  75.6 0.1 collective-permute-start.18
  75.7 0.5 collective-permute-done.20.refs_11_
  76.1 0.0 copy-start.1
  76.2 0.7 copy-done.1
  76.9 0.1 collective-permute-start.17
  77.0 0.1 pad_add_fusion.place_ref
  77.1 0.9 collective-permute-done.19.refs_10_
  78.0 0.8 collective-permute-done.18.refs_9_
  78.8 0.4 collective-permute-done.17.refs_8_
  79.2 0.0 collective-permute-done.15.refs_6_
  79.2 0.0 collective-permute-done.16.refs_7_
  79.2 0.0 copy-start.2
  79.2 1.0 copy-done.2
  80.2 1.6 %shard_map.38.source_ref = bf16[2,64,16,1152]{3,2,1,0:T(8,128)(2,1)S(1)} custom-call(s32[4]{0:T(128)S(1)} %pad_add_fusion.place_ref, bf16[4,64,1152]{2,1,0:T(8,128)(2,1)S(1)} %pad_maximum_fusion.refs_0_, bf16[4,64,1152]{2,1,0:T(8,128)(2,1)S(1)} %collective-permute-done.11.refs_1_, bf16[2,64,1152]{2,1,0:T(8,128)(2,1)S(1)} %pad_maximum_fusion.1.refs_2_, ...), custom_call_target="tpu_custom_call" | custom-call | tf_op jit(solution)/shard_map/pallas_call | solution.py:136
  81.8 0.0 copy-start
  81.8 2.1 %copy-done = bf16[2,64,16,1152]{3,2,1,0:T(8,128)(2,1)} copy-done((bf16[2,64,16,1152]{3,2,1,0:T(8,128)(2,1)}, bf16[2,64,16,1152]{3,2,1,0:T(8,128)(2,1)S(1)}, u32[]{:S(2)}) %copy-start) | copy-done | bytes 4718616
  84.0 1.5 all-to-all-done.1.in_ref
  85.5 8.6 %shard_map.39 = bf16[64,104,128]{2,1,0:T(8,128)(2,1)} custom-call(s32[16]{0:T(128)} %locked_ref.1, bf16[8,8,104,128]{3,2,1,0:T(8,128)(2,1)} %all-to-all-done.1.in_ref, bf16[2,64,16,1152]{3,2,1,0:T(8,128)(2,1)} %copy-done), custom_call_target="tpu_custom_call" | custom-call | tf_op jit(solution)/shard_map/pallas_call | solution.py:212
  94.0 53.7 %all_to_all.15.in_ref = bf16[64,104,128]{2,1,0:T(8,128)(2,1)S(1)} all-to-all(bf16[64,104,128]{2,1,0:T(8,128)(2,1)} %shard_map.39), channel_id=1, replica_groups=mesh['yh'=2,'x'=4,'z'=8,'yl'=2,'c'=2] {'yh','x','z'}, dimensions={0} | all-to-all | bytes 3407872 | tf_op jit(solution)/shard_map/all_to_all | solution.py:269
  147.7 1.7 %shard_map.40 = bf16[32,25600]{1,0:T(8,128)(2,1)} custom-call(bf16[64,104,128]{2,1,0:T(8,128)(2,1)S(1)} %all_to_all.15.in_ref), custom_call_target="tpu_custom_call" | custom-call | tf_op jit(solution)/shard_map/pallas_call | solution.py:109
  (12 shorter events, 0.3 us)
Async XLA Ops:
  3.8 7.4 %copy-start.3 = (bf16[8,2048]{1,0:T(8,128)(2,1)S(1)}, bf16[8,2048]{1,0:T(8,128)(2,1)}, u32[]{:S(2)}) copy-start(bf16[8,2048]{1,0:T(8,128)(2,1)} %param.4) | copy-start | bytes 98308
  3.8 35.5 %all-to-all-start = ((bf16[8,8,104,128]{3,2,1,0:T(8,128)(2,1)}), bf16[8,8,104,128]{3,2,1,0:T(8,128)(2,1)S(1)}, u32[]{:S(2)}, u32[]{:S(2)}) async-start(bf16[8,8,104,128]{3,2,1,0:T(8,128)(2,1)} %bitcast.13), calls=%async_computation | async-start | bytes 3407872 | tf_op jit(solution)/shard_map/all_to_all | solution.py:263
  11.2 6.5 %collective-permute-start.2 = (bf16[1,8,2048]{2,1,0:T(8,128)(2,1)S(1)}, bf16[1,8,2048]{2,1,0:T(8,128)(2,1)S(1)}, u32[]{:S(2)}, u32[]{:S(2)}) collective-permute-start(bf16[1,8,2048]{2,1,0:T(8,128)(2,1)S(1)} %bitcast.22), channel_id=1, source_target_pairs={{0,12},{4,8},{8,4},{12,0},{16,28},{20,24},{24,20},{28,16},{1,13},{... | collective-permute-start | bytes 98312 | tf_op jit(solution)/shard_map/ppermute | solution.py:227
  15.8 4.8 %collective-permute-start.1 = (bf16[1,8,2048]{2,1,0:T(8,128)(2,1)S(1)}, bf16[1,8,2048]{2,1,0:T(8,128)(2,1)S(1)}, u32[]{:S(2)}, u32[]{:S(2)}) collective-permute-start(bf16[1,8,2048]{2,1,0:T(8,128)(2,1)S(1)} %bitcast.23), channel_id=1, source_target_pairs={{0,8},{4,12},{8,0},{12,4},{16,24},{20,28},{24,16},{28,20},{1,9},{5... | collective-permute-start | bytes 98312 | tf_op jit(solution)/shard_map/ppermute | solution.py:227
  15.8 4.8 %collective-permute-start = (bf16[1,8,2048]{2,1,0:T(8,128)(2,1)S(1)}, bf16[1,8,2048]{2,1,0:T(8,128)(2,1)S(1)}, u32[]{:S(2)}, u32[]{:S(2)}) collective-permute-start(bf16[1,8,2048]{2,1,0:T(8,128)(2,1)S(1)} %bitcast.24), channel_id=1, source_target_pairs={{0,4},{4,0},{8,12},{12,8},{16,20},{20,16},{24,28},{28,24},{1,5},{5... | collective-permute-start | bytes 98312 | tf_op jit(solution)/shard_map/ppermute | solution.py:227
  20.7 24.4 %collective-permute-start.5 = (bf16[4,8,896]{2,1,0:T(8,128)(2,1)S(1)}, bf16[4,8,896]{2,1,0:T(8,128)(2,1)S(1)}, u32[]{:S(2)}, u32[]{:S(2)}) collective-permute-start(bf16[4,8,896]{2,1,0:T(8,128)(2,1)S(1)} %pad_maximum_fusion.3), channel_id=1, source_target_pairs={{128,112},{132,116},{136,120},{140,124},{144,96},{148,100},{152,10... | collective-permute-start | bytes 172040 | tf_op jit(solution)/shard_map/ppermute | solution.py:235
  29.2 15.8 %collective-permute-start.4 = (bf16[4,8,896]{2,1,0:T(8,128)(2,1)S(1)}, bf16[4,8,896]{2,1,0:T(8,128)(2,1)S(1)}, u32[]{:S(2)}, u32[]{:S(2)}) collective-permute-start(bf16[4,8,896]{2,1,0:T(8,128)(2,1)S(1)} %pad_maximum_fusion.3), channel_id=1, source_target_pairs={{128,96},{132,100},{136,104},{140,108},{144,112},{148,116},{152,12... | collective-permute-start | bytes 172040 | tf_op jit(solution)/shard_map/ppermute | solution.py:235
  30.6 8.8 %collective-permute-start.3 = (bf16[4,8,1152]{2,1,0:T(8,128)(2,1)S(1)}, bf16[4,8,1152]{2,1,0:T(8,128)(2,1)S(1)}, u32[]{:S(2)}, u32[]{:S(2)}) collective-permute-start(bf16[4,8,1152]{2,1,0:T(8,128)(2,1)S(1)} %slice.21), channel_id=1, source_target_pairs={{0,16},{4,20},{8,24},{12,28},{16,0},{20,4},{24,8},{28,12},{1,17},{... | collective-permute-start | bytes 221192 | tf_op jit(solution)/shard_map/ppermute | solution.py:227
  40.7 44.7 %all-to-all-start.1 = ((bf16[8,8,104,128]{3,2,1,0:T(8,128)(2,1)}), bf16[8,8,104,128]{3,2,1,0:T(8,128)(2,1)}, u32[]{:S(2)}, u32[]{:S(2)}) async-start(bf16[8,8,104,128]{3,2,1,0:T(8,128)(2,1)} %bitcast.12), calls=%async_computation.1 | async-start | bytes 3407872 | tf_op jit(solution)/shard_map/all_to_all | solution.py:268
  45.2 5.2 %collective-permute-start.6 = (bf16[8,8,1152]{2,1,0:T(8,128)(2,1)S(1)}, bf16[8,8,1152]{2,1,0:T(8,128)(2,1)S(1)}, u32[]{:S(2)}, u32[]{:S(2)}) collective-permute-start(bf16[8,8,1152]{2,1,0:T(8,128)(2,1)S(1)} %slice_select_fusion), channel_id=1, source_target_pairs={{0,2},{2,0},{1,3},{3,1},{4,6},{6,4},{5,7},{7,5},{8,10},{10,8},{9,1... | collective-permute-start | bytes 442376 | tf_op jit(solution)/shard_map/ppermute | solution.py:227
  50.5 8.0 %collective-permute-start.9 = (bf16[1,64,1152]{2,1,0:T(8,128)(2,1)S(1)}, bf16[1,64,1152]{2,1,0:T(8,128)(2,1)S(1)}, u32[]{:S(2)}, u32[]{:S(2)}) collective-permute-start(bf16[1,64,1152]{2,1,0:T(8,128)(2,1)S(1)} %bitcast.14), channel_id=1, source_target_pairs={{0,96},{32,64},{64,32},{96,0},{1,97},{33,65},{65,33},{97,1},{2,98}... | collective-permute-start | bytes 442376 | tf_op jit(solution)/shard_map/ppermute | solution.py:227
  51.6 6.9 %collective-permute-start.8 = (bf16[1,64,1152]{2,1,0:T(8,128)(2,1)S(1)}, bf16[1,64,1152]{2,1,0:T(8,128)(2,1)S(1)}, u32[]{:S(2)}, u32[]{:S(2)}) collective-permute-start(bf16[1,64,1152]{2,1,0:T(8,128)(2,1)S(1)} %bitcast.15), channel_id=1, source_target_pairs={{0,64},{32,96},{64,0},{96,32},{1,65},{33,97},{65,1},{97,33},{2,66}... | collective-permute-start | bytes 442376 | tf_op jit(solution)/shard_map/ppermute | solution.py:227
  52.9 6.5 %collective-permute-start.7 = (bf16[1,64,1152]{2,1,0:T(8,128)(2,1)S(1)}, bf16[1,64,1152]{2,1,0:T(8,128)(2,1)S(1)}, u32[]{:S(2)}, u32[]{:S(2)}) collective-permute-start(bf16[1,64,1152]{2,1,0:T(8,128)(2,1)S(1)} %bitcast.16), channel_id=1, source_target_pairs={{0,32},{32,0},{64,96},{96,64},{1,33},{33,1},{65,97},{97,65},{2,34}... | collective-permute-start | bytes 442376 | tf_op jit(solution)/shard_map/ppermute | solution.py:227
  54.7 8.3 %collective-permute-start.10 = (bf16[1,64,1152]{2,1,0:T(8,128)(2,1)S(1)}, bf16[1,64,1152]{2,1,0:T(8,128)(2,1)S(1)}, u32[]{:S(2)}, u32[]{:S(2)}) collective-permute-start(bf16[1,64,1152]{2,1,0:T(8,128)(2,1)S(1)} %bitcast.19), channel_id=1, source_target_pairs={{0,128},{128,0},{1,129},{129,1},{2,130},{130,2},{3,131},{131,3},{4... | collective-permute-start | bytes 442376 | tf_op jit(solution)/shard_map/ppermute | solution.py:227
  59.5 15.1 %collective-permute-start.11 = (bf16[4,64,1152]{2,1,0:T(8,128)(2,1)S(1)}, bf16[4,64,1152]{2,1,0:T(8,128)(2,1)S(1)}, u32[]{:S(2)}, u32[]{:S(2)}) collective-permute-start(bf16[4,64,1152]{2,1,0:T(8,128)(2,1)S(1)} %pad_maximum_fusion.refs_0_), channel_id=1, source_target_pairs={{0,128},{128,0},{1,129},{129,1},{2,130},{130,2},{3,131},{131,3},{4... | collective-permute-start | bytes 1769480 | tf_op jit(solution)/shard_map/ppermute | solution.py:227
  63.0 11.5 %collective-permute-start.14 = (bf16[2,64,1152]{2,1,0:T(8,128)(2,1)S(1)}, bf16[2,64,1152]{2,1,0:T(8,128)(2,1)S(1)}, u32[]{:S(2)}, u32[]{:S(2)}) collective-permute-start(bf16[2,64,1152]{2,1,0:T(8,128)(2,1)S(1)} %pad_maximum_fusion.1.refs_2_), channel_id=1, source_target_pairs={{0,96},{32,64},{64,32},{96,0},{1,97},{33,65},{65,33},{97,1},{2,98}... | collective-permute-start | bytes 884744 | tf_op jit(solution)/shard_map/ppermute | solution.py:227
  63.3 11.8 %collective-permute-start.13 = (bf16[2,64,1152]{2,1,0:T(8,128)(2,1)S(1)}, bf16[2,64,1152]{2,1,0:T(8,128)(2,1)S(1)}, u32[]{:S(2)}, u32[]{:S(2)}) collective-permute-start(bf16[2,64,1152]{2,1,0:T(8,128)(2,1)S(1)} %pad_maximum_fusion.1.refs_2_), channel_id=1, source_target_pairs={{0,64},{32,96},{64,0},{96,32},{1,65},{33,97},{65,1},{97,33},{2,66}... | collective-permute-start | bytes 884744 | tf_op jit(solution)/shard_map/ppermute | solution.py:227
  65.4 10.2 %collective-permute-start.12 = (bf16[2,64,1152]{2,1,0:T(8,128)(2,1)S(1)}, bf16[2,64,1152]{2,1,0:T(8,128)(2,1)S(1)}, u32[]{:S(2)}, u32[]{:S(2)}) collective-permute-start(bf16[2,64,1152]{2,1,0:T(8,128)(2,1)S(1)} %pad_maximum_fusion.1.refs_2_), channel_id=1, source_target_pairs={{0,32},{32,0},{64,96},{96,64},{1,33},{33,1},{65,97},{97,65},{2,34}... | collective-permute-start | bytes 884744 | tf_op jit(solution)/shard_map/ppermute | solution.py:227
  74.6 1.6 %collective-permute-start.20 = (bf16[2,64,1152]{2,1,0:T(8,128)(2,1)S(1)}, bf16[2,64,1152]{2,1,0:T(8,128)(2,1)S(1)}, u32[]{:S(2)}, u32[]{:S(2)}) collective-permute-start(bf16[2,64,1152]{2,1,0:T(8,128)(2,1)S(1)} %collective-permute-done.14.refs_5_), channel_id=1, source_target_pairs={{0,1},{1,0},{2,3},{3,2},{4,5},{5,4},{6,7},{7,6},{8,9},{9,8},{10,11... | collective-permute-start | bytes 884744 | tf_op jit(solution)/shard_map/ppermute | solution.py:227
  74.6 4.7 %collective-permute-start.15 = (bf16[4,64,1152]{2,1,0:T(8,128)(2,1)S(1)}, bf16[4,64,1152]{2,1,0:T(8,128)(2,1)S(1)}, u32[]{:S(2)}, u32[]{:S(2)}) collective-permute-start(bf16[4,64,1152]{2,1,0:T(8,128)(2,1)S(1)} %pad_maximum_fusion.refs_0_), channel_id=1, source_target_pairs={{0,1},{1,0},{2,3},{3,2},{4,5},{5,4},{6,7},{7,6},{8,9},{9,8},{10,11... | collective-permute-start | bytes 1769480 | tf_op jit(solution)/shard_map/ppermute | solution.py:227
  75.1 4.2 %collective-permute-start.16 = (bf16[4,64,1152]{2,1,0:T(8,128)(2,1)S(1)}, bf16[4,64,1152]{2,1,0:T(8,128)(2,1)S(1)}, u32[]{:S(2)}, u32[]{:S(2)}) collective-permute-start(bf16[4,64,1152]{2,1,0:T(8,128)(2,1)S(1)} %collective-permute-done.11.refs_1_), channel_id=1, source_target_pairs={{0,1},{1,0},{2,3},{3,2},{4,5},{5,4},{6,7},{7,6},{8,9},{9,8},{10,11... | collective-permute-start | bytes 1769480 | tf_op jit(solution)/shard_map/ppermute | solution.py:227
  75.1 2.9 %collective-permute-start.19 = (bf16[2,64,1152]{2,1,0:T(8,128)(2,1)S(1)}, bf16[2,64,1152]{2,1,0:T(8,128)(2,1)}, u32[]{:S(2)}, u32[]{:S(2)}) collective-permute-start(bf16[2,64,1152]{2,1,0:T(8,128)(2,1)S(1)} %collective-permute-done.13.refs_4_), channel_id=1, source_target_pairs={{0,1},{1,0},{2,3},{3,2},{4,5},{5,4},{6,7},{7,6},{8,9},{9,8},{10,11... | collective-permute-start | bytes 884744 | tf_op jit(solution)/shard_map/ppermute | solution.py:227
  75.6 3.2 %collective-permute-start.18 = (bf16[2,64,1152]{2,1,0:T(8,128)(2,1)S(1)}, bf16[2,64,1152]{2,1,0:T(8,128)(2,1)}, u32[]{:S(2)}, u32[]{:S(2)}) collective-permute-start(bf16[2,64,1152]{2,1,0:T(8,128)(2,1)S(1)} %collective-permute-done.12.refs_3_), channel_id=1, source_target_pairs={{0,1},{1,0},{2,3},{3,2},{4,5},{5,4},{6,7},{7,6},{8,9},{9,8},{10,11... | collective-permute-start | bytes 884744 | tf_op jit(solution)/shard_map/ppermute | solution.py:227
  76.1 0.7 copy-start.1
  76.9 2.4 %collective-permute-start.17 = (bf16[2,64,1152]{2,1,0:T(8,128)(2,1)S(1)}, bf16[2,64,1152]{2,1,0:T(8,128)(2,1)}, u32[]{:S(2)}, u32[]{:S(2)}) collective-permute-start(bf16[2,64,1152]{2,1,0:T(8,128)(2,1)S(1)} %pad_maximum_fusion.1.refs_2_), channel_id=1, source_target_pairs={{0,1},{1,0},{2,3},{3,2},{4,5},{5,4},{6,7},{7,6},{8,9},{9,8},{10,11... | collective-permute-start | bytes 884744 | tf_op jit(solution)/shard_map/ppermute | solution.py:227
  79.2 1.0 copy-start.2
  81.8 2.1 %copy-start = (bf16[2,64,16,1152]{3,2,1,0:T(8,128)(2,1)}, bf16[2,64,16,1152]{3,2,1,0:T(8,128)(2,1)S(1)}, u32[]{:S(2)}) copy-start(bf16[2,64,16,1152]{3,2,1,0:T(8,128)(2,1)S(1)} %shard_map.38.source_ref) | copy-start | bytes 14155780

commit v2 on v1

v2 whole, which is shorter than its diff:
```python
import functools

import jax
import jax.numpy as jnp
from jax import lax
from jax.experimental import pallas as pl
from jax.experimental.pallas import tpu as pltpu
from jax.sharding import Mesh, PartitionSpec as P

AXES = ("yh", "x", "zh", "zl", "yl", "c")
Z = ("zh", "zl")
EIG = ("yh", "x", "zh", "zl")
SITE = ("yl", "c")
PEERS = 64
ROWS = 32
TILES = 3
CHUNK = 104
KEEP = 1152
WIDTH = 512
F32 = jnp.float32
BF16 = jnp.bfloat16


def seat(z):
    return z % 4 * 2 + z // 4


def place_of(peer):
    yh, x, z = peer // 32, peer // 8 % 4, peer % 8
    return ((x * 4 + z % 4) * 2 + yh) * 2 + z // 4


def lane_group():
    return lax.broadcasted_iota(jnp.int32, (8, 128), 1) // 16


def low_half():
    return lax.broadcasted_iota(jnp.int32, (8, 128), 0) < 4


def regroup(tile):
    low = low_half()
    groups = []
    for k in range(4):
        straight = tile[8 * k : 8 * k + 8]
        turned = pltpu.roll(straight, 4, 0)
        groups.append(jnp.where(low, straight, turned))
        groups.append(jnp.where(low, turned, straight))
    return groups


def gather_lanes(groups, place):
    lanes = lane_group()
    total = jnp.zeros((8, 128), F32)
    for h in range(8):
        total = jnp.where(lanes == h, pltpu.roll(groups[h], (16 * (h - place)) % 128, 1), total)
    return total


def pack_kernel(in_ref, out_ref):
    for group in range(8):
        column = 24576 + 128 * group
        groups = regroup(in_ref[:, column : column + 128].astype(F32))
        for z in range(8):
            for t in range(TILES):
                column = (TILES * (8 * group + z) + t) * 128
                out_ref[group, seat(z), 32 * t : 32 * t + 32, :] = in_ref[:, column : column + 128]
            out_ref[group, seat(z), 96:104, :] = gather_lanes(groups, z).astype(BF16)


def pack(vectors):
    return pl.pallas_call(
        pack_kernel,
        out_shape=jax.ShapeDtypeStruct((8, 8, CHUNK, 128), BF16),
        compiler_params=pltpu.CompilerParams(vmem_limit_bytes=16 * 1024 * 1024),
    )(vectors)


def unpack_kernel(in_ref, out_ref):
    lanes, low = lane_group(), low_half()
    for group in range(8):
        lefts = []
        for z in range(8):
            seat_of = place_of(8 * group + z)
            for t in range(TILES):
                column = (TILES * (8 * group + z) + t) * 128
                out_ref[:, column : column + 128] = in_ref[seat_of, 32 * t : 32 * t + 32, :]
            lefts.append(in_ref[seat_of, 96:104, :].astype(F32))
        pieces = []
        for k in range(4):
            total = jnp.zeros((8, 128), F32)
            for z in range(8):
                first = pltpu.roll(lefts[z], (16 * (z - 2 * k)) % 128, 1)
                second = pltpu.roll(lefts[z], (16 * (z - 2 * k - 1)) % 128, 1)
                total = jnp.where(lanes == z, jnp.where(low, first, second), total)
            pieces.append(total)
        column = 24576 + 128 * group
        out_ref[:, column : column + 128] = jnp.concatenate(pieces, axis=0).astype(BF16)


def unpack(received):
    return pl.pallas_call(
        unpack_kernel,
        out_shape=jax.ShapeDtypeStruct((ROWS, 25600), BF16),
        compiler_params=pltpu.CompilerParams(vmem_limit_bytes=16 * 1024 * 1024),
    )(received)


def place_kernel(place_ref, *refs):
    panels, out_ref = refs[:12], refs[12]
    core, yh, x, z = (place_ref[i] for i in range(4))

    def fill(first_side):
        for first in range(2):
            for dx in range(4):
                group = (yh ^ first) * 4 + (x ^ dx)
                for step in range(8):
                    which, at = (first, dx) if step < 4 else (2 + dx, first)
                    row = 16 * (step % 4)
                    low, high = (panels[6 * side + which][at, row : row + 16, :].astype(F32) for side in (first_side, 1 - first_side))
                    rows = jnp.concatenate([low[:8], high[:8], low[8:], high[8:]], axis=0)
                    out_ref[group * 8 + (z ^ step)] = rows.astype(BF16)

    for side in range(2):
        pl.when(core == side)(functools.partial(fill, side))
    for group in range(8):
        slot, column = (group, 256 * group + 128) if group < 4 else (7 - group, 256 * (8 - group) + 128 * (2 * group - 8))
        out_ref[8 * slot : 8 * slot + 4, :, column : column + 128] = jnp.zeros((4, ROWS, 128), BF16)


def place_panels(place, panels):
    vmem = pl.BlockSpec(memory_space=pltpu.VMEM)
    return pl.pallas_call(
        place_kernel,
        in_specs=[pl.BlockSpec(memory_space=pltpu.SMEM)] + [vmem] * 12,
        out_specs=vmem,
        out_shape=jax.ShapeDtypeStruct((PEERS, ROWS, KEEP), BF16),
        compiler_params=pltpu.CompilerParams(vmem_limit_bytes=16 * 1024 * 1024),
    )(place, *panels)


def rotate_kernel(locked_ref, in_ref, matrix_ref, out_ref, held):
    low64 = lax.broadcasted_iota(jnp.int32, (64, 128), 0) % 8 < 4
    for group in range(8):
        rows = slice(256 * group, 256 * group + 256)
        for z in range(8):
            row = 256 * group + 32 * z
            for t in range(TILES):
                held[row : row + 32, 128 * t : 128 * t + 128] = in_ref[seat(z), group, 32 * t : 32 * t + 32, :]
        left = jnp.concatenate([in_ref[seat(z), group, 96:104, :] for z in range(8)], axis=0).astype(F32)
        parts = []
        for k in range(4):
            a = pltpu.roll(left, (-32 * k) % 128, 1)
            b = pltpu.roll(left, (-32 * k - 16) % 128, 1)
            parts.append(jnp.where(low64, a, b).reshape(8, 8, 128))
        held[rows, 384:512] = jnp.stack(parts, axis=1).reshape(256, 128).astype(BF16)

    def product(lhs, rhs):
        return lax.dot_general(lhs, rhs, (((0,), (0,)), ((), ())), preferred_element_type=F32)

    def panel(group, column, width, groups=1):
        return matrix_ref[8 * group : 8 * (group + groups), :, column : column + width].reshape(256 * groups, width)

    for block in range(8):
        total = None
        terms = []
        if block < 4:
            terms.append((panel(block, 256 * block, 256, 8 - block), held[256 * block :, :]))
        for peer in range(block, 8) if block >= 4 else ():
            at = 256 * (8 - peer) + 128 * (2 * block - 9)
            if block == 4:
                lhs = jnp.concatenate([panel(peer, 1024, 128), panel(7 - peer, at + 128, 128)], axis=1)
            else:
                lhs = panel(7 - peer, at, 256)
            terms.append((lhs, held[256 * peer : 256 * peer + 256, :]))
        for lhs, rhs in terms:
            term = product(lhs, rhs)
            total = term if total is None else total + term
        rows = lax.broadcasted_iota(jnp.int32, (256, 1), 0)
        limit = jnp.where(rows < 128, locked_ref[2 * block], locked_ref[2 * block + 1])
        mine = held[256 * block : 256 * block + 256, :].astype(F32)
        result = jnp.where(rows % 128 < limit, mine, total).astype(BF16)
        left = result[:, 384:512].astype(F32)
        for z in range(8):
            peer = place_of(8 * block + z)
            for t in range(TILES):
                out_ref[peer, 32 * t : 32 * t + 32, :] = result[32 * z : 32 * z + 32, 128 * t : 128 * t + 128]
            groups = regroup(left[32 * z : 32 * z + 32])
            out_ref[peer, 96:104, :] = gather_lanes(groups, 0).astype(BF16)


def rotate(locked, received, matrix):
    vmem = pl.BlockSpec(memory_space=pltpu.VMEM)
    return pl.pallas_call(
        rotate_kernel,
        in_specs=[pl.BlockSpec(memory_space=pltpu.SMEM), vmem, vmem],
        out_specs=vmem,
        out_shape=jax.ShapeDtypeStruct((PEERS, CHUNK, 128), BF16),
        scratch_shapes=[pltpu.VMEM((PEERS * ROWS, WIDTH), BF16)],
        compiler_params=pltpu.CompilerParams(vmem_limit_bytes=16 * 1024 * 1024),
    )(locked, received, matrix)


def exchange(value, axis, size, mask):
    return lax.ppermute(value, axis, [(i, i ^ mask) for i in range(size)])


def gather_near(rotation):
    rows = rotation[None]
    rows = jnp.concatenate([rows] + [exchange(rows, Z, 8, step) for step in (1, 2, 3)])
    late = [i for i in range(PEERS) if i >= 32]
    spare = rows[:, :, KEEP:]
    guests = [lax.ppermute(spare, EIG, [(i, (7 - i // 8) * 8 + (i % 8 ^ far)) for i in late]) for far in (0, 4)]
    return rows[:, :, :KEEP], exchange(rows[:, :, :KEEP], Z, 8, 4), *guests


def gather_panels(near, far, *guests):
    eig, yl = lax.axis_index(EIG), lax.axis_index("yl")
    group = eig // 8
    rows = jnp.concatenate([near, far])
    place = 256 * (group + 1)
    guest = jnp.concatenate([jnp.concatenate(guests), jnp.zeros((8, 8, KEEP), BF16)], axis=2)
    guest = lax.dynamic_update_slice(jnp.zeros((8, 8, 4096), BF16), guest, (0, 0, place))[:, :, :KEEP]
    cols = lax.broadcasted_iota(jnp.int32, (1, 1, KEEP), 2)
    rows = jnp.where((group >= 4) | (cols < place), rows, guest)
    other = exchange(rows, "yl", 2, 1)
    rows = jnp.where(yl == 0, jnp.stack([rows, other], axis=1), jnp.stack([other, rows], axis=1))

    a, b = rows[:4].reshape(1, 64, KEEP), rows[4:].reshape(1, 64, KEEP)
    b = jnp.concatenate([b, exchange(b, "yh", 2, 1)])
    a = jnp.concatenate([a] + [exchange(a, "x", 4, dx) for dx in (1, 2, 3)])
    far_a = exchange(a, "yh", 2, 1)
    far_b = [exchange(b, "x", 4, dx) for dx in (1, 2, 3)]
    a, b, far_a = lax.optimization_barrier((a, b, far_a))
    own = [a, far_a, b] + far_b
    return own + [exchange(panel, "c", 2, 1) for panel in own]


def body(vectors, rotation, locked):
    halfway = lax.all_to_all(pack(vectors), ("yh", "x"), split_axis=0, concat_axis=0, tiled=True)
    near = gather_near(rotation)
    halfway, _ = lax.optimization_barrier((halfway, near[1]))
    place = jnp.stack([lax.axis_index(name) for name in ("c", "yh", "x", Z)]).astype(jnp.int32)
    matrix = place_panels(place, gather_panels(*near))
    received = lax.all_to_all(halfway.transpose(1, 0, 2, 3), ("zl", "zh"), split_axis=0, concat_axis=0, tiled=True)
    back = lax.all_to_all(rotate(locked, received, matrix), ("x", "zl", "yh", "zh"), split_axis=0, concat_axis=0, tiled=True)
    return unpack(back)


def solution(mesh):
    fine = Mesh(mesh.devices.reshape(2, 4, 2, 4, 2, 2), AXES)
    in_specs = (P(EIG, SITE), P(EIG + SITE, None), P())
    return jax.shard_map(body, mesh=fine, in_specs=in_specs, out_specs=P(EIG, SITE), check_vma=False)
```

time: 151 us -> 147 us (0.974)
  Pallas kernels: 15.7 us -> 8.98 us
  local copies, waits for them, and re-layouts: 5.27 us -> 9.09 us
  waiting for transfers between devices: 31 us -> 28.7 us
    pallas_call x1, Pallas kernels: 8.57 us -> 3.48 us  [rotate(): pl.pallas_call(rotate_kernel, in_specs=[pl.BlockSpec(memory_space=pltpu.S...]
    unnamed x8 -> x14, local copies, waits for them, and re-layouts: 3.82 us -> 7.59 us
    pallas_call x2, Pallas kernels: 5.49 us -> 3.4 us  [the longest x1 1.74 us: pack(): pl.pallas_call(pack_kernel, out_shape=jax.ShapeDtypeStruct((8, 8, CHUNK,...]
  transfers between devices with their start and end apart: 23 -> 23, of which waited for: 13 -> 12; matrix products, arithmetic and copies ran while one was open for 1% -> 1% of each run, Pallas kernels for 1% -> 1%
where the time goes in v2:
time: 147 us; the launch traced here: 146 us
  blocking collectives  55 us (37%)
  starting transfers between devices  44 us (30%)
  waiting for transfers between devices  28.7 us (20%)
  local copies, waits for them, and re-layouts  9.09 us (6%)
  Pallas kernels  8.98 us (6%)
    all_to_all x1, blocking collectives, body(): lax.all_to_all(rotate(locked, received, matrix), ('x', 'zl', 'yh', 'zh'),...  55 us
    ppermute x19, waiting for transfers between devices, exchange(): return lax.ppermute(value, axis, [(i, i ^ mask) for i in range(size)])  28.7 us
    ppermute x19, starting transfers between devices, exchange(): return lax.ppermute(value, axis, [(i, i ^ mask) for i in range(size)])  23.2 us
    ppermute x2, starting transfers between devices, gather_near(): lax.ppermute(spare, EIG, [(i, (7 - i // 8) * 8 + (i % 8 ^ far)) for i in...  9.82 us
    unnamed x14, local copies, waits for them, and re-layouts  7.59 us
    all_to_all x1, starting transfers between devices, body(): lax.all_to_all(pack(vectors), ('yh', 'x'), split_axis=0, concat_axis=0, t...  7.39 us
    all_to_all x1, starting transfers between devices, body(): lax.all_to_all(halfway.transpose(1, 0, 2, 3), ('zl', 'zh'), split_axis=0,...  3.59 us
    pallas_call x1, Pallas kernels, rotate(): pl.pallas_call(rotate_kernel, in_specs=[pl.BlockSpec(memory_space=pltpu.S...  3.48 us
  transfers between devices with their start and end apart: 23, of which 12 were waited for; matrix products, arithmetic and copies ran while one was open for 1% of the time, Pallas kernels for 1%

profile of v2, /device:TPU:16, one launch (start us, length us, event | category | flops | bytes accessed | tf_op | source)
XLA Modules:
  0.0 146.3 jit_solution(10639707086378229757)
XLA Ops:
  0.0 0.0 copy-start.2
  0.0 1.4 copy-done.2
  1.4 1.7 %shard_map.37 = bf16[8,8,104,128]{3,2,1,0:T(8,128)(2,1)} custom-call(bf16[32,25600]{1,0:T(8,128)(2,1)S(1)} %copy-done.2), custom_call_target="tpu_custom_call" | custom-call | tf_op jit(solution)/shard_map/pallas_call | solution.py:72
  3.2 0.0 copy-start.6
  3.2 7.4 %all-to-all-start = ((bf16[8,8,104,128]{3,2,1,0:T(8,128)(2,1)}), bf16[8,8,104,128]{3,2,1,0:T(8,128)(2,1)S(1)}, u32[]{:S(2)}, u32[]{:S(2)}) async-start(bf16[8,8,104,128]{3,2,1,0:T(8,128)(2,1)} %shard_map.37), calls=%async_computation | async-start | bytes 3407872 | tf_op jit(solution)/shard_map/all_to_all | solution.py:240
  10.6 0.0 copy-done.6
  10.6 4.6 %collective-permute-start.2 = (bf16[1,8,2048]{2,1,0:T(8,128)(2,1)S(1)}, bf16[1,8,2048]{2,1,0:T(8,128)(2,1)S(1)}, u32[]{:S(2)}, u32[]{:S(2)}) collective-permute-start(bf16[1,8,2048]{2,1,0:T(8,128)(2,1)S(1)} %bitcast.20), channel_id=1, source_target_pairs={{0,12},{4,8},{8,4},{12,0},{16,28},{20,24},{24,20},{28,16},{1,13},{... | collective-permute-start | bytes 98312 | tf_op jit(solution)/shard_map/ppermute | solution.py:205
  15.2 0.0 collective-permute-start.1
  15.2 0.7 collective-permute-start
  15.8 1.3 collective-permute-done.2
  17.1 2.9 %collective-permute-done.1 = bf16[1,8,2048]{2,1,0:T(8,128)(2,1)S(1)} collective-permute-done((bf16[1,8,2048]{2,1,0:T(8,128)(2,1)S(1)}, bf16[1,8,2048]{2,1,0:T(8,128)(2,1)S(1)}, u32[]{:S(2)}, u32[]{:S(2)}) %collective-permute-start.1) | collective-permute-done | bytes 32800 | tf_op jit(solution)/shard_map/ppermute | solution.py:205
  20.0 0.0 collective-permute-done
  20.0 8.5 %collective-permute-start.5 = (bf16[4,8,896]{2,1,0:T(8,128)(2,1)S(1)}, bf16[4,8,896]{2,1,0:T(8,128)(2,1)S(1)}, u32[]{:S(2)}, u32[]{:S(2)}) collective-permute-start(bf16[4,8,896]{2,1,0:T(8,128)(2,1)S(1)} %pad_maximum_fusion.3), channel_id=1, source_target_pairs={{128,112},{132,116},{136,120},{140,124},{144,96},{148,100},{152,10... | collective-permute-start | bytes 172040 | tf_op jit(solution)/shard_map/ppermute | solution.py:213
  28.6 1.3 collective-permute-start.4
  29.9 1.5 %collective-permute-start.3 = (bf16[4,8,1152]{2,1,0:T(8,128)(2,1)S(1)}, bf16[4,8,1152]{2,1,0:T(8,128)(2,1)S(1)}, u32[]{:S(2)}, u32[]{:S(2)}) collective-permute-start(bf16[4,8,1152]{2,1,0:T(8,128)(2,1)S(1)} %slice.21), channel_id=1, source_target_pairs={{0,16},{4,20},{8,24},{12,28},{16,0},{20,4},{24,8},{28,12},{1,17},{... | collective-permute-start | bytes 221192 | tf_op jit(solution)/shard_map/ppermute | solution.py:205
  31.4 7.3 %collective-permute-done.3 = bf16[4,8,1152]{2,1,0:T(8,128)(2,1)S(1)} collective-permute-done((bf16[4,8,1152]{2,1,0:T(8,128)(2,1)S(1)}, bf16[4,8,1152]{2,1,0:T(8,128)(2,1)S(1)}, u32[]{:S(2)}, u32[]{:S(2)}) %collective-permute-start.3) | collective-permute-done | bytes 73760 | tf_op jit(solution)/shard_map/ppermute | solution.py:205
  38.7 0.0 all-to-all-done
  38.7 1.4 copy.11
  40.1 3.6 %all-to-all-start.1 = ((bf16[8,8,104,128]{3,2,1,0:T(8,128)(2,1)}), bf16[8,8,104,128]{3,2,1,0:T(8,128)(2,1)S(1)}, u32[]{:S(2)}, u32[]{:S(2)}) async-start(bf16[8,8,104,128]{3,2,1,0:T(8,128)(2,1)} %bitcast.11), calls=%async_computation.1 | async-start | bytes 3407872 | tf_op jit(solution)/shard_map/all_to_all | solution.py:245
  43.7 0.0 collective-permute-done.5
  43.7 0.0 collective-permute-done.4
  43.8 1.4 collective-permute-start.6
  45.2 3.9 %collective-permute-done.6 = bf16[8,8,1152]{2,1,0:T(8,128)(2,1)S(1)} collective-permute-done((bf16[8,8,1152]{2,1,0:T(8,128)(2,1)S(1)}, bf16[8,8,1152]{2,1,0:T(8,128)(2,1)S(1)}, u32[]{:S(2)}, u32[]{:S(2)}) %collective-permute-start.6) | collective-permute-done | bytes 147488 | tf_op jit(solution)/shard_map/ppermute | solution.py:205
  49.2 1.9 %collective-permute-start.9 = (bf16[1,64,1152]{2,1,0:T(8,128)(2,1)S(1)}, bf16[1,64,1152]{2,1,0:T(8,128)(2,1)S(1)}, u32[]{:S(2)}, u32[]{:S(2)}) collective-permute-start(bf16[1,64,1152]{2,1,0:T(8,128)(2,1)S(1)} %bitcast.12), channel_id=1, source_target_pairs={{0,96},{32,64},{64,32},{96,0},{1,97},{33,65},{65,33},{97,1},{2,98}... | collective-permute-start | bytes 442376 | tf_op jit(solution)/shard_map/ppermute | solution.py:205
  51.0 0.5 collective-permute-start.8
  51.6 1.8 %collective-permute-start.7 = (bf16[1,64,1152]{2,1,0:T(8,128)(2,1)S(1)}, bf16[1,64,1152]{2,1,0:T(8,128)(2,1)S(1)}, u32[]{:S(2)}, u32[]{:S(2)}) collective-permute-start(bf16[1,64,1152]{2,1,0:T(8,128)(2,1)S(1)} %bitcast.14), channel_id=1, source_target_pairs={{0,32},{32,0},{64,96},{96,64},{1,33},{33,1},{65,97},{97,65},{2,34}... | collective-permute-start | bytes 442376 | tf_op jit(solution)/shard_map/ppermute | solution.py:205
  53.4 2.7 %collective-permute-start.10 = (bf16[1,64,1152]{2,1,0:T(8,128)(2,1)S(1)}, bf16[1,64,1152]{2,1,0:T(8,128)(2,1)S(1)}, u32[]{:S(2)}, u32[]{:S(2)}) collective-permute-start(bf16[1,64,1152]{2,1,0:T(8,128)(2,1)S(1)} %bitcast.17), channel_id=1, source_target_pairs={{0,128},{128,0},{1,129},{129,1},{2,130},{130,2},{3,131},{131,3},{4... | collective-permute-start | bytes 442376 | tf_op jit(solution)/shard_map/ppermute | solution.py:205
  56.1 0.0 collective-permute-done.9
  56.1 1.6 %collective-permute-done.8 = bf16[1,64,1152]{2,1,0:T(8,128)(2,1)S(1)} collective-permute-done((bf16[1,64,1152]{2,1,0:T(8,128)(2,1)S(1)}, bf16[1,64,1152]{2,1,0:T(8,128)(2,1)S(1)}, u32[]{:S(2)}, u32[]{:S(2)}) %collective-permute-start.8) | collective-permute-done | bytes 147488 | tf_op jit(solution)/shard_map/ppermute | solution.py:205
  57.7 0.4 collective-permute-done.7
  58.1 0.1 pad_maximum_fusion.refs_0_
  58.1 2.7 %collective-permute-start.11 = (bf16[4,64,1152]{2,1,0:T(8,128)(2,1)S(1)}, bf16[4,64,1152]{2,1,0:T(8,128)(2,1)S(1)}, u32[]{:S(2)}, u32[]{:S(2)}) collective-permute-start(bf16[4,64,1152]{2,1,0:T(8,128)(2,1)S(1)} %pad_maximum_fusion.refs_0_), channel_id=1, source_target_pairs={{0,128},{128,0},{1,129},{129,1},{2,130},{130,2},{3,131},{131,3},{4... | collective-permute-start | bytes 1769480 | tf_op jit(solution)/shard_map/ppermute | solution.py:205
  60.9 0.8 collective-permute-done.10
  61.7 1.4 collective-permute-start.14
  63.1 1.0 collective-permute-start.13
  64.1 1.8 %collective-permute-start.12 = (bf16[2,64,1152]{2,1,0:T(8,128)(2,1)S(1)}, bf16[2,64,1152]{2,1,0:T(8,128)(2,1)}, u32[]{:S(2)}, u32[]{:S(2)}) collective-permute-start(bf16[2,64,1152]{2,1,0:T(8,128)(2,1)S(1)} %pad_maximum_fusion.1.refs_2_), channel_id=1, source_target_pairs={{0,32},{32,0},{64,96},{96,64},{1,33},{33,1},{65,97},{97,65},{2,34}... | collective-permute-start | bytes 884744 | tf_op jit(solution)/shard_map/ppermute | solution.py:205
  65.9 7.9 %collective-permute-done.14.refs_5_ = bf16[2,64,1152]{2,1,0:T(8,128)(2,1)S(1)} collective-permute-done((bf16[2,64,1152]{2,1,0:T(8,128)(2,1)S(1)}, bf16[2,64,1152]{2,1,0:T(8,128)(2,1)S(1)}, u32[]{:S(2)}, u32[]{:S(2)}) %collective-permute-start.14) | collective-permute-done | bytes 294944 | tf_op jit(solution)/shard_map/ppermute | solution.py:205
  73.9 0.0 collective-permute-start.20
  73.9 0.0 collective-permute-done.11.refs_1_
  73.9 0.5 collective-permute-start.15
  74.4 0.0 collective-permute-start.16
  74.4 0.0 collective-permute-done.13.refs_4_
  74.4 0.5 collective-permute-start.19
  74.9 0.0 collective-permute-done.12.refs_3_
  74.9 0.1 collective-permute-start.18
  75.0 0.8 collective-permute-done.20.refs_11_
  75.8 0.7 copy-done.3
  76.5 0.1 collective-permute-start.17
  76.6 0.1 pad_add_fusion.place_ref
  76.7 0.5 collective-permute-done.19.refs_10_
  77.2 0.8 collective-permute-done.18.refs_9_
  78.0 0.5 collective-permute-done.17.refs_8_
  78.5 0.0 collective-permute-done.15.refs_6_
  78.5 0.0 collective-permute-done.16.refs_7_
  78.5 1.0 copy-done.4
  79.5 2.1 %shard_map.38.matrix_ref = bf16[64,32,1152]{2,1,0:T(8,128)(2,1)S(1)} custom-call(s32[4]{0:T(128)S(1)} %pad_add_fusion.place_ref, bf16[4,64,1152]{2,1,0:T(8,128)(2,1)S(1)} %pad_maximum_fusion.refs_0_, bf16[4,64,1152]{2,1,0:T(8,128)(2,1)S(1)} %collective-permute-done.11.refs_1_, bf16[2,64,1152]{2,1,0:T(8,128)(2,1)S(1)} %pad_maximum_fusion.1.refs_2_, ...), custom_call_target="tpu_custom_call" | custom-call | tf_op jit(solution)/shard_map/pallas_call | solution.py:133
  81.6 0.0 copy-start
  81.6 2.1 %copy-done = bf16[64,32,1152]{2,1,0:T(8,128)(2,1)} copy-done((bf16[64,32,1152]{2,1,0:T(8,128)(2,1)}, bf16[64,32,1152]{2,1,0:T(8,128)(2,1)S(1)}, u32[]{:S(2)}) %copy-start) | copy-done | bytes 4718616
  83.8 0.0 all-to-all-done.1.in_ref
  83.8 0.0 copy-done.5
  83.8 2.3 %copy-done.1 = bf16[64,32,1152]{2,1,0:T(8,128)(2,1)S(1)} copy-done((bf16[64,32,1152]{2,1,0:T(8,128)(2,1)S(1)}, bf16[64,32,1152]{2,1,0:T(8,128)(2,1)}, u32[]{:S(2)}) %copy-start.1) | copy-done | bytes 4718616
  86.1 3.5 %shard_map.39 = bf16[64,104,128]{2,1,0:T(8,128)(2,1)S(1)} custom-call(s32[16]{0:T(128)S(1)} %copy-done.5, bf16[8,8,104,128]{3,2,1,0:T(8,128)(2,1)S(1)} %all-to-all-done.1.in_ref, bf16[64,32,1152]{2,1,0:T(8,128)(2,1)S(1)} %copy-done.1), custom_call_target="tpu_custom_call" | custom-call | tf_op jit(solution)/shard_map/pallas_call | solution.py:194
  89.6 55.0 %all_to_all.15.in_ref = bf16[64,104,128]{2,1,0:T(8,128)(2,1)S(1)} all-to-all(bf16[64,104,128]{2,1,0:T(8,128)(2,1)S(1)} %shard_map.39), channel_id=1, replica_groups=mesh['yh'=2,'x'=4,'zh'=2,'zl'=4,'yl'=2,'c'=2] {'x','zl','yh','zh'}, dimensions={0} | all-to-all | bytes 3407872 | tf_op jit(solution)/shard_map/all_to_all | solution.py:246
  144.6 1.7 %shard_map.40 = bf16[32,25600]{1,0:T(8,128)(2,1)} custom-call(bf16[64,104,128]{2,1,0:T(8,128)(2,1)S(1)} %all_to_all.15.in_ref), custom_call_target="tpu_custom_call" | custom-call | tf_op jit(solution)/shard_map/pallas_call | solution.py:102
  (16 shorter events, 0.3 us)
Async XLA Ops:
  0.0 1.4 copy-start.2
  3.2 7.4 %copy-start.6 = (bf16[8,2048]{1,0:T(8,128)(2,1)S(1)}, bf16[8,2048]{1,0:T(8,128)(2,1)}, u32[]{:S(2)}) copy-start(bf16[8,2048]{1,0:T(8,128)(2,1)} %param.4) | copy-start | bytes 98308
  3.2 35.5 %all-to-all-start = ((bf16[8,8,104,128]{3,2,1,0:T(8,128)(2,1)}), bf16[8,8,104,128]{3,2,1,0:T(8,128)(2,1)S(1)}, u32[]{:S(2)}, u32[]{:S(2)}) async-start(bf16[8,8,104,128]{3,2,1,0:T(8,128)(2,1)} %shard_map.37), calls=%async_computation | async-start | bytes 3407872 | tf_op jit(solution)/shard_map/all_to_all | solution.py:240
  10.6 6.5 %collective-permute-start.2 = (bf16[1,8,2048]{2,1,0:T(8,128)(2,1)S(1)}, bf16[1,8,2048]{2,1,0:T(8,128)(2,1)S(1)}, u32[]{:S(2)}, u32[]{:S(2)}) collective-permute-start(bf16[1,8,2048]{2,1,0:T(8,128)(2,1)S(1)} %bitcast.20), channel_id=1, source_target_pairs={{0,12},{4,8},{8,4},{12,0},{16,28},{20,24},{24,20},{28,16},{1,13},{... | collective-permute-start | bytes 98312 | tf_op jit(solution)/shard_map/ppermute | solution.py:205
  15.2 4.8 %collective-permute-start.1 = (bf16[1,8,2048]{2,1,0:T(8,128)(2,1)S(1)}, bf16[1,8,2048]{2,1,0:T(8,128)(2,1)S(1)}, u32[]{:S(2)}, u32[]{:S(2)}) collective-permute-start(bf16[1,8,2048]{2,1,0:T(8,128)(2,1)S(1)} %bitcast.21), channel_id=1, source_target_pairs={{0,8},{4,12},{8,0},{12,4},{16,24},{20,28},{24,16},{28,20},{1,9},{5... | collective-permute-start | bytes 98312 | tf_op jit(solution)/shard_map/ppermute | solution.py:205
  15.2 4.8 %collective-permute-start = (bf16[1,8,2048]{2,1,0:T(8,128)(2,1)S(1)}, bf16[1,8,2048]{2,1,0:T(8,128)(2,1)S(1)}, u32[]{:S(2)}, u32[]{:S(2)}) collective-permute-start(bf16[1,8,2048]{2,1,0:T(8,128)(2,1)S(1)} %bitcast.22), channel_id=1, source_target_pairs={{0,4},{4,0},{8,12},{12,8},{16,20},{20,16},{24,28},{28,24},{1,5},{5... | collective-permute-start | bytes 98312 | tf_op jit(solution)/shard_map/ppermute | solution.py:205
  20.0 23.7 %collective-permute-start.5 = (bf16[4,8,896]{2,1,0:T(8,128)(2,1)S(1)}, bf16[4,8,896]{2,1,0:T(8,128)(2,1)S(1)}, u32[]{:S(2)}, u32[]{:S(2)}) collective-permute-start(bf16[4,8,896]{2,1,0:T(8,128)(2,1)S(1)} %pad_maximum_fusion.3), channel_id=1, source_target_pairs={{128,112},{132,116},{136,120},{140,124},{144,96},{148,100},{152,10... | collective-permute-start | bytes 172040 | tf_op jit(solution)/shard_map/ppermute | solution.py:213
  28.6 15.2 %collective-permute-start.4 = (bf16[4,8,896]{2,1,0:T(8,128)(2,1)S(1)}, bf16[4,8,896]{2,1,0:T(8,128)(2,1)S(1)}, u32[]{:S(2)}, u32[]{:S(2)}) collective-permute-start(bf16[4,8,896]{2,1,0:T(8,128)(2,1)S(1)} %pad_maximum_fusion.3), channel_id=1, source_target_pairs={{128,96},{132,100},{136,104},{140,108},{144,112},{148,116},{152,12... | collective-permute-start | bytes 172040 | tf_op jit(solution)/shard_map/ppermute | solution.py:213
  29.9 8.8 %collective-permute-start.3 = (bf16[4,8,1152]{2,1,0:T(8,128)(2,1)S(1)}, bf16[4,8,1152]{2,1,0:T(8,128)(2,1)S(1)}, u32[]{:S(2)}, u32[]{:S(2)}) collective-permute-start(bf16[4,8,1152]{2,1,0:T(8,128)(2,1)S(1)} %slice.21), channel_id=1, source_target_pairs={{0,16},{4,20},{8,24},{12,28},{16,0},{20,4},{24,8},{28,12},{1,17},{... | collective-permute-start | bytes 221192 | tf_op jit(solution)/shard_map/ppermute | solution.py:205
  40.1 43.6 %all-to-all-start.1 = ((bf16[8,8,104,128]{3,2,1,0:T(8,128)(2,1)}), bf16[8,8,104,128]{3,2,1,0:T(8,128)(2,1)S(1)}, u32[]{:S(2)}, u32[]{:S(2)}) async-start(bf16[8,8,104,128]{3,2,1,0:T(8,128)(2,1)} %bitcast.11), calls=%async_computation.1 | async-start | bytes 3407872 | tf_op jit(solution)/shard_map/all_to_all | solution.py:245
  43.8 5.2 %collective-permute-start.6 = (bf16[8,8,1152]{2,1,0:T(8,128)(2,1)S(1)}, bf16[8,8,1152]{2,1,0:T(8,128)(2,1)S(1)}, u32[]{:S(2)}, u32[]{:S(2)}) collective-permute-start(bf16[8,8,1152]{2,1,0:T(8,128)(2,1)S(1)} %slice_select_fusion), channel_id=1, source_target_pairs={{0,2},{2,0},{1,3},{3,1},{4,6},{6,4},{5,7},{7,5},{8,10},{10,8},{9,1... | collective-permute-start | bytes 442376 | tf_op jit(solution)/shard_map/ppermute | solution.py:205
  49.2 6.9 %collective-permute-start.9 = (bf16[1,64,1152]{2,1,0:T(8,128)(2,1)S(1)}, bf16[1,64,1152]{2,1,0:T(8,128)(2,1)S(1)}, u32[]{:S(2)}, u32[]{:S(2)}) collective-permute-start(bf16[1,64,1152]{2,1,0:T(8,128)(2,1)S(1)} %bitcast.12), channel_id=1, source_target_pairs={{0,96},{32,64},{64,32},{96,0},{1,97},{33,65},{65,33},{97,1},{2,98}... | collective-permute-start | bytes 442376 | tf_op jit(solution)/shard_map/ppermute | solution.py:205
  51.0 6.6 %collective-permute-start.8 = (bf16[1,64,1152]{2,1,0:T(8,128)(2,1)S(1)}, bf16[1,64,1152]{2,1,0:T(8,128)(2,1)S(1)}, u32[]{:S(2)}, u32[]{:S(2)}) collective-permute-start(bf16[1,64,1152]{2,1,0:T(8,128)(2,1)S(1)} %bitcast.13), channel_id=1, source_target_pairs={{0,64},{32,96},{64,0},{96,32},{1,65},{33,97},{65,1},{97,33},{2,66}... | collective-permute-start | bytes 442376 | tf_op jit(solution)/shard_map/ppermute | solution.py:205
  51.6 6.5 %collective-permute-start.7 = (bf16[1,64,1152]{2,1,0:T(8,128)(2,1)S(1)}, bf16[1,64,1152]{2,1,0:T(8,128)(2,1)S(1)}, u32[]{:S(2)}, u32[]{:S(2)}) collective-permute-start(bf16[1,64,1152]{2,1,0:T(8,128)(2,1)S(1)} %bitcast.14), channel_id=1, source_target_pairs={{0,32},{32,0},{64,96},{96,64},{1,33},{33,1},{65,97},{97,65},{2,34}... | collective-permute-start | bytes 442376 | tf_op jit(solution)/shard_map/ppermute | solution.py:205
  53.4 8.3 %collective-permute-start.10 = (bf16[1,64,1152]{2,1,0:T(8,128)(2,1)S(1)}, bf16[1,64,1152]{2,1,0:T(8,128)(2,1)S(1)}, u32[]{:S(2)}, u32[]{:S(2)}) collective-permute-start(bf16[1,64,1152]{2,1,0:T(8,128)(2,1)S(1)} %bitcast.17), channel_id=1, source_target_pairs={{0,128},{128,0},{1,129},{129,1},{2,130},{130,2},{3,131},{131,3},{4... | collective-permute-start | bytes 442376 | tf_op jit(solution)/shard_map/ppermute | solution.py:205
  58.1 15.7 %collective-permute-start.11 = (bf16[4,64,1152]{2,1,0:T(8,128)(2,1)S(1)}, bf16[4,64,1152]{2,1,0:T(8,128)(2,1)S(1)}, u32[]{:S(2)}, u32[]{:S(2)}) collective-permute-start(bf16[4,64,1152]{2,1,0:T(8,128)(2,1)S(1)} %pad_maximum_fusion.refs_0_), channel_id=1, source_target_pairs={{0,128},{128,0},{1,129},{129,1},{2,130},{130,2},{3,131},{131,3},{4... | collective-permute-start | bytes 1769480 | tf_op jit(solution)/shard_map/ppermute | solution.py:205
  61.7 12.1 %collective-permute-start.14 = (bf16[2,64,1152]{2,1,0:T(8,128)(2,1)S(1)}, bf16[2,64,1152]{2,1,0:T(8,128)(2,1)S(1)}, u32[]{:S(2)}, u32[]{:S(2)}) collective-permute-start(bf16[2,64,1152]{2,1,0:T(8,128)(2,1)S(1)} %pad_maximum_fusion.1.refs_2_), channel_id=1, source_target_pairs={{0,96},{32,64},{64,32},{96,0},{1,97},{33,65},{65,33},{97,1},{2,98}... | collective-permute-start | bytes 884744 | tf_op jit(solution)/shard_map/ppermute | solution.py:205
  63.1 11.3 %collective-permute-start.13 = (bf16[2,64,1152]{2,1,0:T(8,128)(2,1)S(1)}, bf16[2,64,1152]{2,1,0:T(8,128)(2,1)}, u32[]{:S(2)}, u32[]{:S(2)}) collective-permute-start(bf16[2,64,1152]{2,1,0:T(8,128)(2,1)S(1)} %pad_maximum_fusion.1.refs_2_), channel_id=1, source_target_pairs={{0,64},{32,96},{64,0},{96,32},{1,65},{33,97},{65,1},{97,33},{2,66}... | collective-permute-start | bytes 884744 | tf_op jit(solution)/shard_map/ppermute | solution.py:205
  64.1 10.8 %collective-permute-start.12 = (bf16[2,64,1152]{2,1,0:T(8,128)(2,1)S(1)}, bf16[2,64,1152]{2,1,0:T(8,128)(2,1)}, u32[]{:S(2)}, u32[]{:S(2)}) collective-permute-start(bf16[2,64,1152]{2,1,0:T(8,128)(2,1)S(1)} %pad_maximum_fusion.1.refs_2_), channel_id=1, source_target_pairs={{0,32},{32,0},{64,96},{96,64},{1,33},{33,1},{65,97},{97,65},{2,34}... | collective-permute-start | bytes 884744 | tf_op jit(solution)/shard_map/ppermute | solution.py:205
  73.9 1.9 %collective-permute-start.20 = (bf16[2,64,1152]{2,1,0:T(8,128)(2,1)S(1)}, bf16[2,64,1152]{2,1,0:T(8,128)(2,1)S(1)}, u32[]{:S(2)}, u32[]{:S(2)}) collective-permute-start(bf16[2,64,1152]{2,1,0:T(8,128)(2,1)S(1)} %collective-permute-done.14.refs_5_), channel_id=1, source_target_pairs={{0,1},{1,0},{2,3},{3,2},{4,5},{5,4},{6,7},{7,6},{8,9},{9,8},{10,11... | collective-permute-start | bytes 884744 | tf_op jit(solution)/shard_map/ppermute | solution.py:205
  73.9 4.7 %collective-permute-start.15 = (bf16[4,64,1152]{2,1,0:T(8,128)(2,1)S(1)}, bf16[4,64,1152]{2,1,0:T(8,128)(2,1)}, u32[]{:S(2)}, u32[]{:S(2)}) collective-permute-start(bf16[4,64,1152]{2,1,0:T(8,128)(2,1)S(1)} %pad_maximum_fusion.refs_0_), channel_id=1, source_target_pairs={{0,1},{1,0},{2,3},{3,2},{4,5},{5,4},{6,7},{7,6},{8,9},{9,8},{10,11... | collective-permute-start | bytes 1769480 | tf_op jit(solution)/shard_map/ppermute | solution.py:205
  74.4 4.2 %collective-permute-start.16 = (bf16[4,64,1152]{2,1,0:T(8,128)(2,1)S(1)}, bf16[4,64,1152]{2,1,0:T(8,128)(2,1)}, u32[]{:S(2)}, u32[]{:S(2)}) collective-permute-start(bf16[4,64,1152]{2,1,0:T(8,128)(2,1)S(1)} %collective-permute-done.11.refs_1_), channel_id=1, source_target_pairs={{0,1},{1,0},{2,3},{3,2},{4,5},{5,4},{6,7},{7,6},{8,9},{9,8},{10,11... | collective-permute-start | bytes 1769480 | tf_op jit(solution)/shard_map/ppermute | solution.py:205
  74.4 2.8 %collective-permute-start.19 = (bf16[2,64,1152]{2,1,0:T(8,128)(2,1)}, bf16[2,64,1152]{2,1,0:T(8,128)(2,1)}, u32[]{:S(2)}, u32[]{:S(2)}) collective-permute-start(bf16[2,64,1152]{2,1,0:T(8,128)(2,1)} %collective-permute-done.13.refs_4_), channel_id=1, source_target_pairs={{0,1},{1,0},{2,3},{3,2},{4,5},{5,4},{6,7},{7,6},{8,9},{9,8},{10,11... | collective-permute-start | bytes 884744 | tf_op jit(solution)/shard_map/ppermute | solution.py:205
  74.9 3.1 %collective-permute-start.18 = (bf16[2,64,1152]{2,1,0:T(8,128)(2,1)}, bf16[2,64,1152]{2,1,0:T(8,128)(2,1)}, u32[]{:S(2)}, u32[]{:S(2)}) collective-permute-start(bf16[2,64,1152]{2,1,0:T(8,128)(2,1)} %collective-permute-done.12.refs_3_), channel_id=1, source_target_pairs={{0,1},{1,0},{2,3},{3,2},{4,5},{5,4},{6,7},{7,6},{8,9},{9,8},{10,11... | collective-permute-start | bytes 884744 | tf_op jit(solution)/shard_map/ppermute | solution.py:205
  75.8 0.7 copy-start.3
  76.5 2.0 %collective-permute-start.17 = (bf16[2,64,1152]{2,1,0:T(8,128)(2,1)S(1)}, bf16[2,64,1152]{2,1,0:T(8,128)(2,1)}, u32[]{:S(2)}, u32[]{:S(2)}) collective-permute-start(bf16[2,64,1152]{2,1,0:T(8,128)(2,1)S(1)} %pad_maximum_fusion.1.refs_2_), channel_id=1, source_target_pairs={{0,1},{1,0},{2,3},{3,2},{4,5},{5,4},{6,7},{7,6},{8,9},{9,8},{10,11... | collective-permute-start | bytes 884744 | tf_op jit(solution)/shard_map/ppermute | solution.py:205
  76.6 7.1 %copy-start.5 = (s32[16]{0:T(128)S(1)}, s32[16]{0:T(128)}, u32[]{:S(2)}) copy-start(s32[16]{0:T(128)} %locked_ref.1) | copy-start | bytes 196
  78.5 1.0 copy-start.4
  81.6 2.2 %copy-start = (bf16[64,32,1152]{2,1,0:T(8,128)(2,1)}, bf16[64,32,1152]{2,1,0:T(8,128)(2,1)S(1)}, u32[]{:S(2)}) copy-start(bf16[64,32,1152]{2,1,0:T(8,128)(2,1)S(1)} %shard_map.38.matrix_ref) | copy-start | bytes 14155780
  83.8 2.3 %copy-start.1 = (bf16[64,32,1152]{2,1,0:T(8,128)(2,1)S(1)}, bf16[64,32,1152]{2,1,0:T(8,128)(2,1)}, u32[]{:S(2)}) copy-start(bf16[64,32,1152]{2,1,0:T(8,128)(2,1)} %copy-done) | copy-start | bytes 14155780

commit v3 on v2

--- a/solution.py
+++ b/solution.py
@@ -57,27 +57,57 @@
     return total
 
 
-def pack_kernel(in_ref, out_ref):
+def pack_kernel(source_ref, target_ref, in_ref, out_ref, in_sems, out_sems):
+    spans = [(24576, 1024)] + [(3072 * group, 3072) for group in range(8)]
+    loads = []
+    for index, (column, width) in enumerate(spans):
+        columns = (slice(None), pl.ds(column, width))
+        loads.append(pltpu.make_async_copy(source_ref.at[columns], in_ref.at[columns], in_sems.at[index]))
+        loads[-1].start()
+    loads[0].wait()
+    stores = []
     for group in range(8):
         column = 24576 + 128 * group
         groups = regroup(in_ref[:, column : column + 128].astype(F32))
         for z in range(8):
+            out_ref[group, seat(z), 96:104, :] = gather_lanes(groups, z).astype(BF16)
+        loads[1 + group].wait()
+        for z in range(8):
             for t in range(TILES):
                 column = (TILES * (8 * group + z) + t) * 128
                 out_ref[group, seat(z), 32 * t : 32 * t + 32, :] = in_ref[:, column : column + 128]
-            out_ref[group, seat(z), 96:104, :] = gather_lanes(groups, z).astype(BF16)
+        stores.append(pltpu.make_async_copy(out_ref.at[group], target_ref.at[group], out_sems.at[group]))
+        stores[-1].start()
+    for store in stores:
+        store.wait()
 
 
 def pack(vectors):
+    anywhere = pl.BlockSpec(memory_space=pl.ANY)
     return pl.pallas_call(
         pack_kernel,
+        in_specs=[anywhere],
+        out_specs=anywhere,
         out_shape=jax.ShapeDtypeStruct((8, 8, CHUNK, 128), BF16),
-        compiler_params=pltpu.CompilerParams(vmem_limit_bytes=16 * 1024 * 1024),
+        scratch_shapes=[
+            pltpu.VMEM((ROWS, 25600), BF16),
+            pltpu.VMEM((8, 8, CHUNK, 128), BF16),
+            pltpu.SemaphoreType.DMA((9,)),
+            pltpu.SemaphoreType.DMA((8,)),
+        ],
+        compiler_params=pltpu.CompilerParams(vmem_limit_bytes=60 * 1024 * 1024),
     )(vectors)
 
 
-def unpack_kernel(in_ref, out_ref):
+def unpack_kernel(in_ref, target_ref, out_ref, sems):
     lanes, low = lane_group(), low_half()
+    stores = []
+
+    def store(column, width):
+        columns = (slice(None), pl.ds(column, width))
+        stores.append(pltpu.make_async_copy(out_ref.at[columns], target_ref.at[columns], sems.at[len(stores)]))
+        stores[-1].start()
+
     for group in range(8):
         lefts = []
         for z in range(8):
@@ -86,6 +116,7 @@
                 column = (TILES * (8 * group + z) + t) * 128
                 out_ref[:, column : column + 128] = in_ref[seat_of, 32 * t : 32 * t + 32, :]
             lefts.append(in_ref[seat_of, 96:104, :].astype(F32))
+        store(3072 * group, 3072)
         pieces = []
         for k in range(4):
             total = jnp.zeros((8, 128), F32)
@@ -96,36 +127,50 @@
             pieces.append(total)
         column = 24576 + 128 * group
         out_ref[:, column : column + 128] = jnp.concatenate(pieces, axis=0).astype(BF16)
+    store(24576, 1024)
+    for copy in stores:
+        copy.wait()
 
 
 def unpack(received):
     return pl.pallas_call(
         unpack_kernel,
+        in_specs=[pl.BlockSpec(memory_space=pltpu.VMEM)],
+        out_specs=pl.BlockSpec(memory_space=pl.ANY),
         out_shape=jax.ShapeDtypeStruct((ROWS, 25600), BF16),
+        scratch_shapes=[pltpu.VMEM((ROWS, 25600), BF16), pltpu.SemaphoreType.DMA((9,))],
         compiler_params=pltpu.CompilerParams(vmem_limit_bytes=16 * 1024 * 1024),
     )(received)
 
 
 def place_kernel(place_ref, *refs):
-    panels, out_ref = refs[:12], refs[12]
+    panels, (out_ref, matrix_ref, sems) = refs[:12], refs[12:]
     core, yh, x, z = (place_ref[i] for i in range(4))
 
-    def fill(first_side):
-        for first in range(2):
-            for dx in range(4):
-                group = (yh ^ first) * 4 + (x ^ dx)
-                for step in range(8):
-                    which, at = (first, dx) if step < 4 else (2 + dx, first)
-                    row = 16 * (step % 4)
-                    low, high = (panels[6 * side + which][at, row : row + 16, :].astype(F32) for side in (first_side, 1 - first_side))
-                    rows = jnp.concatenate([low[:8], high[:8], low[8:], high[8:]], axis=0)
-                    out_ref[group * 8 + (z ^ step)] = rows.astype(BF16)
-
-    for side in range(2):
-        pl.when(core == side)(functools.partial(fill, side))
-    for group in range(8):
-        slot, column = (group, 256 * group + 128) if group < 4 else (7 - group, 256 * (8 - group) + 128 * (2 * group - 8))
-        out_ref[8 * slot : 8 * slot + 4, :, column : column + 128] = jnp.zeros((4, ROWS, 128), BF16)
+    def copy(group, index):
+        part = pl.ds(8 * group, 8)
+        return pltpu.make_async_copy(matrix_ref.at[part], out_ref.at[part], sems.at[index])
+
+    def fill(group, first, dx, first_side):
+        for step in range(8):
+            which, at = (first, dx) if step < 4 else (2 + dx, first)
+            row = 16 * (step % 4)
+            low, high = (panels[6 * side + which][at, row : row + 16, :].astype(F32) for side in (first_side, 1 - first_side))
+            rows = jnp.concatenate([low[:8], high[:8], low[8:], high[8:]], axis=0)
+            matrix_ref[group * 8 + (z ^ step)] = rows.astype(BF16)
+
+    def mask(group):
+        for column in (pl.multiple_of(256 * group + 128, 128), 1024):
+            matrix_ref[pl.ds(8 * group, 4), :, pl.ds(column, 128)] = jnp.zeros((4, ROWS, 128), BF16)
+
+    groups = [((yh ^ first) * 4 + (x ^ dx), first, dx) for first in range(2) for dx in range(4)]
+    for index, (group, first, dx) in enumerate(groups):
+        for side in range(2):
+            pl.when(core == side)(functools.partial(fill, group, first, dx, side))
+        pl.when(group < 4)(functools.partial(mask, group))
+        copy(group, index).start()
+    for index, (group, first, dx) in enumerate(groups):
+        copy(group, index).wait()
 
 
 def place_panels(place, panels):
@@ -133,13 +178,19 @@
     return pl.pallas_call(
         place_kernel,
         in_specs=[pl.BlockSpec(memory_space=pltpu.SMEM)] + [vmem] * 12,
-        out_specs=vmem,
+        out_specs=pl.BlockSpec(memory_space=pl.ANY),
         out_shape=jax.ShapeDtypeStruct((PEERS, ROWS, KEEP), BF16),
-        compiler_params=pltpu.CompilerParams(vmem_limit_bytes=16 * 1024 * 1024),
+        scratch_shapes=[pltpu.VMEM((PEERS, ROWS, KEEP), BF16), pltpu.SemaphoreType.DMA((8,))],
+        compiler_params=pltpu.CompilerParams(vmem_limit_bytes=50 * 1024 * 1024),
     )(place, *panels)
 
 
-def rotate_kernel(locked_ref, in_ref, matrix_ref, out_ref, held):
+def rotate_kernel(locked_ref, in_ref, source_ref, out_ref, held, matrix_ref, sems):
+    copies = []
+    for group in range(8):
+        part = pl.ds(8 * group, 8)
+        copies.append(pltpu.make_async_copy(source_ref.at[part], matrix_ref.at[part], sems.at[group]))
+        copies[-1].start()
     low64 = lax.broadcasted_iota(jnp.int32, (64, 128), 0) % 8 < 4
     for group in range(8):
         rows = slice(256 * group, 256 * group + 256)
@@ -161,7 +212,9 @@
     def panel(group, column, width, groups=1):
         return matrix_ref[8 * group : 8 * (group + groups), :, column : column + width].reshape(256 * groups, width)
 
-    for block in range(8):
+    for block in range(7, -1, -1):
+        for copy in copies[7 - block : 8 - block] if block > 4 else copies[3:] if block == 4 else ():
+            copy.wait()
         total = None
         terms = []
         if block < 4:
@@ -193,11 +246,15 @@
     vmem = pl.BlockSpec(memory_space=pltpu.VMEM)
     return pl.pallas_call(
         rotate_kernel,
-        in_specs=[pl.BlockSpec(memory_space=pltpu.SMEM), vmem, vmem],
+        in_specs=[pl.BlockSpec(memory_space=pltpu.SMEM), vmem, pl.BlockSpec(memory_space=pl.ANY)],
         out_specs=vmem,
         out_shape=jax.ShapeDtypeStruct((PEERS, CHUNK, 128), BF16),
-        scratch_shapes=[pltpu.VMEM((PEERS * ROWS, WIDTH), BF16)],
-        compiler_params=pltpu.CompilerParams(vmem_limit_bytes=16 * 1024 * 1024),
+        scratch_shapes=[
+            pltpu.VMEM((PEERS * ROWS, WIDTH), BF16),
+            pltpu.VMEM((PEERS, ROWS, KEEP), BF16),
+            pltpu.SemaphoreType.DMA((8,)),
+        ],
+        compiler_params=pltpu.CompilerParams(vmem_limit_bytes=50 * 1024 * 1024),
     )(locked, received, matrix)
 
 
@@ -231,7 +288,7 @@
     a = jnp.concatenate([a] + [exchange(a, "x", 4, dx) for dx in (1, 2, 3)])
     far_a = exchange(a, "yh", 2, 1)
     far_b = [exchange(b, "x", 4, dx) for dx in (1, 2, 3)]
-    a, b, far_a = lax.optimization_barrier((a, b, far_a))
+    a, b, far_b[2] = lax.optimization_barrier((a, b, far_b[2]))
     own = [a, far_a, b] + far_b
     return own + [exchange(panel, "c", 2, 1) for panel in own]
 

time: 147 us -> 145 us (0.986)
  local copies, waits for them, and re-layouts: 9.09 us -> 3.19 us
  Pallas kernels: 8.98 us -> 13.1 us
    unnamed x14 -> x8, local copies, waits for them, and re-layouts: 7.59 us -> 1.68 us
    pallas_call x1, Pallas kernels: 2.1 us -> 3.97 us  [place_panels(): pl.pallas_call(place_kernel, in_specs=[pl.BlockSpec(memory_space=pltpu.SM...]
    pallas_call x1, Pallas kernels: 3.48 us -> 5.25 us  [rotate(): pl.pallas_call(rotate_kernel, in_specs=[pl.BlockSpec(memory_space=pltpu.S...]
  transfers between devices with their start and end apart: 23 -> 23, of which waited for: 12 -> 12; matrix products, arithmetic and copies ran while one was open for 1% -> 1% of each run, Pallas kernels for 1% -> 3%
where the time goes in v3:
time: 145 us
  blocking collectives  55 us (38%)
  starting transfers between devices  43 us (30%)
  waiting for transfers between devices  29.7 us (20%)
  Pallas kernels  13.1 us (9%)
  local copies, waits for them, and re-layouts  3.19 us (2%)
    all_to_all x1, blocking collectives, body(): lax.all_to_all(rotate(locked, received, matrix), ('x', 'zl', 'yh', 'zh'),...  55 us
    ppermute x19, waiting for transfers between devices, exchange(): return lax.ppermute(value, axis, [(i, i ^ mask) for i in range(size)])  29.7 us
    ppermute x19, starting transfers between devices, exchange(): return lax.ppermute(value, axis, [(i, i ^ mask) for i in range(size)])  22.4 us
    ppermute x2, starting transfers between devices, gather_near(): lax.ppermute(spare, EIG, [(i, (7 - i // 8) * 8 + (i % 8 ^ far)) for i in...  9.82 us
    all_to_all x1, starting transfers between devices, body(): lax.all_to_all(pack(vectors), ('yh', 'x'), split_axis=0, concat_axis=0, t...  7.28 us
    pallas_call x1, Pallas kernels, rotate(): pl.pallas_call(rotate_kernel, in_specs=[pl.BlockSpec(memory_space=pltpu.S...  5.25 us
    pallas_call x1, Pallas kernels, place_panels(): pl.pallas_call(place_kernel, in_specs=[pl.BlockSpec(memory_space=pltpu.SM...  3.97 us
    all_to_all x1, starting transfers between devices, body(): lax.all_to_all(halfway.transpose(1, 0, 2, 3), ('zl', 'zh'), split_axis=0,...  3.59 us
  transfers between devices with their start and end apart: 23, of which 12 were waited for; matrix products, arithmetic and copies ran while one was open for 1% of the time, Pallas kernels for 3%

profile of v3, /device:TPU:16, one launch (start us, length us, event | category | flops | bytes accessed | tf_op | source)
XLA Modules:
  0.0 144.7 jit_solution(8297252342808226807)
XLA Ops:
  0.0 2.6 %shard_map.37 = bf16[8,8,104,128]{3,2,1,0:T(8,128)(2,1)} custom-call(bf16[32,25600]{1,0:T(8,128)(2,1)} %source_ref.1), custom_call_target="tpu_custom_call" | custom-call | tf_op jit(solution)/shard_map/pallas_call | solution.py:87
  2.6 0.0 copy-start.3
  2.6 7.3 %all-to-all-start = ((bf16[8,8,104,128]{3,2,1,0:T(8,128)(2,1)}), bf16[8,8,104,128]{3,2,1,0:T(8,128)(2,1)S(1)}, u32[]{:S(2)}, u32[]{:S(2)}) async-start(bf16[8,8,104,128]{3,2,1,0:T(8,128)(2,1)} %shard_map.37), calls=%async_computation | async-start | bytes 3407872 | tf_op jit(solution)/shard_map/all_to_all | solution.py:297
  9.9 0.0 copy-done.3
  9.9 4.6 %collective-permute-start.2 = (bf16[1,8,2048]{2,1,0:T(8,128)(2,1)S(1)}, bf16[1,8,2048]{2,1,0:T(8,128)(2,1)S(1)}, u32[]{:S(2)}, u32[]{:S(2)}) collective-permute-start(bf16[1,8,2048]{2,1,0:T(8,128)(2,1)S(1)} %bitcast.20), channel_id=1, source_target_pairs={{0,12},{4,8},{8,4},{12,0},{16,28},{20,24},{24,20},{28,16},{1,13},{... | collective-permute-start | bytes 98312 | tf_op jit(solution)/shard_map/ppermute | solution.py:262
  14.5 0.0 collective-permute-start.1
  14.5 0.7 collective-permute-start
  15.1 1.3 collective-permute-done.2
  16.4 2.9 %collective-permute-done.1 = bf16[1,8,2048]{2,1,0:T(8,128)(2,1)S(1)} collective-permute-done((bf16[1,8,2048]{2,1,0:T(8,128)(2,1)S(1)}, bf16[1,8,2048]{2,1,0:T(8,128)(2,1)S(1)}, u32[]{:S(2)}, u32[]{:S(2)}) %collective-permute-start.1) | collective-permute-done | bytes 32800 | tf_op jit(solution)/shard_map/ppermute | solution.py:262
  19.3 0.0 collective-permute-done
  19.3 8.5 %collective-permute-start.5 = (bf16[4,8,896]{2,1,0:T(8,128)(2,1)S(1)}, bf16[4,8,896]{2,1,0:T(8,128)(2,1)S(1)}, u32[]{:S(2)}, u32[]{:S(2)}) collective-permute-start(bf16[4,8,896]{2,1,0:T(8,128)(2,1)S(1)} %pad_maximum_fusion.3), channel_id=1, source_target_pairs={{128,112},{132,116},{136,120},{140,124},{144,96},{148,100},{152,10... | collective-permute-start | bytes 172040 | tf_op jit(solution)/shard_map/ppermute | solution.py:270
  27.8 1.3 collective-permute-start.4
  29.2 1.5 %collective-permute-start.3 = (bf16[4,8,1152]{2,1,0:T(8,128)(2,1)S(1)}, bf16[4,8,1152]{2,1,0:T(8,128)(2,1)S(1)}, u32[]{:S(2)}, u32[]{:S(2)}) collective-permute-start(bf16[4,8,1152]{2,1,0:T(8,128)(2,1)S(1)} %slice.21), channel_id=1, source_target_pairs={{0,16},{4,20},{8,24},{12,28},{16,0},{20,4},{24,8},{28,12},{1,17},{... | collective-permute-start | bytes 221192 | tf_op jit(solution)/shard_map/ppermute | solution.py:262
  30.7 7.3 %collective-permute-done.3 = bf16[4,8,1152]{2,1,0:T(8,128)(2,1)S(1)} collective-permute-done((bf16[4,8,1152]{2,1,0:T(8,128)(2,1)S(1)}, bf16[4,8,1152]{2,1,0:T(8,128)(2,1)S(1)}, u32[]{:S(2)}, u32[]{:S(2)}) %collective-permute-start.3) | collective-permute-done | bytes 73760 | tf_op jit(solution)/shard_map/ppermute | solution.py:262
  38.0 0.0 all-to-all-done
  38.0 1.4 copy.11
  39.4 3.6 %all-to-all-start.1 = ((bf16[8,8,104,128]{3,2,1,0:T(8,128)(2,1)}), bf16[8,8,104,128]{3,2,1,0:T(8,128)(2,1)S(1)}, u32[]{:S(2)}, u32[]{:S(2)}) async-start(bf16[8,8,104,128]{3,2,1,0:T(8,128)(2,1)} %bitcast.11), calls=%async_computation.1 | async-start | bytes 3407872 | tf_op jit(solution)/shard_map/all_to_all | solution.py:302
  43.0 0.0 collective-permute-done.5
  43.0 0.0 collective-permute-done.4
  43.1 1.4 collective-permute-start.6
  44.5 3.9 %collective-permute-done.6 = bf16[8,8,1152]{2,1,0:T(8,128)(2,1)S(1)} collective-permute-done((bf16[8,8,1152]{2,1,0:T(8,128)(2,1)S(1)}, bf16[8,8,1152]{2,1,0:T(8,128)(2,1)S(1)}, u32[]{:S(2)}, u32[]{:S(2)}) %collective-permute-start.6) | collective-permute-done | bytes 147488 | tf_op jit(solution)/shard_map/ppermute | solution.py:262
  48.5 1.9 %collective-permute-start.9 = (bf16[1,64,1152]{2,1,0:T(8,128)(2,1)S(1)}, bf16[1,64,1152]{2,1,0:T(8,128)(2,1)S(1)}, u32[]{:S(2)}, u32[]{:S(2)}) collective-permute-start(bf16[1,64,1152]{2,1,0:T(8,128)(2,1)S(1)} %bitcast.12), channel_id=1, source_target_pairs={{0,96},{32,64},{64,32},{96,0},{1,97},{33,65},{65,33},{97,1},{2,98}... | collective-permute-start | bytes 442376 | tf_op jit(solution)/shard_map/ppermute | solution.py:262
  50.3 0.5 collective-permute-start.8
  50.9 1.8 %collective-permute-start.7 = (bf16[1,64,1152]{2,1,0:T(8,128)(2,1)S(1)}, bf16[1,64,1152]{2,1,0:T(8,128)(2,1)S(1)}, u32[]{:S(2)}, u32[]{:S(2)}) collective-permute-start(bf16[1,64,1152]{2,1,0:T(8,128)(2,1)S(1)} %bitcast.14), channel_id=1, source_target_pairs={{0,32},{32,0},{64,96},{96,64},{1,33},{33,1},{65,97},{97,65},{2,34}... | collective-permute-start | bytes 442376 | tf_op jit(solution)/shard_map/ppermute | solution.py:262
  52.7 2.7 %collective-permute-start.10 = (bf16[1,64,1152]{2,1,0:T(8,128)(2,1)S(1)}, bf16[1,64,1152]{2,1,0:T(8,128)(2,1)S(1)}, u32[]{:S(2)}, u32[]{:S(2)}) collective-permute-start(bf16[1,64,1152]{2,1,0:T(8,128)(2,1)S(1)} %bitcast.17), channel_id=1, source_target_pairs={{0,128},{128,0},{1,129},{129,1},{2,130},{130,2},{3,131},{131,3},{4... | collective-permute-start | bytes 442376 | tf_op jit(solution)/shard_map/ppermute | solution.py:262
  55.4 0.0 collective-permute-done.9
  55.4 1.6 %collective-permute-done.8 = bf16[1,64,1152]{2,1,0:T(8,128)(2,1)S(1)} collective-permute-done((bf16[1,64,1152]{2,1,0:T(8,128)(2,1)S(1)}, bf16[1,64,1152]{2,1,0:T(8,128)(2,1)S(1)}, u32[]{:S(2)}, u32[]{:S(2)}) %collective-permute-start.8) | collective-permute-done | bytes 147488 | tf_op jit(solution)/shard_map/ppermute | solution.py:262
  57.0 0.4 collective-permute-done.7
  57.3 0.1 pad_maximum_fusion.refs_0_
  57.4 2.7 %collective-permute-start.12 = (bf16[4,64,1152]{2,1,0:T(8,128)(2,1)S(1)}, bf16[4,64,1152]{2,1,0:T(8,128)(2,1)S(1)}, u32[]{:S(2)}, u32[]{:S(2)}) collective-permute-start(bf16[4,64,1152]{2,1,0:T(8,128)(2,1)S(1)} %pad_maximum_fusion.refs_0_), channel_id=1, source_target_pairs={{0,128},{128,0},{1,129},{129,1},{2,130},{130,2},{3,131},{131,3},{4... | collective-permute-start | bytes 1769480 | tf_op jit(solution)/shard_map/ppermute | solution.py:262
  60.2 0.8 collective-permute-done.10
  61.0 0.8 collective-permute-start.14
  61.8 2.2 %collective-permute-start.11 = (bf16[2,64,1152]{2,1,0:T(8,128)(2,1)S(1)}, bf16[2,64,1152]{2,1,0:T(8,128)(2,1)}, u32[]{:S(2)}, u32[]{:S(2)}) collective-permute-start(bf16[2,64,1152]{2,1,0:T(8,128)(2,1)S(1)} %pad_maximum_fusion.1.refs_2_), channel_id=1, source_target_pairs={{0,96},{32,64},{64,32},{96,0},{1,97},{33,65},{65,33},{97,1},{2,98}... | collective-permute-start | bytes 884744 | tf_op jit(solution)/shard_map/ppermute | solution.py:262
  64.0 0.6 collective-permute-start.13
  64.6 5.8 %collective-permute-done.14.refs_4_ = bf16[2,64,1152]{2,1,0:T(8,128)(2,1)S(1)} collective-permute-done((bf16[2,64,1152]{2,1,0:T(8,128)(2,1)S(1)}, bf16[2,64,1152]{2,1,0:T(8,128)(2,1)S(1)}, u32[]{:S(2)}, u32[]{:S(2)}) %collective-permute-start.14) | collective-permute-done | bytes 294944 | tf_op jit(solution)/shard_map/ppermute | solution.py:262
  70.4 0.0 collective-permute-start.19
  70.4 3.2 %collective-permute-done.11.refs_5_ = bf16[2,64,1152]{2,1,0:T(8,128)(2,1)} collective-permute-done((bf16[2,64,1152]{2,1,0:T(8,128)(2,1)S(1)}, bf16[2,64,1152]{2,1,0:T(8,128)(2,1)}, u32[]{:S(2)}, u32[]{:S(2)}) %collective-permute-start.11) | collective-permute-done | bytes 294944 | tf_op jit(solution)/shard_map/ppermute | solution.py:262
  73.5 0.0 collective-permute-start.15
  73.5 0.0 collective-permute-done.12.refs_1_
  73.5 0.5 collective-permute-start.16
  74.1 0.0 collective-permute-start.17
  74.1 0.0 collective-permute-done.13.refs_3_
  74.1 0.5 collective-permute-start.18
  74.6 0.0 collective-permute-done.19.refs_10_
  74.6 0.0 copy-start
  74.6 0.7 copy-done
  75.3 0.0 collective-permute-start.20
  75.3 0.0 copy-start.2
  75.3 0.1 pad_add_fusion.place_ref
  75.4 1.8 %collective-permute-done.18.refs_9_ = bf16[2,64,1152]{2,1,0:T(8,128)(2,1)} collective-permute-done((bf16[2,64,1152]{2,1,0:T(8,128)(2,1)}, bf16[2,64,1152]{2,1,0:T(8,128)(2,1)}, u32[]{:S(2)}, u32[]{:S(2)}) %collective-permute-start.18) | collective-permute-done | bytes 294944 | tf_op jit(solution)/shard_map/ppermute | solution.py:262
  77.2 0.6 collective-permute-done.17.refs_8_
  77.8 0.2 collective-permute-done.20.refs_11_
  78.0 0.0 collective-permute-done.15.refs_6_
  78.0 0.0 collective-permute-done.16.refs_7_
  78.0 0.0 copy-start.1
  78.0 1.0 copy-done.1
  79.0 4.0 %shard_map.38.source_ref = bf16[64,32,1152]{2,1,0:T(8,128)(2,1)} custom-call(s32[4]{0:T(128)S(1)} %pad_add_fusion.place_ref, bf16[4,64,1152]{2,1,0:T(8,128)(2,1)S(1)} %pad_maximum_fusion.refs_0_, bf16[4,64,1152]{2,1,0:T(8,128)(2,1)S(1)} %collective-permute-done.12.refs_1_, bf16[2,64,1152]{2,1,0:T(8,128)(2,1)S(1)} %pad_maximum_fusion.1.refs_2_, ...), custom_call_target="tpu_custom_call" | custom-call | tf_op jit(solution)/shard_map/pallas_call | solution.py:178
  82.9 0.0 all-to-all-done.1.in_ref
  83.0 0.0 copy-done.2
  83.0 5.3 %shard_map.39 = bf16[64,104,128]{2,1,0:T(8,128)(2,1)S(1)} custom-call(s32[16]{0:T(128)S(1)} %copy-done.2, bf16[8,8,104,128]{3,2,1,0:T(8,128)(2,1)S(1)} %all-to-all-done.1.in_ref, bf16[64,32,1152]{2,1,0:T(8,128)(2,1)} %shard_map.38.source_ref), custom_call_target="tpu_custom_call" | custom-call | tf_op jit(solution)/shard_map/pallas_call | solution.py:247
  88.2 55.0 %all_to_all.15.in_ref = bf16[64,104,128]{2,1,0:T(8,128)(2,1)S(1)} all-to-all(bf16[64,104,128]{2,1,0:T(8,128)(2,1)S(1)} %shard_map.39), channel_id=1, replica_groups=mesh['yh'=2,'x'=4,'zh'=2,'zl'=4,'yl'=2,'c'=2] {'x','zl','yh','zh'}, dimensions={0} | all-to-all | bytes 3407872 | tf_op jit(solution)/shard_map/all_to_all | solution.py:303
  143.3 1.3 shard_map.40
  (12 shorter events, 0.3 us)
Async XLA Ops:
  2.6 7.3 %copy-start.3 = (bf16[8,2048]{1,0:T(8,128)(2,1)S(1)}, bf16[8,2048]{1,0:T(8,128)(2,1)}, u32[]{:S(2)}) copy-start(bf16[8,2048]{1,0:T(8,128)(2,1)} %param.4) | copy-start | bytes 98308
  2.6 35.4 %all-to-all-start = ((bf16[8,8,104,128]{3,2,1,0:T(8,128)(2,1)}), bf16[8,8,104,128]{3,2,1,0:T(8,128)(2,1)S(1)}, u32[]{:S(2)}, u32[]{:S(2)}) async-start(bf16[8,8,104,128]{3,2,1,0:T(8,128)(2,1)} %shard_map.37), calls=%async_computation | async-start | bytes 3407872 | tf_op jit(solution)/shard_map/all_to_all | solution.py:297
  9.9 6.5 %collective-permute-start.2 = (bf16[1,8,2048]{2,1,0:T(8,128)(2,1)S(1)}, bf16[1,8,2048]{2,1,0:T(8,128)(2,1)S(1)}, u32[]{:S(2)}, u32[]{:S(2)}) collective-permute-start(bf16[1,8,2048]{2,1,0:T(8,128)(2,1)S(1)} %bitcast.20), channel_id=1, source_target_pairs={{0,12},{4,8},{8,4},{12,0},{16,28},{20,24},{24,20},{28,16},{1,13},{... | collective-permute-start | bytes 98312 | tf_op jit(solution)/shard_map/ppermute | solution.py:262
  14.5 4.8 %collective-permute-start.1 = (bf16[1,8,2048]{2,1,0:T(8,128)(2,1)S(1)}, bf16[1,8,2048]{2,1,0:T(8,128)(2,1)S(1)}, u32[]{:S(2)}, u32[]{:S(2)}) collective-permute-start(bf16[1,8,2048]{2,1,0:T(8,128)(2,1)S(1)} %bitcast.21), channel_id=1, source_target_pairs={{0,8},{4,12},{8,0},{12,4},{16,24},{20,28},{24,16},{28,20},{1,9},{5... | collective-permute-start | bytes 98312 | tf_op jit(solution)/shard_map/ppermute | solution.py:262
  14.5 4.8 %collective-permute-start = (bf16[1,8,2048]{2,1,0:T(8,128)(2,1)S(1)}, bf16[1,8,2048]{2,1,0:T(8,128)(2,1)S(1)}, u32[]{:S(2)}, u32[]{:S(2)}) collective-permute-start(bf16[1,8,2048]{2,1,0:T(8,128)(2,1)S(1)} %bitcast.22), channel_id=1, source_target_pairs={{0,4},{4,0},{8,12},{12,8},{16,20},{20,16},{24,28},{28,24},{1,5},{5... | collective-permute-start | bytes 98312 | tf_op jit(solution)/shard_map/ppermute | solution.py:262
  19.3 23.7 %collective-permute-start.5 = (bf16[4,8,896]{2,1,0:T(8,128)(2,1)S(1)}, bf16[4,8,896]{2,1,0:T(8,128)(2,1)S(1)}, u32[]{:S(2)}, u32[]{:S(2)}) collective-permute-start(bf16[4,8,896]{2,1,0:T(8,128)(2,1)S(1)} %pad_maximum_fusion.3), channel_id=1, source_target_pairs={{128,112},{132,116},{136,120},{140,124},{144,96},{148,100},{152,10... | collective-permute-start | bytes 172040 | tf_op jit(solution)/shard_map/ppermute | solution.py:270
  27.8 15.2 %collective-permute-start.4 = (bf16[4,8,896]{2,1,0:T(8,128)(2,1)S(1)}, bf16[4,8,896]{2,1,0:T(8,128)(2,1)S(1)}, u32[]{:S(2)}, u32[]{:S(2)}) collective-permute-start(bf16[4,8,896]{2,1,0:T(8,128)(2,1)S(1)} %pad_maximum_fusion.3), channel_id=1, source_target_pairs={{128,96},{132,100},{136,104},{140,108},{144,112},{148,116},{152,12... | collective-permute-start | bytes 172040 | tf_op jit(solution)/shard_map/ppermute | solution.py:270
  29.2 8.8 %collective-permute-start.3 = (bf16[4,8,1152]{2,1,0:T(8,128)(2,1)S(1)}, bf16[4,8,1152]{2,1,0:T(8,128)(2,1)S(1)}, u32[]{:S(2)}, u32[]{:S(2)}) collective-permute-start(bf16[4,8,1152]{2,1,0:T(8,128)(2,1)S(1)} %slice.21), channel_id=1, source_target_pairs={{0,16},{4,20},{8,24},{12,28},{16,0},{20,4},{24,8},{28,12},{1,17},{... | collective-permute-start | bytes 221192 | tf_op jit(solution)/shard_map/ppermute | solution.py:262
  39.4 43.5 %all-to-all-start.1 = ((bf16[8,8,104,128]{3,2,1,0:T(8,128)(2,1)}), bf16[8,8,104,128]{3,2,1,0:T(8,128)(2,1)S(1)}, u32[]{:S(2)}, u32[]{:S(2)}) async-start(bf16[8,8,104,128]{3,2,1,0:T(8,128)(2,1)} %bitcast.11), calls=%async_computation.1 | async-start | bytes 3407872 | tf_op jit(solution)/shard_map/all_to_all | solution.py:302
  43.1 5.2 %collective-permute-start.6 = (bf16[8,8,1152]{2,1,0:T(8,128)(2,1)S(1)}, bf16[8,8,1152]{2,1,0:T(8,128)(2,1)S(1)}, u32[]{:S(2)}, u32[]{:S(2)}) collective-permute-start(bf16[8,8,1152]{2,1,0:T(8,128)(2,1)S(1)} %slice_select_fusion), channel_id=1, source_target_pairs={{0,2},{2,0},{1,3},{3,1},{4,6},{6,4},{5,7},{7,5},{8,10},{10,8},{9,1... | collective-permute-start | bytes 442376 | tf_op jit(solution)/shard_map/ppermute | solution.py:262
  48.5 6.9 %collective-permute-start.9 = (bf16[1,64,1152]{2,1,0:T(8,128)(2,1)S(1)}, bf16[1,64,1152]{2,1,0:T(8,128)(2,1)S(1)}, u32[]{:S(2)}, u32[]{:S(2)}) collective-permute-start(bf16[1,64,1152]{2,1,0:T(8,128)(2,1)S(1)} %bitcast.12), channel_id=1, source_target_pairs={{0,96},{32,64},{64,32},{96,0},{1,97},{33,65},{65,33},{97,1},{2,98}... | collective-permute-start | bytes 442376 | tf_op jit(solution)/shard_map/ppermute | solution.py:262
  50.3 6.6 %collective-permute-start.8 = (bf16[1,64,1152]{2,1,0:T(8,128)(2,1)S(1)}, bf16[1,64,1152]{2,1,0:T(8,128)(2,1)S(1)}, u32[]{:S(2)}, u32[]{:S(2)}) collective-permute-start(bf16[1,64,1152]{2,1,0:T(8,128)(2,1)S(1)} %bitcast.13), channel_id=1, source_target_pairs={{0,64},{32,96},{64,0},{96,32},{1,65},{33,97},{65,1},{97,33},{2,66}... | collective-permute-start | bytes 442376 | tf_op jit(solution)/shard_map/ppermute | solution.py:262
  50.9 6.5 %collective-permute-start.7 = (bf16[1,64,1152]{2,1,0:T(8,128)(2,1)S(1)}, bf16[1,64,1152]{2,1,0:T(8,128)(2,1)S(1)}, u32[]{:S(2)}, u32[]{:S(2)}) collective-permute-start(bf16[1,64,1152]{2,1,0:T(8,128)(2,1)S(1)} %bitcast.14), channel_id=1, source_target_pairs={{0,32},{32,0},{64,96},{96,64},{1,33},{33,1},{65,97},{97,65},{2,34}... | collective-permute-start | bytes 442376 | tf_op jit(solution)/shard_map/ppermute | solution.py:262
  52.7 8.3 %collective-permute-start.10 = (bf16[1,64,1152]{2,1,0:T(8,128)(2,1)S(1)}, bf16[1,64,1152]{2,1,0:T(8,128)(2,1)S(1)}, u32[]{:S(2)}, u32[]{:S(2)}) collective-permute-start(bf16[1,64,1152]{2,1,0:T(8,128)(2,1)S(1)} %bitcast.17), channel_id=1, source_target_pairs={{0,128},{128,0},{1,129},{129,1},{2,130},{130,2},{3,131},{131,3},{4... | collective-permute-start | bytes 442376 | tf_op jit(solution)/shard_map/ppermute | solution.py:262
  57.4 16.1 %collective-permute-start.12 = (bf16[4,64,1152]{2,1,0:T(8,128)(2,1)S(1)}, bf16[4,64,1152]{2,1,0:T(8,128)(2,1)S(1)}, u32[]{:S(2)}, u32[]{:S(2)}) collective-permute-start(bf16[4,64,1152]{2,1,0:T(8,128)(2,1)S(1)} %pad_maximum_fusion.refs_0_), channel_id=1, source_target_pairs={{0,128},{128,0},{1,129},{129,1},{2,130},{130,2},{3,131},{131,3},{4... | collective-permute-start | bytes 1769480 | tf_op jit(solution)/shard_map/ppermute | solution.py:262
  61.0 9.4 %collective-permute-start.14 = (bf16[2,64,1152]{2,1,0:T(8,128)(2,1)S(1)}, bf16[2,64,1152]{2,1,0:T(8,128)(2,1)S(1)}, u32[]{:S(2)}, u32[]{:S(2)}) collective-permute-start(bf16[2,64,1152]{2,1,0:T(8,128)(2,1)S(1)} %pad_maximum_fusion.1.refs_2_), channel_id=1, source_target_pairs={{0,64},{32,96},{64,0},{96,32},{1,65},{33,97},{65,1},{97,33},{2,66}... | collective-permute-start | bytes 884744 | tf_op jit(solution)/shard_map/ppermute | solution.py:262
  61.8 11.7 %collective-permute-start.11 = (bf16[2,64,1152]{2,1,0:T(8,128)(2,1)S(1)}, bf16[2,64,1152]{2,1,0:T(8,128)(2,1)}, u32[]{:S(2)}, u32[]{:S(2)}) collective-permute-start(bf16[2,64,1152]{2,1,0:T(8,128)(2,1)S(1)} %pad_maximum_fusion.1.refs_2_), channel_id=1, source_target_pairs={{0,96},{32,64},{64,32},{96,0},{1,97},{33,65},{65,33},{97,1},{2,98}... | collective-permute-start | bytes 884744 | tf_op jit(solution)/shard_map/ppermute | solution.py:262
  64.0 10.0 %collective-permute-start.13 = (bf16[2,64,1152]{2,1,0:T(8,128)(2,1)S(1)}, bf16[2,64,1152]{2,1,0:T(8,128)(2,1)}, u32[]{:S(2)}, u32[]{:S(2)}) collective-permute-start(bf16[2,64,1152]{2,1,0:T(8,128)(2,1)S(1)} %pad_maximum_fusion.1.refs_2_), channel_id=1, source_target_pairs={{0,32},{32,0},{64,96},{96,64},{1,33},{33,1},{65,97},{97,65},{2,34}... | collective-permute-start | bytes 884744 | tf_op jit(solution)/shard_map/ppermute | solution.py:262
  70.4 4.2 %collective-permute-start.19 = (bf16[2,64,1152]{2,1,0:T(8,128)(2,1)S(1)}, bf16[2,64,1152]{2,1,0:T(8,128)(2,1)S(1)}, u32[]{:S(2)}, u32[]{:S(2)}) collective-permute-start(bf16[2,64,1152]{2,1,0:T(8,128)(2,1)S(1)} %collective-permute-done.14.refs_4_), channel_id=1, source_target_pairs={{0,1},{1,0},{2,3},{3,2},{4,5},{5,4},{6,7},{7,6},{8,9},{9,8},{10,11... | collective-permute-start | bytes 884744 | tf_op jit(solution)/shard_map/ppermute | solution.py:262
  73.5 4.5 %collective-permute-start.15 = (bf16[4,64,1152]{2,1,0:T(8,128)(2,1)S(1)}, bf16[4,64,1152]{2,1,0:T(8,128)(2,1)}, u32[]{:S(2)}, u32[]{:S(2)}) collective-permute-start(bf16[4,64,1152]{2,1,0:T(8,128)(2,1)S(1)} %pad_maximum_fusion.refs_0_), channel_id=1, source_target_pairs={{0,1},{1,0},{2,3},{3,2},{4,5},{5,4},{6,7},{7,6},{8,9},{9,8},{10,11... | collective-permute-start | bytes 1769480 | tf_op jit(solution)/shard_map/ppermute | solution.py:262
  73.5 4.5 %collective-permute-start.16 = (bf16[4,64,1152]{2,1,0:T(8,128)(2,1)S(1)}, bf16[4,64,1152]{2,1,0:T(8,128)(2,1)}, u32[]{:S(2)}, u32[]{:S(2)}) collective-permute-start(bf16[4,64,1152]{2,1,0:T(8,128)(2,1)S(1)} %collective-permute-done.12.refs_1_), channel_id=1, source_target_pairs={{0,1},{1,0},{2,3},{3,2},{4,5},{5,4},{6,7},{7,6},{8,9},{9,8},{10,11... | collective-permute-start | bytes 1769480 | tf_op jit(solution)/shard_map/ppermute | solution.py:262
  74.1 3.7 %collective-permute-start.17 = (bf16[2,64,1152]{2,1,0:T(8,128)(2,1)S(1)}, bf16[2,64,1152]{2,1,0:T(8,128)(2,1)}, u32[]{:S(2)}, u32[]{:S(2)}) collective-permute-start(bf16[2,64,1152]{2,1,0:T(8,128)(2,1)S(1)} %pad_maximum_fusion.1.refs_2_), channel_id=1, source_target_pairs={{0,1},{1,0},{2,3},{3,2},{4,5},{5,4},{6,7},{7,6},{8,9},{9,8},{10,11... | collective-permute-start | bytes 884744 | tf_op jit(solution)/shard_map/ppermute | solution.py:262
  74.1 3.1 %collective-permute-start.18 = (bf16[2,64,1152]{2,1,0:T(8,128)(2,1)}, bf16[2,64,1152]{2,1,0:T(8,128)(2,1)}, u32[]{:S(2)}, u32[]{:S(2)}) collective-permute-start(bf16[2,64,1152]{2,1,0:T(8,128)(2,1)} %collective-permute-done.13.refs_3_), channel_id=1, source_target_pairs={{0,1},{1,0},{2,3},{3,2},{4,5},{5,4},{6,7},{7,6},{8,9},{9,8},{10,11... | collective-permute-start | bytes 884744 | tf_op jit(solution)/shard_map/ppermute | solution.py:262
  74.6 0.7 copy-start
  75.3 2.7 %collective-permute-start.20 = (bf16[2,64,1152]{2,1,0:T(8,128)(2,1)}, bf16[2,64,1152]{2,1,0:T(8,128)(2,1)}, u32[]{:S(2)}, u32[]{:S(2)}) collective-permute-start(bf16[2,64,1152]{2,1,0:T(8,128)(2,1)} %collective-permute-done.11.refs_5_), channel_id=1, source_target_pairs={{0,1},{1,0},{2,3},{3,2},{4,5},{5,4},{6,7},{7,6},{8,9},{9,8},{10,11... | collective-permute-start | bytes 884744 | tf_op jit(solution)/shard_map/ppermute | solution.py:262
  75.3 7.7 %copy-start.2 = (s32[16]{0:T(128)S(1)}, s32[16]{0:T(128)}, u32[]{:S(2)}) copy-start(s32[16]{0:T(128)} %locked_ref.1) | copy-start | bytes 196
  78.0 1.0 copy-start.1

commit v4 on v3

--- a/solution.py
+++ b/solution.py
@@ -266,9 +266,10 @@
     rows = rotation[None]
     rows = jnp.concatenate([rows] + [exchange(rows, Z, 8, step) for step in (1, 2, 3)])
     late = [i for i in range(PEERS) if i >= 32]
-    spare = rows[:, :, KEEP:]
-    guests = [lax.ppermute(spare, EIG, [(i, (7 - i // 8) * 8 + (i % 8 ^ far)) for i in late]) for far in (0, 4)]
-    return rows[:, :, :KEEP], exchange(rows[:, :, :KEEP], Z, 8, 4), *guests
+    far = exchange(rows[:, :, :KEEP], Z, 8, 4)
+    spare, far = lax.optimization_barrier((rows[:, :, KEEP:], far))
+    guests = [lax.ppermute(spare, EIG, [(i, (7 - i // 8) * 8 + (i % 8 ^ half)) for i in late]) for half in (0, 4)]
+    return rows[:, :, :KEEP], far, *guests
 
 
 def gather_panels(near, far, *guests):
@@ -288,7 +289,7 @@
     a = jnp.concatenate([a] + [exchange(a, "x", 4, dx) for dx in (1, 2, 3)])
     far_a = exchange(a, "yh", 2, 1)
     far_b = [exchange(b, "x", 4, dx) for dx in (1, 2, 3)]
-    a, b, far_b[2] = lax.optimization_barrier((a, b, far_b[2]))
+    a, b, far_a = lax.optimization_barrier((a, b, far_a))
     own = [a, far_a, b] + far_b
     return own + [exchange(panel, "c", 2, 1) for panel in own]
 

time: 145 us -> 143 us (0.986)
  waiting for transfers between devices: 29.7 us -> 26.7 us
  starting transfers between devices: 43 us -> 44.9 us
    ppermute x19, waiting for transfers between devices: 29.7 us -> 26.7 us  [exchange(): return lax.ppermute(value, axis, [(i, i ^ mask) for i in range(size)])]
    ppermute x19, starting transfers between devices: 22.4 us -> 23.9 us  [exchange(): return lax.ppermute(value, axis, [(i, i ^ mask) for i in range(size)])]
where the time goes in v4:
time: 143 us
  blocking collectives  54.5 us (38%)
  starting transfers between devices  44.9 us (31%)
  waiting for transfers between devices  26.7 us (19%)
  Pallas kernels  13.1 us (9%)
  local copies, waits for them, and re-layouts  3.18 us (2%)
    all_to_all x1, blocking collectives, body(): lax.all_to_all(rotate(locked, received, matrix), ('x', 'zl', 'yh', 'zh'),...  54.5 us
    ppermute x19, waiting for transfers between devices, exchange(): return lax.ppermute(value, axis, [(i, i ^ mask) for i in range(size)])  26.7 us
    ppermute x19, starting transfers between devices, exchange(): return lax.ppermute(value, axis, [(i, i ^ mask) for i in range(size)])  23.9 us
    ppermute x2, starting transfers between devices, gather_near(): lax.ppermute(spare, EIG, [(i, (7 - i // 8) * 8 + (i % 8 ^ half)) for i in...  10.2 us
    all_to_all x1, starting transfers between devices, body(): lax.all_to_all(pack(vectors), ('yh', 'x'), split_axis=0, concat_axis=0, t...  7.28 us
    pallas_call x1, Pallas kernels, rotate(): pl.pallas_call(rotate_kernel, in_specs=[pl.BlockSpec(memory_space=pltpu.S...  5.26 us
    pallas_call x1, Pallas kernels, place_panels(): pl.pallas_call(place_kernel, in_specs=[pl.BlockSpec(memory_space=pltpu.SM...  3.97 us
    all_to_all x1, starting transfers between devices, body(): lax.all_to_all(halfway.transpose(1, 0, 2, 3), ('zl', 'zh'), split_axis=0,...  3.59 us
  transfers between devices with their start and end apart: 23, of which 12 were waited for; matrix products, arithmetic and copies ran while one was open for 1% of the time, Pallas kernels for 3%

profile of v4, /device:TPU:16, one launch (start us, length us, event | category | flops | bytes accessed | tf_op | source)
XLA Modules:
  0.0 143.0 jit_solution(12139627705194254485)
XLA Ops:
  0.0 2.6 %shard_map.37 = bf16[8,8,104,128]{3,2,1,0:T(8,128)(2,1)} custom-call(bf16[32,25600]{1,0:T(8,128)(2,1)} %source_ref.1), custom_call_target="tpu_custom_call" | custom-call | tf_op jit(solution)/shard_map/pallas_call | solution.py:87
  2.6 0.0 copy-start.3
  2.6 7.3 %all-to-all-start = ((bf16[8,8,104,128]{3,2,1,0:T(8,128)(2,1)}), bf16[8,8,104,128]{3,2,1,0:T(8,128)(2,1)S(1)}, u32[]{:S(2)}, u32[]{:S(2)}) async-start(bf16[8,8,104,128]{3,2,1,0:T(8,128)(2,1)} %shard_map.37), calls=%async_computation | async-start | bytes 3407872 | tf_op jit(solution)/shard_map/all_to_all | solution.py:298
  9.9 0.0 copy-done.3
  9.9 4.6 %collective-permute-start.2 = (bf16[1,8,2048]{2,1,0:T(8,128)(2,1)S(1)}, bf16[1,8,2048]{2,1,0:T(8,128)(2,1)S(1)}, u32[]{:S(2)}, u32[]{:S(2)}) collective-permute-start(bf16[1,8,2048]{2,1,0:T(8,128)(2,1)S(1)} %bitcast.20), channel_id=1, source_target_pairs={{0,12},{4,8},{8,4},{12,0},{16,28},{20,24},{24,20},{28,16},{1,13},{... | collective-permute-start | bytes 98312 | tf_op jit(solution)/shard_map/ppermute | solution.py:262
  14.5 0.0 collective-permute-start.1
  14.5 0.7 collective-permute-start
  15.1 1.3 collective-permute-done.2
  16.4 2.9 %collective-permute-done.1 = bf16[1,8,2048]{2,1,0:T(8,128)(2,1)S(1)} collective-permute-done((bf16[1,8,2048]{2,1,0:T(8,128)(2,1)S(1)}, bf16[1,8,2048]{2,1,0:T(8,128)(2,1)S(1)}, u32[]{:S(2)}, u32[]{:S(2)}) %collective-permute-start.1) | collective-permute-done | bytes 32800 | tf_op jit(solution)/shard_map/ppermute | solution.py:262
  19.3 0.0 collective-permute-done
  19.3 4.6 %collective-permute-start.3 = (bf16[4,8,1152]{2,1,0:T(8,128)(2,1)S(1)}, bf16[4,8,1152]{2,1,0:T(8,128)(2,1)S(1)}, u32[]{:S(2)}, u32[]{:S(2)}) collective-permute-start(bf16[4,8,1152]{2,1,0:T(8,128)(2,1)S(1)} %pad_maximum_fusion.2), channel_id=1, source_target_pairs={{0,16},{4,20},{8,24},{12,28},{16,0},{20,4},{24,8},{28,12},{1,17},{... | collective-permute-start | bytes 221192 | tf_op jit(solution)/shard_map/ppermute | solution.py:262
  23.9 3.8 %collective-permute-done.3 = bf16[4,8,1152]{2,1,0:T(8,128)(2,1)S(1)} collective-permute-done((bf16[4,8,1152]{2,1,0:T(8,128)(2,1)S(1)}, bf16[4,8,1152]{2,1,0:T(8,128)(2,1)S(1)}, u32[]{:S(2)}, u32[]{:S(2)}) %collective-permute-start.3) | collective-permute-done | bytes 73760 | tf_op jit(solution)/shard_map/ppermute | solution.py:262
  27.8 8.9 %collective-permute-start.5 = (bf16[4,8,896]{2,1,0:T(8,128)(2,1)S(1)}, bf16[4,8,896]{2,1,0:T(8,128)(2,1)S(1)}, u32[]{:S(2)}, u32[]{:S(2)}) collective-permute-start(bf16[4,8,896]{2,1,0:T(8,128)(2,1)S(1)} %pad_maximum_fusion.5), channel_id=1, source_target_pairs={{128,112},{132,116},{136,120},{140,124},{144,96},{148,100},{152,10... | collective-permute-start | bytes 172040 | tf_op jit(solution)/shard_map/ppermute | solution.py:271
  36.6 1.3 collective-permute-start.4
  38.0 0.0 all-to-all-done
  38.0 1.4 copy.11
  39.4 3.6 %all-to-all-start.1 = ((bf16[8,8,104,128]{3,2,1,0:T(8,128)(2,1)}), bf16[8,8,104,128]{3,2,1,0:T(8,128)(2,1)S(1)}, u32[]{:S(2)}, u32[]{:S(2)}) async-start(bf16[8,8,104,128]{3,2,1,0:T(8,128)(2,1)} %bitcast.11), calls=%async_computation.1 | async-start | bytes 3407872 | tf_op jit(solution)/shard_map/all_to_all | solution.py:303
  43.0 0.0 collective-permute-done.5
  43.0 0.0 collective-permute-done.4
  43.1 1.4 collective-permute-start.6
  44.5 3.9 %collective-permute-done.6 = bf16[8,8,1152]{2,1,0:T(8,128)(2,1)S(1)} collective-permute-done((bf16[8,8,1152]{2,1,0:T(8,128)(2,1)S(1)}, bf16[8,8,1152]{2,1,0:T(8,128)(2,1)S(1)}, u32[]{:S(2)}, u32[]{:S(2)}) %collective-permute-start.6) | collective-permute-done | bytes 147488 | tf_op jit(solution)/shard_map/ppermute | solution.py:262
  48.4 0.3 collective-permute-start.9
  48.7 2.1 %collective-permute-start.8 = (bf16[1,64,1152]{2,1,0:T(8,128)(2,1)S(1)}, bf16[1,64,1152]{2,1,0:T(8,128)(2,1)S(1)}, u32[]{:S(2)}, u32[]{:S(2)}) collective-permute-start(bf16[1,64,1152]{2,1,0:T(8,128)(2,1)S(1)} %bitcast.13), channel_id=1, source_target_pairs={{0,64},{32,96},{64,0},{96,32},{1,65},{33,97},{65,1},{97,33},{2,66}... | collective-permute-start | bytes 442376 | tf_op jit(solution)/shard_map/ppermute | solution.py:262
  50.8 1.8 %collective-permute-start.7 = (bf16[1,64,1152]{2,1,0:T(8,128)(2,1)S(1)}, bf16[1,64,1152]{2,1,0:T(8,128)(2,1)S(1)}, u32[]{:S(2)}, u32[]{:S(2)}) collective-permute-start(bf16[1,64,1152]{2,1,0:T(8,128)(2,1)S(1)} %bitcast.14), channel_id=1, source_target_pairs={{0,32},{32,0},{64,96},{96,64},{1,33},{33,1},{65,97},{97,65},{2,34}... | collective-permute-start | bytes 442376 | tf_op jit(solution)/shard_map/ppermute | solution.py:262
  52.6 1.5 %collective-permute-start.10 = (bf16[1,64,1152]{2,1,0:T(8,128)(2,1)S(1)}, bf16[1,64,1152]{2,1,0:T(8,128)(2,1)S(1)}, u32[]{:S(2)}, u32[]{:S(2)}) collective-permute-start(bf16[1,64,1152]{2,1,0:T(8,128)(2,1)S(1)} %bitcast.17), channel_id=1, source_target_pairs={{0,128},{128,0},{1,129},{129,1},{2,130},{130,2},{3,131},{131,3},{4... | collective-permute-start | bytes 442376 | tf_op jit(solution)/shard_map/ppermute | solution.py:262
  54.1 2.3 %collective-permute-done.9 = bf16[1,64,1152]{2,1,0:T(8,128)(2,1)S(1)} collective-permute-done((bf16[1,64,1152]{2,1,0:T(8,128)(2,1)S(1)}, bf16[1,64,1152]{2,1,0:T(8,128)(2,1)S(1)}, u32[]{:S(2)}, u32[]{:S(2)}) %collective-permute-start.9) | collective-permute-done | bytes 147488 | tf_op jit(solution)/shard_map/ppermute | solution.py:262
  56.4 0.0 collective-permute-done.8
  56.5 0.9 collective-permute-done.7
  57.3 0.1 pad_maximum_fusion.refs_0_
  57.4 1.5 %collective-permute-start.11 = (bf16[4,64,1152]{2,1,0:T(8,128)(2,1)S(1)}, bf16[4,64,1152]{2,1,0:T(8,128)(2,1)S(1)}, u32[]{:S(2)}, u32[]{:S(2)}) collective-permute-start(bf16[4,64,1152]{2,1,0:T(8,128)(2,1)S(1)} %pad_maximum_fusion.refs_0_), channel_id=1, source_target_pairs={{0,128},{128,0},{1,129},{129,1},{2,130},{130,2},{3,131},{131,3},{4... | collective-permute-start | bytes 1769480 | tf_op jit(solution)/shard_map/ppermute | solution.py:262
  58.9 2.1 %collective-permute-done.10 = bf16[1,64,1152]{2,1,0:T(8,128)(2,1)S(1)} collective-permute-done((bf16[1,64,1152]{2,1,0:T(8,128)(2,1)S(1)}, bf16[1,64,1152]{2,1,0:T(8,128)(2,1)S(1)}, u32[]{:S(2)}, u32[]{:S(2)}) %collective-permute-start.10) | collective-permute-done | bytes 147488 | tf_op jit(solution)/shard_map/ppermute | solution.py:262
  61.0 0.3 collective-permute-start.14
  61.3 2.1 %collective-permute-start.13 = (bf16[2,64,1152]{2,1,0:T(8,128)(2,1)S(1)}, bf16[2,64,1152]{2,1,0:T(8,128)(2,1)}, u32[]{:S(2)}, u32[]{:S(2)}) collective-permute-start(bf16[2,64,1152]{2,1,0:T(8,128)(2,1)S(1)} %pad_maximum_fusion.1.refs_2_), channel_id=1, source_target_pairs={{0,64},{32,96},{64,0},{96,32},{1,65},{33,97},{65,1},{97,33},{2,66}... | collective-permute-start | bytes 884744 | tf_op jit(solution)/shard_map/ppermute | solution.py:262
  63.4 1.8 %collective-permute-start.12 = (bf16[2,64,1152]{2,1,0:T(8,128)(2,1)S(1)}, bf16[2,64,1152]{2,1,0:T(8,128)(2,1)}, u32[]{:S(2)}, u32[]{:S(2)}) collective-permute-start(bf16[2,64,1152]{2,1,0:T(8,128)(2,1)S(1)} %pad_maximum_fusion.1.refs_2_), channel_id=1, source_target_pairs={{0,32},{32,0},{64,96},{96,64},{1,33},{33,1},{65,97},{97,65},{2,34}... | collective-permute-start | bytes 884744 | tf_op jit(solution)/shard_map/ppermute | solution.py:262
  65.2 7.0 %collective-permute-done.14.refs_5_ = bf16[2,64,1152]{2,1,0:T(8,128)(2,1)S(1)} collective-permute-done((bf16[2,64,1152]{2,1,0:T(8,128)(2,1)S(1)}, bf16[2,64,1152]{2,1,0:T(8,128)(2,1)S(1)}, u32[]{:S(2)}, u32[]{:S(2)}) %collective-permute-start.14) | collective-permute-done | bytes 294944 | tf_op jit(solution)/shard_map/ppermute | solution.py:262
  72.2 0.0 collective-permute-start.20
  72.2 0.0 collective-permute-done.11.refs_1_
  72.2 0.5 collective-permute-start.15
  72.7 0.0 collective-permute-start.16
  72.7 0.0 collective-permute-done.13.refs_4_
  72.7 0.5 collective-permute-start.19
  73.2 0.0 collective-permute-done.12.refs_3_
  73.2 0.1 collective-permute-start.18
  73.3 0.8 collective-permute-done.20.refs_11_
  74.1 0.0 copy-start
  74.1 0.7 copy-done
  74.8 0.1 collective-permute-start.17
  75.0 0.0 copy-start.2
  75.0 0.1 pad_add_fusion.place_ref
  75.1 0.5 collective-permute-done.19.refs_10_
  75.5 0.8 collective-permute-done.18.refs_9_
  76.4 0.5 collective-permute-done.17.refs_8_
  76.9 0.0 collective-permute-done.15.refs_6_
  76.9 0.0 collective-permute-done.16.refs_7_
  76.9 0.0 copy-start.1
  76.9 1.0 copy-done.1
  77.8 4.0 %shard_map.38.source_ref = bf16[64,32,1152]{2,1,0:T(8,128)(2,1)} custom-call(s32[4]{0:T(128)S(1)} %pad_add_fusion.place_ref, bf16[4,64,1152]{2,1,0:T(8,128)(2,1)S(1)} %pad_maximum_fusion.refs_0_, bf16[4,64,1152]{2,1,0:T(8,128)(2,1)S(1)} %collective-permute-done.11.refs_1_, bf16[2,64,1152]{2,1,0:T(8,128)(2,1)S(1)} %pad_maximum_fusion.1.refs_2_, ...), custom_call_target="tpu_custom_call" | custom-call | tf_op jit(solution)/shard_map/pallas_call | solution.py:178
  81.8 0.0 all-to-all-done.1.in_ref
  81.8 0.0 copy-done.2
  81.8 5.3 %shard_map.39 = bf16[64,104,128]{2,1,0:T(8,128)(2,1)S(1)} custom-call(s32[16]{0:T(128)S(1)} %copy-done.2, bf16[8,8,104,128]{3,2,1,0:T(8,128)(2,1)S(1)} %all-to-all-done.1.in_ref, bf16[64,32,1152]{2,1,0:T(8,128)(2,1)} %shard_map.38.source_ref), custom_call_target="tpu_custom_call" | custom-call | tf_op jit(solution)/shard_map/pallas_call | solution.py:247
  87.1 54.5 %all_to_all.15.in_ref = bf16[64,104,128]{2,1,0:T(8,128)(2,1)S(1)} all-to-all(bf16[64,104,128]{2,1,0:T(8,128)(2,1)S(1)} %shard_map.39), channel_id=1, replica_groups=mesh['yh'=2,'x'=4,'zh'=2,'zl'=4,'yl'=2,'c'=2] {'x','zl','yh','zh'}, dimensions={0} | all-to-all | bytes 3407872 | tf_op jit(solution)/shard_map/all_to_all | solution.py:304
  141.6 1.3 shard_map.40
  (11 shorter events, 0.2 us)
Async XLA Ops:
  2.6 7.3 %copy-start.3 = (bf16[8,2048]{1,0:T(8,128)(2,1)S(1)}, bf16[8,2048]{1,0:T(8,128)(2,1)}, u32[]{:S(2)}) copy-start(bf16[8,2048]{1,0:T(8,128)(2,1)} %param.4) | copy-start | bytes 98308
  2.6 35.4 %all-to-all-start = ((bf16[8,8,104,128]{3,2,1,0:T(8,128)(2,1)}), bf16[8,8,104,128]{3,2,1,0:T(8,128)(2,1)S(1)}, u32[]{:S(2)}, u32[]{:S(2)}) async-start(bf16[8,8,104,128]{3,2,1,0:T(8,128)(2,1)} %shard_map.37), calls=%async_computation | async-start | bytes 3407872 | tf_op jit(solution)/shard_map/all_to_all | solution.py:298
  9.9 6.5 %collective-permute-start.2 = (bf16[1,8,2048]{2,1,0:T(8,128)(2,1)S(1)}, bf16[1,8,2048]{2,1,0:T(8,128)(2,1)S(1)}, u32[]{:S(2)}, u32[]{:S(2)}) collective-permute-start(bf16[1,8,2048]{2,1,0:T(8,128)(2,1)S(1)} %bitcast.20), channel_id=1, source_target_pairs={{0,12},{4,8},{8,4},{12,0},{16,28},{20,24},{24,20},{28,16},{1,13},{... | collective-permute-start | bytes 98312 | tf_op jit(solution)/shard_map/ppermute | solution.py:262
  14.5 4.8 %collective-permute-start.1 = (bf16[1,8,2048]{2,1,0:T(8,128)(2,1)S(1)}, bf16[1,8,2048]{2,1,0:T(8,128)(2,1)S(1)}, u32[]{:S(2)}, u32[]{:S(2)}) collective-permute-start(bf16[1,8,2048]{2,1,0:T(8,128)(2,1)S(1)} %bitcast.21), channel_id=1, source_target_pairs={{0,8},{4,12},{8,0},{12,4},{16,24},{20,28},{24,16},{28,20},{1,9},{5... | collective-permute-start | bytes 98312 | tf_op jit(solution)/shard_map/ppermute | solution.py:262
  14.5 4.8 %collective-permute-start = (bf16[1,8,2048]{2,1,0:T(8,128)(2,1)S(1)}, bf16[1,8,2048]{2,1,0:T(8,128)(2,1)S(1)}, u32[]{:S(2)}, u32[]{:S(2)}) collective-permute-start(bf16[1,8,2048]{2,1,0:T(8,128)(2,1)S(1)} %bitcast.22), channel_id=1, source_target_pairs={{0,4},{4,0},{8,12},{12,8},{16,20},{20,16},{24,28},{28,24},{1,5},{5... | collective-permute-start | bytes 98312 | tf_op jit(solution)/shard_map/ppermute | solution.py:262
  19.3 8.5 %collective-permute-start.3 = (bf16[4,8,1152]{2,1,0:T(8,128)(2,1)S(1)}, bf16[4,8,1152]{2,1,0:T(8,128)(2,1)S(1)}, u32[]{:S(2)}, u32[]{:S(2)}) collective-permute-start(bf16[4,8,1152]{2,1,0:T(8,128)(2,1)S(1)} %pad_maximum_fusion.2), channel_id=1, source_target_pairs={{0,16},{4,20},{8,24},{12,28},{16,0},{20,4},{24,8},{28,12},{1,17},{... | collective-permute-start | bytes 221192 | tf_op jit(solution)/shard_map/ppermute | solution.py:262
  27.8 15.2 %collective-permute-start.5 = (bf16[4,8,896]{2,1,0:T(8,128)(2,1)S(1)}, bf16[4,8,896]{2,1,0:T(8,128)(2,1)S(1)}, u32[]{:S(2)}, u32[]{:S(2)}) collective-permute-start(bf16[4,8,896]{2,1,0:T(8,128)(2,1)S(1)} %pad_maximum_fusion.5), channel_id=1, source_target_pairs={{128,112},{132,116},{136,120},{140,124},{144,96},{148,100},{152,10... | collective-permute-start | bytes 172040 | tf_op jit(solution)/shard_map/ppermute | solution.py:271
  36.6 6.3 %collective-permute-start.4 = (bf16[4,8,896]{2,1,0:T(8,128)(2,1)S(1)}, bf16[4,8,896]{2,1,0:T(8,128)(2,1)S(1)}, u32[]{:S(2)}, u32[]{:S(2)}) collective-permute-start(bf16[4,8,896]{2,1,0:T(8,128)(2,1)S(1)} %pad_maximum_fusion.5), channel_id=1, source_target_pairs={{128,96},{132,100},{136,104},{140,108},{144,112},{148,116},{152,12... | collective-permute-start | bytes 172040 | tf_op jit(solution)/shard_map/ppermute | solution.py:271
  39.4 42.4 %all-to-all-start.1 = ((bf16[8,8,104,128]{3,2,1,0:T(8,128)(2,1)}), bf16[8,8,104,128]{3,2,1,0:T(8,128)(2,1)S(1)}, u32[]{:S(2)}, u32[]{:S(2)}) async-start(bf16[8,8,104,128]{3,2,1,0:T(8,128)(2,1)} %bitcast.11), calls=%async_computation.1 | async-start | bytes 3407872 | tf_op jit(solution)/shard_map/all_to_all | solution.py:303
  43.1 5.2 %collective-permute-start.6 = (bf16[8,8,1152]{2,1,0:T(8,128)(2,1)S(1)}, bf16[8,8,1152]{2,1,0:T(8,128)(2,1)S(1)}, u32[]{:S(2)}, u32[]{:S(2)}) collective-permute-start(bf16[8,8,1152]{2,1,0:T(8,128)(2,1)S(1)} %slice_select_fusion), channel_id=1, source_target_pairs={{0,2},{2,0},{1,3},{3,1},{4,6},{6,4},{5,7},{7,5},{8,10},{10,8},{9,1... | collective-permute-start | bytes 442376 | tf_op jit(solution)/shard_map/ppermute | solution.py:262
  48.4 8.0 %collective-permute-start.9 = (bf16[1,64,1152]{2,1,0:T(8,128)(2,1)S(1)}, bf16[1,64,1152]{2,1,0:T(8,128)(2,1)S(1)}, u32[]{:S(2)}, u32[]{:S(2)}) collective-permute-start(bf16[1,64,1152]{2,1,0:T(8,128)(2,1)S(1)} %bitcast.12), channel_id=1, source_target_pairs={{0,96},{32,64},{64,32},{96,0},{1,97},{33,65},{65,33},{97,1},{2,98}... | collective-permute-start | bytes 442376 | tf_op jit(solution)/shard_map/ppermute | solution.py:262
  48.7 7.7 %collective-permute-start.8 = (bf16[1,64,1152]{2,1,0:T(8,128)(2,1)S(1)}, bf16[1,64,1152]{2,1,0:T(8,128)(2,1)S(1)}, u32[]{:S(2)}, u32[]{:S(2)}) collective-permute-start(bf16[1,64,1152]{2,1,0:T(8,128)(2,1)S(1)} %bitcast.13), channel_id=1, source_target_pairs={{0,64},{32,96},{64,0},{96,32},{1,65},{33,97},{65,1},{97,33},{2,66}... | collective-permute-start | bytes 442376 | tf_op jit(solution)/shard_map/ppermute | solution.py:262
  50.8 6.5 %collective-permute-start.7 = (bf16[1,64,1152]{2,1,0:T(8,128)(2,1)S(1)}, bf16[1,64,1152]{2,1,0:T(8,128)(2,1)S(1)}, u32[]{:S(2)}, u32[]{:S(2)}) collective-permute-start(bf16[1,64,1152]{2,1,0:T(8,128)(2,1)S(1)} %bitcast.14), channel_id=1, source_target_pairs={{0,32},{32,0},{64,96},{96,64},{1,33},{33,1},{65,97},{97,65},{2,34}... | collective-permute-start | bytes 442376 | tf_op jit(solution)/shard_map/ppermute | solution.py:262
  52.6 8.4 %collective-permute-start.10 = (bf16[1,64,1152]{2,1,0:T(8,128)(2,1)S(1)}, bf16[1,64,1152]{2,1,0:T(8,128)(2,1)S(1)}, u32[]{:S(2)}, u32[]{:S(2)}) collective-permute-start(bf16[1,64,1152]{2,1,0:T(8,128)(2,1)S(1)} %bitcast.17), channel_id=1, source_target_pairs={{0,128},{128,0},{1,129},{129,1},{2,130},{130,2},{3,131},{131,3},{4... | collective-permute-start | bytes 442376 | tf_op jit(solution)/shard_map/ppermute | solution.py:262
  57.4 14.8 %collective-permute-start.11 = (bf16[4,64,1152]{2,1,0:T(8,128)(2,1)S(1)}, bf16[4,64,1152]{2,1,0:T(8,128)(2,1)S(1)}, u32[]{:S(2)}, u32[]{:S(2)}) collective-permute-start(bf16[4,64,1152]{2,1,0:T(8,128)(2,1)S(1)} %pad_maximum_fusion.refs_0_), channel_id=1, source_target_pairs={{0,128},{128,0},{1,129},{129,1},{2,130},{130,2},{3,131},{131,3},{4... | collective-permute-start | bytes 1769480 | tf_op jit(solution)/shard_map/ppermute | solution.py:262
  61.0 11.2 %collective-permute-start.14 = (bf16[2,64,1152]{2,1,0:T(8,128)(2,1)S(1)}, bf16[2,64,1152]{2,1,0:T(8,128)(2,1)S(1)}, u32[]{:S(2)}, u32[]{:S(2)}) collective-permute-start(bf16[2,64,1152]{2,1,0:T(8,128)(2,1)S(1)} %pad_maximum_fusion.1.refs_2_), channel_id=1, source_target_pairs={{0,96},{32,64},{64,32},{96,0},{1,97},{33,65},{65,33},{97,1},{2,98}... | collective-permute-start | bytes 884744 | tf_op jit(solution)/shard_map/ppermute | solution.py:262
  61.3 11.4 %collective-permute-start.13 = (bf16[2,64,1152]{2,1,0:T(8,128)(2,1)S(1)}, bf16[2,64,1152]{2,1,0:T(8,128)(2,1)}, u32[]{:S(2)}, u32[]{:S(2)}) collective-permute-start(bf16[2,64,1152]{2,1,0:T(8,128)(2,1)S(1)} %pad_maximum_fusion.1.refs_2_), channel_id=1, source_target_pairs={{0,64},{32,96},{64,0},{96,32},{1,65},{33,97},{65,1},{97,33},{2,66}... | collective-permute-start | bytes 884744 | tf_op jit(solution)/shard_map/ppermute | solution.py:262
  63.4 9.8 %collective-permute-start.12 = (bf16[2,64,1152]{2,1,0:T(8,128)(2,1)S(1)}, bf16[2,64,1152]{2,1,0:T(8,128)(2,1)}, u32[]{:S(2)}, u32[]{:S(2)}) collective-permute-start(bf16[2,64,1152]{2,1,0:T(8,128)(2,1)S(1)} %pad_maximum_fusion.1.refs_2_), channel_id=1, source_target_pairs={{0,32},{32,0},{64,96},{96,64},{1,33},{33,1},{65,97},{97,65},{2,34}... | collective-permute-start | bytes 884744 | tf_op jit(solution)/shard_map/ppermute | solution.py:262
  72.2 1.9 %collective-permute-start.20 = (bf16[2,64,1152]{2,1,0:T(8,128)(2,1)S(1)}, bf16[2,64,1152]{2,1,0:T(8,128)(2,1)S(1)}, u32[]{:S(2)}, u32[]{:S(2)}) collective-permute-start(bf16[2,64,1152]{2,1,0:T(8,128)(2,1)S(1)} %collective-permute-done.14.refs_5_), channel_id=1, source_target_pairs={{0,1},{1,0},{2,3},{3,2},{4,5},{5,4},{6,7},{7,6},{8,9},{9,8},{10,11... | collective-permute-start | bytes 884744 | tf_op jit(solution)/shard_map/ppermute | solution.py:262
  72.2 4.7 %collective-permute-start.15 = (bf16[4,64,1152]{2,1,0:T(8,128)(2,1)S(1)}, bf16[4,64,1152]{2,1,0:T(8,128)(2,1)}, u32[]{:S(2)}, u32[]{:S(2)}) collective-permute-start(bf16[4,64,1152]{2,1,0:T(8,128)(2,1)S(1)} %pad_maximum_fusion.refs_0_), channel_id=1, source_target_pairs={{0,1},{1,0},{2,3},{3,2},{4,5},{5,4},{6,7},{7,6},{8,9},{9,8},{10,11... | collective-permute-start | bytes 1769480 | tf_op jit(solution)/shard_map/ppermute | solution.py:262
  72.7 4.2 %collective-permute-start.16 = (bf16[4,64,1152]{2,1,0:T(8,128)(2,1)S(1)}, bf16[4,64,1152]{2,1,0:T(8,128)(2,1)}, u32[]{:S(2)}, u32[]{:S(2)}) collective-permute-start(bf16[4,64,1152]{2,1,0:T(8,128)(2,1)S(1)} %collective-permute-done.11.refs_1_), channel_id=1, source_target_pairs={{0,1},{1,0},{2,3},{3,2},{4,5},{5,4},{6,7},{7,6},{8,9},{9,8},{10,11... | collective-permute-start | bytes 1769480 | tf_op jit(solution)/shard_map/ppermute | solution.py:262
  72.7 2.8 %collective-permute-start.19 = (bf16[2,64,1152]{2,1,0:T(8,128)(2,1)}, bf16[2,64,1152]{2,1,0:T(8,128)(2,1)}, u32[]{:S(2)}, u32[]{:S(2)}) collective-permute-start(bf16[2,64,1152]{2,1,0:T(8,128)(2,1)} %collective-permute-done.13.refs_4_), channel_id=1, source_target_pairs={{0,1},{1,0},{2,3},{3,2},{4,5},{5,4},{6,7},{7,6},{8,9},{9,8},{10,11... | collective-permute-start | bytes 884744 | tf_op jit(solution)/shard_map/ppermute | solution.py:262
  73.2 3.1 %collective-permute-start.18 = (bf16[2,64,1152]{2,1,0:T(8,128)(2,1)}, bf16[2,64,1152]{2,1,0:T(8,128)(2,1)}, u32[]{:S(2)}, u32[]{:S(2)}) collective-permute-start(bf16[2,64,1152]{2,1,0:T(8,128)(2,1)} %collective-permute-done.12.refs_3_), channel_id=1, source_target_pairs={{0,1},{1,0},{2,3},{3,2},{4,5},{5,4},{6,7},{7,6},{8,9},{9,8},{10,11... | collective-permute-start | bytes 884744 | tf_op jit(solution)/shard_map/ppermute | solution.py:262
  74.1 0.7 copy-start
  74.8 2.0 %collective-permute-start.17 = (bf16[2,64,1152]{2,1,0:T(8,128)(2,1)S(1)}, bf16[2,64,1152]{2,1,0:T(8,128)(2,1)}, u32[]{:S(2)}, u32[]{:S(2)}) collective-permute-start(bf16[2,64,1152]{2,1,0:T(8,128)(2,1)S(1)} %pad_maximum_fusion.1.refs_2_), channel_id=1, source_target_pairs={{0,1},{1,0},{2,3},{3,2},{4,5},{5,4},{6,7},{7,6},{8,9},{9,8},{10,11... | collective-permute-start | bytes 884744 | tf_op jit(solution)/shard_map/ppermute | solution.py:262
  75.0 6.9 %copy-start.2 = (s32[16]{0:T(128)S(1)}, s32[16]{0:T(128)}, u32[]{:S(2)}) copy-start(s32[16]{0:T(128)} %locked_ref.1) | copy-start | bytes 196
  76.9 1.0 copy-start.1

commit v5 on v4

--- a/solution.py
+++ b/solution.py
@@ -265,24 +265,29 @@
 def gather_near(rotation):
     rows = rotation[None]
     rows = jnp.concatenate([rows] + [exchange(rows, Z, 8, step) for step in (1, 2, 3)])
-    late = [i for i in range(PEERS) if i >= 32]
-    far = exchange(rows[:, :, :KEEP], Z, 8, 4)
-    spare, far = lax.optimization_barrier((rows[:, :, KEEP:], far))
-    guests = [lax.ppermute(spare, EIG, [(i, (7 - i // 8) * 8 + (i % 8 ^ half)) for i in late]) for half in (0, 4)]
-    return rows[:, :, :KEEP], far, *guests
-
-
-def gather_panels(near, far, *guests):
+    parts = (rows[:, :, :KEEP], rows[:, :, KEEP:])
+    return [jnp.concatenate([part, exchange(part, Z, 8, 4)]) for part in parts]
+
+
+def gather_panels(keep, spare):
     eig, yl = lax.axis_index(EIG), lax.axis_index("yl")
     group = eig // 8
-    rows = jnp.concatenate([near, far])
+    late = [i for i in range(PEERS) if i >= 32]
+    mirror = {i: (7 - i // 8) * 8 + i % 8 for i in late}
+    keep, spare = lax.optimization_barrier((keep, spare))
+    pairs = [[(2 * i + s, 2 * mirror[i] + (s ^ flip)) for i in late for s in range(2)] for flip in (0, 1)]
+    guests = [lax.ppermute(spare, EIG + ("yl",), pair) for pair in pairs]
+    other = exchange(keep, "yl", 2, 1)
     place = 256 * (group + 1)
-    guest = jnp.concatenate([jnp.concatenate(guests), jnp.zeros((8, 8, KEEP), BF16)], axis=2)
-    guest = lax.dynamic_update_slice(jnp.zeros((8, 8, 4096), BF16), guest, (0, 0, place))[:, :, :KEEP]
     cols = lax.broadcasted_iota(jnp.int32, (1, 1, KEEP), 2)
-    rows = jnp.where((group >= 4) | (cols < place), rows, guest)
-    other = exchange(rows, "yl", 2, 1)
-    rows = jnp.where(yl == 0, jnp.stack([rows, other], axis=1), jnp.stack([other, rows], axis=1))
+
+    def fold(own, guest):
+        guest = jnp.concatenate([guest, jnp.zeros((8, 8, KEEP), BF16)], axis=2)
+        guest = lax.dynamic_update_slice(jnp.zeros((8, 8, 4096), BF16), guest, (0, 0, place))[:, :, :KEEP]
+        return jnp.where((group >= 4) | (cols < place), own, guest)
+
+    keep, other = fold(keep, guests[0]), fold(other, guests[1])
+    rows = jnp.where(yl == 0, jnp.stack([keep, other], axis=1), jnp.stack([other, keep], axis=1))
 
     a, b = rows[:4].reshape(1, 64, KEEP), rows[4:].reshape(1, 64, KEEP)
     b = jnp.concatenate([b, exchange(b, "yh", 2, 1)])
@@ -296,10 +301,10 @@
 
 def body(vectors, rotation, locked):
     halfway = lax.all_to_all(pack(vectors), ("yh", "x"), split_axis=0, concat_axis=0, tiled=True)
-    near = gather_near(rotation)
-    halfway, _ = lax.optimization_barrier((halfway, near[1]))
+    keep, spare = gather_near(rotation)
+    halfway, *_ = lax.optimization_barrier((halfway, keep, spare))
     place = jnp.stack([lax.axis_index(name) for name in ("c", "yh", "x", Z)]).astype(jnp.int32)
-    matrix = place_panels(place, gather_panels(*near))
+    matrix = place_panels(place, gather_panels(keep, spare))
     received = lax.all_to_all(halfway.transpose(1, 0, 2, 3), ("zl", "zh"), split_axis=0, concat_axis=0, tiled=True)
     back = lax.all_to_all(rotate(locked, received, matrix), ("x", "zl", "yh", "zh"), split_axis=0, concat_axis=0, tiled=True)
     return unpack(back)

time: 143 us -> 144 us (level)
  starting transfers between devices: 44.9 us -> 47.1 us
  waiting for transfers between devices: 26.7 us -> 24.7 us
    ppermute x19 -> x20, starting transfers between devices: 23.9 us -> 30.4 us  [exchange(): return lax.ppermute(value, axis, [(i, i ^ mask) for i in range(size)])]
    ppermute x2, starting transfers between devices: 10.2 us -> 5.88 us  [gather_panels(): guests = [lax.ppermute(spare, EIG + ('yl',), pair) for pair in pairs]]
    ppermute x19 -> x20, waiting for transfers between devices: 26.7 us -> 22.9 us  [exchange(): return lax.ppermute(value, axis, [(i, i ^ mask) for i in range(size)])]
    all_to_all x1, waiting for transfers between devices: 0.01 us -> 1.77 us  [body(): lax.all_to_all(halfway.transpose(1, 0, 2, 3), ('zl', 'zh'), split_axis=0,...]
  transfers between devices with their start and end apart: 23 -> 24, of which waited for: 12 -> 12; matrix products, arithmetic and copies ran while one was open for 1% -> 1% of each run, Pallas kernels for 3% -> 3%
where the time goes in v5:
time: 144 us; the launch traced here: 143 us
  blocking collectives  54.1 us (38%)
  starting transfers between devices  47.1 us (33%)
  waiting for transfers between devices  24.7 us (17%)
  Pallas kernels  13.1 us (9%)
  local copies, waits for them, and re-layouts  3.27 us (2%)
    all_to_all x1, blocking collectives, body(): lax.all_to_all(rotate(locked, received, matrix), ('x', 'zl', 'yh', 'zh'),...  54.1 us
    ppermute x20, starting transfers between devices, exchange(): return lax.ppermute(value, axis, [(i, i ^ mask) for i in range(size)])  30.4 us
    ppermute x20, waiting for transfers between devices, exchange(): return lax.ppermute(value, axis, [(i, i ^ mask) for i in range(size)])  22.9 us
    all_to_all x1, starting transfers between devices, body(): lax.all_to_all(pack(vectors), ('yh', 'x'), split_axis=0, concat_axis=0, t...  7.28 us
    ppermute x2, starting transfers between devices, gather_panels(): guests = [lax.ppermute(spare, EIG + ('yl',), pair) for pair in pairs]  5.88 us
    pallas_call x1, Pallas kernels, rotate(): pl.pallas_call(rotate_kernel, in_specs=[pl.BlockSpec(memory_space=pltpu.S...  5.25 us
    pallas_call x1, Pallas kernels, place_panels(): pl.pallas_call(place_kernel, in_specs=[pl.BlockSpec(memory_space=pltpu.SM...  3.96 us
    all_to_all x1, starting transfers between devices, body(): lax.all_to_all(halfway.transpose(1, 0, 2, 3), ('zl', 'zh'), split_axis=0,...  3.59 us
  transfers between devices with their start and end apart: 24, of which 12 were waited for; matrix products, arithmetic and copies ran while one was open for 1% of the time, Pallas kernels for 3%

profile of v5, /device:TPU:16, one launch (start us, length us, event | category | flops | bytes accessed | tf_op | source)
XLA Modules:
  0.0 143.0 jit_solution(3888938586215055921)
XLA Ops:
  0.0 2.6 %shard_map.37 = bf16[8,8,104,128]{3,2,1,0:T(8,128)(2,1)} custom-call(bf16[32,25600]{1,0:T(8,128)(2,1)} %source_ref.1), custom_call_target="tpu_custom_call" | custom-call | tf_op jit(solution)/shard_map/pallas_call | solution.py:87
  2.6 0.0 copy-start.3
  2.6 7.3 %all-to-all-start = ((bf16[8,8,104,128]{3,2,1,0:T(8,128)(2,1)}), bf16[8,8,104,128]{3,2,1,0:T(8,128)(2,1)S(1)}, u32[]{:S(2)}, u32[]{:S(2)}) async-start(bf16[8,8,104,128]{3,2,1,0:T(8,128)(2,1)} %shard_map.37), calls=%async_computation | async-start | bytes 3407872 | tf_op jit(solution)/shard_map/all_to_all | solution.py:303
  9.9 0.0 copy-done.3
  9.9 4.6 %collective-permute-start.2 = (bf16[1,8,2048]{2,1,0:T(8,128)(2,1)S(1)}, bf16[1,8,2048]{2,1,0:T(8,128)(2,1)S(1)}, u32[]{:S(2)}, u32[]{:S(2)}) collective-permute-start(bf16[1,8,2048]{2,1,0:T(8,128)(2,1)S(1)} %bitcast.20), channel_id=1, source_target_pairs={{0,12},{4,8},{8,4},{12,0},{16,28},{20,24},{24,20},{28,16},{1,13},{... | collective-permute-start | bytes 98312 | tf_op jit(solution)/shard_map/ppermute | solution.py:262
  14.5 0.0 collective-permute-start.1
  14.5 0.7 collective-permute-start
  15.1 1.3 collective-permute-done.2
  16.4 2.9 %collective-permute-done.1 = bf16[1,8,2048]{2,1,0:T(8,128)(2,1)S(1)} collective-permute-done((bf16[1,8,2048]{2,1,0:T(8,128)(2,1)S(1)}, bf16[1,8,2048]{2,1,0:T(8,128)(2,1)S(1)}, u32[]{:S(2)}, u32[]{:S(2)}) %collective-permute-start.1) | collective-permute-done | bytes 32800 | tf_op jit(solution)/shard_map/ppermute | solution.py:262
  19.3 0.0 collective-permute-done
  19.3 4.6 %collective-permute-start.4 = (bf16[4,8,896]{2,1,0:T(8,128)(2,1)S(1)}, bf16[4,8,896]{2,1,0:T(8,128)(2,1)S(1)}, u32[]{:S(2)}, u32[]{:S(2)}) collective-permute-start(bf16[4,8,896]{2,1,0:T(8,128)(2,1)S(1)} %pad_maximum_fusion.5), channel_id=1, source_target_pairs={{0,16},{4,20},{8,24},{12,28},{16,0},{20,4},{24,8},{28,12},{1,17},{... | collective-permute-start | bytes 172040 | tf_op jit(solution)/shard_map/ppermute | solution.py:262
  24.0 1.5 %collective-permute-start.3 = (bf16[4,8,1152]{2,1,0:T(8,128)(2,1)S(1)}, bf16[4,8,1152]{2,1,0:T(8,128)(2,1)S(1)}, u32[]{:S(2)}, u32[]{:S(2)}) collective-permute-start(bf16[4,8,1152]{2,1,0:T(8,128)(2,1)S(1)} %slice.24), channel_id=1, source_target_pairs={{0,16},{4,20},{8,24},{12,28},{16,0},{20,4},{24,8},{28,12},{1,17},{... | collective-permute-start | bytes 221192 | tf_op jit(solution)/shard_map/ppermute | solution.py:262
  25.5 2.1 %collective-permute-done.4 = bf16[4,8,896]{2,1,0:T(8,128)(2,1)S(1)} collective-permute-done((bf16[4,8,896]{2,1,0:T(8,128)(2,1)S(1)}, bf16[4,8,896]{2,1,0:T(8,128)(2,1)S(1)}, u32[]{:S(2)}, u32[]{:S(2)}) %collective-permute-start.4) | collective-permute-done | bytes 57376 | tf_op jit(solution)/shard_map/ppermute | solution.py:262
  27.6 5.8 %collective-permute-done.3 = bf16[4,8,1152]{2,1,0:T(8,128)(2,1)S(1)} collective-permute-done((bf16[4,8,1152]{2,1,0:T(8,128)(2,1)S(1)}, bf16[4,8,1152]{2,1,0:T(8,128)(2,1)S(1)}, u32[]{:S(2)}, u32[]{:S(2)}) %collective-permute-start.3) | collective-permute-done | bytes 73760 | tf_op jit(solution)/shard_map/ppermute | solution.py:262
  33.5 4.6 %collective-permute-start.5 = (bf16[8,8,896]{2,1,0:T(8,128)(2,1)S(1)}, bf16[8,8,896]{2,1,0:T(8,128)(2,1)S(1)}, u32[]{:S(2)}, u32[]{:S(2)}) collective-permute-start(bf16[8,8,896]{2,1,0:T(8,128)(2,1)S(1)} %pad_maximum_fusion.4), channel_id=1, source_target_pairs={{128,96},{130,98},{132,100},{134,102},{136,104},{138,106},{140,108... | collective-permute-start | bytes 344072 | tf_op jit(solution)/shard_map/ppermute | solution.py:279
  38.1 1.3 collective-permute-start.7
  39.4 1.4 collective-permute-start.6
  40.8 0.0 collective-permute-done.5
  40.9 0.0 all-to-all-done
  40.9 1.4 copy.11
  42.3 3.6 %all-to-all-start.1 = ((bf16[8,8,104,128]{3,2,1,0:T(8,128)(2,1)}), bf16[8,8,104,128]{3,2,1,0:T(8,128)(2,1)S(1)}, u32[]{:S(2)}, u32[]{:S(2)}) async-start(bf16[8,8,104,128]{3,2,1,0:T(8,128)(2,1)} %bitcast.13), calls=%async_computation.1 | async-start | bytes 3407872 | tf_op jit(solution)/shard_map/all_to_all | solution.py:308
  45.9 0.0 collective-permute-done.7
  46.0 0.0 collective-permute-done.6
  46.1 0.1 collective-permute-start.10
  46.2 2.3 %collective-permute-start.9 = (bf16[1,64,1152]{2,1,0:T(8,128)(2,1)S(1)}, bf16[1,64,1152]{2,1,0:T(8,128)(2,1)S(1)}, u32[]{:S(2)}, u32[]{:S(2)}) collective-permute-start(bf16[1,64,1152]{2,1,0:T(8,128)(2,1)S(1)} %bitcast.15), channel_id=1, source_target_pairs={{0,64},{32,96},{64,0},{96,32},{1,65},{33,97},{65,1},{97,33},{2,66}... | collective-permute-start | bytes 442376 | tf_op jit(solution)/shard_map/ppermute | solution.py:262
  48.5 1.8 %collective-permute-start.8 = (bf16[1,64,1152]{2,1,0:T(8,128)(2,1)S(1)}, bf16[1,64,1152]{2,1,0:T(8,128)(2,1)S(1)}, u32[]{:S(2)}, u32[]{:S(2)}) collective-permute-start(bf16[1,64,1152]{2,1,0:T(8,128)(2,1)S(1)} %bitcast.16), channel_id=1, source_target_pairs={{0,32},{32,0},{64,96},{96,64},{1,33},{33,1},{65,97},{97,65},{2,34}... | collective-permute-start | bytes 442376 | tf_op jit(solution)/shard_map/ppermute | solution.py:262
  50.3 3.4 %collective-permute-start.11 = (bf16[1,64,1152]{2,1,0:T(8,128)(2,1)S(1)}, bf16[1,64,1152]{2,1,0:T(8,128)(2,1)S(1)}, u32[]{:S(2)}, u32[]{:S(2)}) collective-permute-start(bf16[1,64,1152]{2,1,0:T(8,128)(2,1)S(1)} %bitcast.18), channel_id=1, source_target_pairs={{0,128},{128,0},{1,129},{129,1},{2,130},{130,2},{3,131},{131,3},{4... | collective-permute-start | bytes 442376 | tf_op jit(solution)/shard_map/ppermute | solution.py:262
  53.7 0.4 collective-permute-done.10
  54.1 0.0 collective-permute-done.9
  54.2 0.9 collective-permute-done.8
  55.0 0.1 pad_maximum_fusion.refs_0_
  55.1 4.5 %collective-permute-start.12 = (bf16[4,64,1152]{2,1,0:T(8,128)(2,1)S(1)}, bf16[4,64,1152]{2,1,0:T(8,128)(2,1)S(1)}, u32[]{:S(2)}, u32[]{:S(2)}) collective-permute-start(bf16[4,64,1152]{2,1,0:T(8,128)(2,1)S(1)} %pad_maximum_fusion.refs_0_), channel_id=1, source_target_pairs={{0,128},{128,0},{1,129},{129,1},{2,130},{130,2},{3,131},{131,3},{4... | collective-permute-start | bytes 1769480 | tf_op jit(solution)/shard_map/ppermute | solution.py:262
  59.6 0.0 collective-permute-done.11
  59.6 2.3 %collective-permute-start.15 = (bf16[2,64,1152]{2,1,0:T(8,128)(2,1)S(1)}, bf16[2,64,1152]{2,1,0:T(8,128)(2,1)S(1)}, u32[]{:S(2)}, u32[]{:S(2)}) collective-permute-start(bf16[2,64,1152]{2,1,0:T(8,128)(2,1)S(1)} %pad_maximum_fusion.1.refs_2_), channel_id=1, source_target_pairs={{0,96},{32,64},{64,32},{96,0},{1,97},{33,65},{65,33},{97,1},{2,98}... | collective-permute-start | bytes 884744 | tf_op jit(solution)/shard_map/ppermute | solution.py:262
  61.9 0.2 collective-permute-start.14
  62.1 1.7 %collective-permute-start.13 = (bf16[2,64,1152]{2,1,0:T(8,128)(2,1)S(1)}, bf16[2,64,1152]{2,1,0:T(8,128)(2,1)}, u32[]{:S(2)}, u32[]{:S(2)}) collective-permute-start(bf16[2,64,1152]{2,1,0:T(8,128)(2,1)S(1)} %pad_maximum_fusion.1.refs_2_), channel_id=1, source_target_pairs={{0,32},{32,0},{64,96},{96,64},{1,33},{33,1},{65,97},{97,65},{2,34}... | collective-permute-start | bytes 884744 | tf_op jit(solution)/shard_map/ppermute | solution.py:262
  63.8 7.0 %collective-permute-done.15.refs_5_ = bf16[2,64,1152]{2,1,0:T(8,128)(2,1)S(1)} collective-permute-done((bf16[2,64,1152]{2,1,0:T(8,128)(2,1)S(1)}, bf16[2,64,1152]{2,1,0:T(8,128)(2,1)S(1)}, u32[]{:S(2)}, u32[]{:S(2)}) %collective-permute-start.15) | collective-permute-done | bytes 294944 | tf_op jit(solution)/shard_map/ppermute | solution.py:262
  70.8 0.0 collective-permute-start.21
  70.8 0.0 collective-permute-done.12.refs_1_
  70.8 0.5 collective-permute-start.16
  71.3 0.0 collective-permute-start.17
  71.3 0.0 collective-permute-done.14.refs_4_
  71.3 0.5 collective-permute-start.20
  71.8 0.0 collective-permute-done.13.refs_3_
  71.8 0.3 collective-permute-start.19
  72.1 0.6 collective-permute-done.21.refs_11_
  72.7 0.0 copy-start
  72.7 0.7 copy-done
  73.4 0.1 collective-permute-start.18
  73.6 0.0 copy-start.2
  73.6 0.1 pad_add_fusion.place_ref
  73.7 0.5 collective-permute-done.20.refs_10_
  74.1 0.8 collective-permute-done.19.refs_9_
  75.0 0.5 collective-permute-done.18.refs_8_
  75.5 0.0 collective-permute-done.16.refs_6_
  75.5 0.0 collective-permute-done.17.refs_7_
  75.5 0.0 copy-start.1
  75.5 1.0 copy-done.1
  76.4 4.0 %shard_map.38.source_ref = bf16[64,32,1152]{2,1,0:T(8,128)(2,1)} custom-call(s32[4]{0:T(128)S(1)} %pad_add_fusion.place_ref, bf16[4,64,1152]{2,1,0:T(8,128)(2,1)S(1)} %pad_maximum_fusion.refs_0_, bf16[4,64,1152]{2,1,0:T(8,128)(2,1)S(1)} %collective-permute-done.12.refs_1_, bf16[2,64,1152]{2,1,0:T(8,128)(2,1)S(1)} %pad_maximum_fusion.1.refs_2_, ...), custom_call_target="tpu_custom_call" | custom-call | tf_op jit(solution)/shard_map/pallas_call | solution.py:178
  80.4 1.8 %all-to-all-done.1.in_ref = bf16[8,8,104,128]{3,2,1,0:T(8,128)(2,1)S(1)} async-done(((bf16[8,8,104,128]{3,2,1,0:T(8,128)(2,1)}), bf16[8,8,104,128]{3,2,1,0:T(8,128)(2,1)S(1)}, u32[]{:S(2)}, u32[]{:S(2)}) %all-to-all-start.1) | async-done | bytes 1703968 | tf_op jit(solution)/shard_map/all_to_all | solution.py:308
  82.2 0.0 copy-done.2
  82.2 5.3 %shard_map.39 = bf16[64,104,128]{2,1,0:T(8,128)(2,1)S(1)} custom-call(s32[16]{0:T(128)S(1)} %copy-done.2, bf16[8,8,104,128]{3,2,1,0:T(8,128)(2,1)S(1)} %all-to-all-done.1.in_ref, bf16[64,32,1152]{2,1,0:T(8,128)(2,1)} %shard_map.38.source_ref), custom_call_target="tpu_custom_call" | custom-call | tf_op jit(solution)/shard_map/pallas_call | solution.py:247
  87.4 54.1 %all_to_all.15.in_ref = bf16[64,104,128]{2,1,0:T(8,128)(2,1)S(1)} all-to-all(bf16[64,104,128]{2,1,0:T(8,128)(2,1)S(1)} %shard_map.39), channel_id=1, replica_groups=mesh['yh'=2,'x'=4,'zh'=2,'zl'=4,'yl'=2,'c'=2] {'x','zl','yh','zh'}, dimensions={0} | all-to-all | bytes 3407872 | tf_op jit(solution)/shard_map/all_to_all | solution.py:309
  141.6 1.3 shard_map.40
  (16 shorter events, 0.4 us)
Async XLA Ops:
  2.6 7.3 %copy-start.3 = (bf16[8,2048]{1,0:T(8,128)(2,1)S(1)}, bf16[8,2048]{1,0:T(8,128)(2,1)}, u32[]{:S(2)}) copy-start(bf16[8,2048]{1,0:T(8,128)(2,1)} %param.4) | copy-start | bytes 98308
  2.6 38.3 %all-to-all-start = ((bf16[8,8,104,128]{3,2,1,0:T(8,128)(2,1)}), bf16[8,8,104,128]{3,2,1,0:T(8,128)(2,1)S(1)}, u32[]{:S(2)}, u32[]{:S(2)}) async-start(bf16[8,8,104,128]{3,2,1,0:T(8,128)(2,1)} %shard_map.37), calls=%async_computation | async-start | bytes 3407872 | tf_op jit(solution)/shard_map/all_to_all | solution.py:303
  9.9 6.5 %collective-permute-start.2 = (bf16[1,8,2048]{2,1,0:T(8,128)(2,1)S(1)}, bf16[1,8,2048]{2,1,0:T(8,128)(2,1)S(1)}, u32[]{:S(2)}, u32[]{:S(2)}) collective-permute-start(bf16[1,8,2048]{2,1,0:T(8,128)(2,1)S(1)} %bitcast.20), channel_id=1, source_target_pairs={{0,12},{4,8},{8,4},{12,0},{16,28},{20,24},{24,20},{28,16},{1,13},{... | collective-permute-start | bytes 98312 | tf_op jit(solution)/shard_map/ppermute | solution.py:262
  14.5 4.8 %collective-permute-start.1 = (bf16[1,8,2048]{2,1,0:T(8,128)(2,1)S(1)}, bf16[1,8,2048]{2,1,0:T(8,128)(2,1)S(1)}, u32[]{:S(2)}, u32[]{:S(2)}) collective-permute-start(bf16[1,8,2048]{2,1,0:T(8,128)(2,1)S(1)} %bitcast.21), channel_id=1, source_target_pairs={{0,8},{4,12},{8,0},{12,4},{16,24},{20,28},{24,16},{28,20},{1,9},{5... | collective-permute-start | bytes 98312 | tf_op jit(solution)/shard_map/ppermute | solution.py:262
  14.5 4.8 %collective-permute-start = (bf16[1,8,2048]{2,1,0:T(8,128)(2,1)S(1)}, bf16[1,8,2048]{2,1,0:T(8,128)(2,1)S(1)}, u32[]{:S(2)}, u32[]{:S(2)}) collective-permute-start(bf16[1,8,2048]{2,1,0:T(8,128)(2,1)S(1)} %bitcast.22), channel_id=1, source_target_pairs={{0,4},{4,0},{8,12},{12,8},{16,20},{20,16},{24,28},{28,24},{1,5},{5... | collective-permute-start | bytes 98312 | tf_op jit(solution)/shard_map/ppermute | solution.py:262
  19.3 8.3 %collective-permute-start.4 = (bf16[4,8,896]{2,1,0:T(8,128)(2,1)S(1)}, bf16[4,8,896]{2,1,0:T(8,128)(2,1)S(1)}, u32[]{:S(2)}, u32[]{:S(2)}) collective-permute-start(bf16[4,8,896]{2,1,0:T(8,128)(2,1)S(1)} %pad_maximum_fusion.5), channel_id=1, source_target_pairs={{0,16},{4,20},{8,24},{12,28},{16,0},{20,4},{24,8},{28,12},{1,17},{... | collective-permute-start | bytes 172040 | tf_op jit(solution)/shard_map/ppermute | solution.py:262
  24.0 9.5 %collective-permute-start.3 = (bf16[4,8,1152]{2,1,0:T(8,128)(2,1)S(1)}, bf16[4,8,1152]{2,1,0:T(8,128)(2,1)S(1)}, u32[]{:S(2)}, u32[]{:S(2)}) collective-permute-start(bf16[4,8,1152]{2,1,0:T(8,128)(2,1)S(1)} %slice.24), channel_id=1, source_target_pairs={{0,16},{4,20},{8,24},{12,28},{16,0},{20,4},{24,8},{28,12},{1,17},{... | collective-permute-start | bytes 221192 | tf_op jit(solution)/shard_map/ppermute | solution.py:262
  33.5 7.3 %collective-permute-start.5 = (bf16[8,8,896]{2,1,0:T(8,128)(2,1)S(1)}, bf16[8,8,896]{2,1,0:T(8,128)(2,1)S(1)}, u32[]{:S(2)}, u32[]{:S(2)}) collective-permute-start(bf16[8,8,896]{2,1,0:T(8,128)(2,1)S(1)} %pad_maximum_fusion.4), channel_id=1, source_target_pairs={{128,96},{130,98},{132,100},{134,102},{136,104},{138,106},{140,108... | collective-permute-start | bytes 344072 | tf_op jit(solution)/shard_map/ppermute | solution.py:279
  38.1 7.8 %collective-permute-start.7 = (bf16[8,8,896]{2,1,0:T(8,128)(2,1)S(1)}, bf16[8,8,896]{2,1,0:T(8,128)(2,1)S(1)}, u32[]{:S(2)}, u32[]{:S(2)}) collective-permute-start(bf16[8,8,896]{2,1,0:T(8,128)(2,1)S(1)} %pad_maximum_fusion.4), channel_id=1, source_target_pairs={{128,98},{130,96},{132,102},{134,100},{136,106},{138,104},{140,110... | collective-permute-start | bytes 344072 | tf_op jit(solution)/shard_map/ppermute | solution.py:279
  39.4 6.6 %collective-permute-start.6 = (bf16[8,8,1152]{2,1,0:T(8,128)(2,1)S(1)}, bf16[8,8,1152]{2,1,0:T(8,128)(2,1)S(1)}, u32[]{:S(2)}, u32[]{:S(2)}) collective-permute-start(bf16[8,8,1152]{2,1,0:T(8,128)(2,1)S(1)} %pad_maximum_fusion.2), channel_id=1, source_target_pairs={{0,2},{2,0},{1,3},{3,1},{4,6},{6,4},{5,7},{7,5},{8,10},{10,8},{9,1... | collective-permute-start | bytes 442376 | tf_op jit(solution)/shard_map/ppermute | solution.py:262
  42.3 39.9 %all-to-all-start.1 = ((bf16[8,8,104,128]{3,2,1,0:T(8,128)(2,1)}), bf16[8,8,104,128]{3,2,1,0:T(8,128)(2,1)S(1)}, u32[]{:S(2)}, u32[]{:S(2)}) async-start(bf16[8,8,104,128]{3,2,1,0:T(8,128)(2,1)} %bitcast.13), calls=%async_computation.1 | async-start | bytes 3407872 | tf_op jit(solution)/shard_map/all_to_all | solution.py:308
  46.1 8.0 %collective-permute-start.10 = (bf16[1,64,1152]{2,1,0:T(8,128)(2,1)S(1)}, bf16[1,64,1152]{2,1,0:T(8,128)(2,1)S(1)}, u32[]{:S(2)}, u32[]{:S(2)}) collective-permute-start(bf16[1,64,1152]{2,1,0:T(8,128)(2,1)S(1)} %bitcast.14), channel_id=1, source_target_pairs={{0,96},{32,64},{64,32},{96,0},{1,97},{33,65},{65,33},{97,1},{2,98}... | collective-permute-start | bytes 442376 | tf_op jit(solution)/shard_map/ppermute | solution.py:262
  46.2 7.9 %collective-permute-start.9 = (bf16[1,64,1152]{2,1,0:T(8,128)(2,1)S(1)}, bf16[1,64,1152]{2,1,0:T(8,128)(2,1)S(1)}, u32[]{:S(2)}, u32[]{:S(2)}) collective-permute-start(bf16[1,64,1152]{2,1,0:T(8,128)(2,1)S(1)} %bitcast.15), channel_id=1, source_target_pairs={{0,64},{32,96},{64,0},{96,32},{1,65},{33,97},{65,1},{97,33},{2,66}... | collective-permute-start | bytes 442376 | tf_op jit(solution)/shard_map/ppermute | solution.py:262
  48.5 6.5 %collective-permute-start.8 = (bf16[1,64,1152]{2,1,0:T(8,128)(2,1)S(1)}, bf16[1,64,1152]{2,1,0:T(8,128)(2,1)S(1)}, u32[]{:S(2)}, u32[]{:S(2)}) collective-permute-start(bf16[1,64,1152]{2,1,0:T(8,128)(2,1)S(1)} %bitcast.16), channel_id=1, source_target_pairs={{0,32},{32,0},{64,96},{96,64},{1,33},{33,1},{65,97},{97,65},{2,34}... | collective-permute-start | bytes 442376 | tf_op jit(solution)/shard_map/ppermute | solution.py:262
  50.3 9.3 %collective-permute-start.11 = (bf16[1,64,1152]{2,1,0:T(8,128)(2,1)S(1)}, bf16[1,64,1152]{2,1,0:T(8,128)(2,1)S(1)}, u32[]{:S(2)}, u32[]{:S(2)}) collective-permute-start(bf16[1,64,1152]{2,1,0:T(8,128)(2,1)S(1)} %bitcast.18), channel_id=1, source_target_pairs={{0,128},{128,0},{1,129},{129,1},{2,130},{130,2},{3,131},{131,3},{4... | collective-permute-start | bytes 442376 | tf_op jit(solution)/shard_map/ppermute | solution.py:262
  55.1 15.7 %collective-permute-start.12 = (bf16[4,64,1152]{2,1,0:T(8,128)(2,1)S(1)}, bf16[4,64,1152]{2,1,0:T(8,128)(2,1)S(1)}, u32[]{:S(2)}, u32[]{:S(2)}) collective-permute-start(bf16[4,64,1152]{2,1,0:T(8,128)(2,1)S(1)} %pad_maximum_fusion.refs_0_), channel_id=1, source_target_pairs={{0,128},{128,0},{1,129},{129,1},{2,130},{130,2},{3,131},{131,3},{4... | collective-permute-start | bytes 1769480 | tf_op jit(solution)/shard_map/ppermute | solution.py:262
  59.6 11.2 %collective-permute-start.15 = (bf16[2,64,1152]{2,1,0:T(8,128)(2,1)S(1)}, bf16[2,64,1152]{2,1,0:T(8,128)(2,1)S(1)}, u32[]{:S(2)}, u32[]{:S(2)}) collective-permute-start(bf16[2,64,1152]{2,1,0:T(8,128)(2,1)S(1)} %pad_maximum_fusion.1.refs_2_), channel_id=1, source_target_pairs={{0,96},{32,64},{64,32},{96,0},{1,97},{33,65},{65,33},{97,1},{2,98}... | collective-permute-start | bytes 884744 | tf_op jit(solution)/shard_map/ppermute | solution.py:262
  61.9 9.4 %collective-permute-start.14 = (bf16[2,64,1152]{2,1,0:T(8,128)(2,1)S(1)}, bf16[2,64,1152]{2,1,0:T(8,128)(2,1)}, u32[]{:S(2)}, u32[]{:S(2)}) collective-permute-start(bf16[2,64,1152]{2,1,0:T(8,128)(2,1)S(1)} %pad_maximum_fusion.1.refs_2_), channel_id=1, source_target_pairs={{0,64},{32,96},{64,0},{96,32},{1,65},{33,97},{65,1},{97,33},{2,66}... | collective-permute-start | bytes 884744 | tf_op jit(solution)/shard_map/ppermute | solution.py:262
  62.1 9.7 %collective-permute-start.13 = (bf16[2,64,1152]{2,1,0:T(8,128)(2,1)S(1)}, bf16[2,64,1152]{2,1,0:T(8,128)(2,1)}, u32[]{:S(2)}, u32[]{:S(2)}) collective-permute-start(bf16[2,64,1152]{2,1,0:T(8,128)(2,1)S(1)} %pad_maximum_fusion.1.refs_2_), channel_id=1, source_target_pairs={{0,32},{32,0},{64,96},{96,64},{1,33},{33,1},{65,97},{97,65},{2,34}... | collective-permute-start | bytes 884744 | tf_op jit(solution)/shard_map/ppermute | solution.py:262
  70.8 1.9 %collective-permute-start.21 = (bf16[2,64,1152]{2,1,0:T(8,128)(2,1)S(1)}, bf16[2,64,1152]{2,1,0:T(8,128)(2,1)S(1)}, u32[]{:S(2)}, u32[]{:S(2)}) collective-permute-start(bf16[2,64,1152]{2,1,0:T(8,128)(2,1)S(1)} %collective-permute-done.15.refs_5_), channel_id=1, source_target_pairs={{0,1},{1,0},{2,3},{3,2},{4,5},{5,4},{6,7},{7,6},{8,9},{9,8},{10,11... | collective-permute-start | bytes 884744 | tf_op jit(solution)/shard_map/ppermute | solution.py:262
  70.8 4.7 %collective-permute-start.16 = (bf16[4,64,1152]{2,1,0:T(8,128)(2,1)S(1)}, bf16[4,64,1152]{2,1,0:T(8,128)(2,1)}, u32[]{:S(2)}, u32[]{:S(2)}) collective-permute-start(bf16[4,64,1152]{2,1,0:T(8,128)(2,1)S(1)} %pad_maximum_fusion.refs_0_), channel_id=1, source_target_pairs={{0,1},{1,0},{2,3},{3,2},{4,5},{5,4},{6,7},{7,6},{8,9},{9,8},{10,11... | collective-permute-start | bytes 1769480 | tf_op jit(solution)/shard_map/ppermute | solution.py:262
  71.3 4.2 %collective-permute-start.17 = (bf16[4,64,1152]{2,1,0:T(8,128)(2,1)S(1)}, bf16[4,64,1152]{2,1,0:T(8,128)(2,1)}, u32[]{:S(2)}, u32[]{:S(2)}) collective-permute-start(bf16[4,64,1152]{2,1,0:T(8,128)(2,1)S(1)} %collective-permute-done.12.refs_1_), channel_id=1, source_target_pairs={{0,1},{1,0},{2,3},{3,2},{4,5},{5,4},{6,7},{7,6},{8,9},{9,8},{10,11... | collective-permute-start | bytes 1769480 | tf_op jit(solution)/shard_map/ppermute | solution.py:262
  71.3 2.8 %collective-permute-start.20 = (bf16[2,64,1152]{2,1,0:T(8,128)(2,1)}, bf16[2,64,1152]{2,1,0:T(8,128)(2,1)}, u32[]{:S(2)}, u32[]{:S(2)}) collective-permute-start(bf16[2,64,1152]{2,1,0:T(8,128)(2,1)} %collective-permute-done.14.refs_4_), channel_id=1, source_target_pairs={{0,1},{1,0},{2,3},{3,2},{4,5},{5,4},{6,7},{7,6},{8,9},{9,8},{10,11... | collective-permute-start | bytes 884744 | tf_op jit(solution)/shard_map/ppermute | solution.py:262
  71.8 3.1 %collective-permute-start.19 = (bf16[2,64,1152]{2,1,0:T(8,128)(2,1)}, bf16[2,64,1152]{2,1,0:T(8,128)(2,1)}, u32[]{:S(2)}, u32[]{:S(2)}) collective-permute-start(bf16[2,64,1152]{2,1,0:T(8,128)(2,1)} %collective-permute-done.13.refs_3_), channel_id=1, source_target_pairs={{0,1},{1,0},{2,3},{3,2},{4,5},{5,4},{6,7},{7,6},{8,9},{9,8},{10,11... | collective-permute-start | bytes 884744 | tf_op jit(solution)/shard_map/ppermute | solution.py:262
  72.7 0.7 copy-start
  73.4 2.0 %collective-permute-start.18 = (bf16[2,64,1152]{2,1,0:T(8,128)(2,1)S(1)}, bf16[2,64,1152]{2,1,0:T(8,128)(2,1)}, u32[]{:S(2)}, u32[]{:S(2)}) collective-permute-start(bf16[2,64,1152]{2,1,0:T(8,128)(2,1)S(1)} %pad_maximum_fusion.1.refs_2_), channel_id=1, source_target_pairs={{0,1},{1,0},{2,3},{3,2},{4,5},{5,4},{6,7},{7,6},{8,9},{9,8},{10,11... | collective-permute-start | bytes 884744 | tf_op jit(solution)/shard_map/ppermute | solution.py:262
  73.6 8.6 %copy-start.2 = (s32[16]{0:T(128)S(1)}, s32[16]{0:T(128)}, u32[]{:S(2)}) copy-start(s32[16]{0:T(128)} %locked_ref.1) | copy-start | bytes 196
  75.5 1.0 copy-start.1

commit v6 on v5

--- a/solution.py
+++ b/solution.py
@@ -269,7 +269,7 @@
     return [jnp.concatenate([part, exchange(part, Z, 8, 4)]) for part in parts]
 
 
-def gather_panels(keep, spare):
+def gather_panels(keep, spare, halfway):
     eig, yl = lax.axis_index(EIG), lax.axis_index("yl")
     group = eig // 8
     late = [i for i in range(PEERS) if i >= 32]
@@ -278,6 +278,7 @@
     pairs = [[(2 * i + s, 2 * mirror[i] + (s ^ flip)) for i in late for s in range(2)] for flip in (0, 1)]
     guests = [lax.ppermute(spare, EIG + ("yl",), pair) for pair in pairs]
     other = exchange(keep, "yl", 2, 1)
+    *guests, _ = lax.optimization_barrier((*guests, halfway))
     place = 256 * (group + 1)
     cols = lax.broadcasted_iota(jnp.int32, (1, 1, KEEP), 2)
 
@@ -304,7 +305,7 @@
     keep, spare = gather_near(rotation)
     halfway, *_ = lax.optimization_barrier((halfway, keep, spare))
     place = jnp.stack([lax.axis_index(name) for name in ("c", "yh", "x", Z)]).astype(jnp.int32)
-    matrix = place_panels(place, gather_panels(keep, spare))
+    matrix = place_panels(place, gather_panels(keep, spare, halfway))
     received = lax.all_to_all(halfway.transpose(1, 0, 2, 3), ("zl", "zh"), split_axis=0, concat_axis=0, tiled=True)
     back = lax.all_to_all(rotate(locked, received, matrix), ("x", "zl", "yh", "zh"), split_axis=0, concat_axis=0, tiled=True)
     return unpack(back)

time: 144 us -> 143 us (level)
  no operation moved by 1% of the time
where the time goes in v6:
time: 143 us
  blocking collectives  53.9 us (38%)
  starting transfers between devices  46.5 us (33%)
  waiting for transfers between devices  25.2 us (18%)
  Pallas kernels  13.1 us (9%)
  local copies, waits for them, and re-layouts  3.28 us (2%)
    all_to_all x1, blocking collectives, body(): lax.all_to_all(rotate(locked, received, matrix), ('x', 'zl', 'yh', 'zh'),...  53.9 us
    ppermute x20, starting transfers between devices, exchange(): return lax.ppermute(value, axis, [(i, i ^ mask) for i in range(size)])  29.8 us
    ppermute x20, waiting for transfers between devices, exchange(): return lax.ppermute(value, axis, [(i, i ^ mask) for i in range(size)])  23.1 us
    all_to_all x1, starting transfers between devices, body(): lax.all_to_all(pack(vectors), ('yh', 'x'), split_axis=0, concat_axis=0, t...  7.28 us
    ppermute x2, starting transfers between devices, gather_panels(): guests = [lax.ppermute(spare, EIG + ('yl',), pair) for pair in pairs]  5.87 us
    pallas_call x1, Pallas kernels, rotate(): pl.pallas_call(rotate_kernel, in_specs=[pl.BlockSpec(memory_space=pltpu.S...  5.26 us
    pallas_call x1, Pallas kernels, place_panels(): pl.pallas_call(place_kernel, in_specs=[pl.BlockSpec(memory_space=pltpu.SM...  3.96 us
    all_to_all x1, starting transfers between devices, body(): lax.all_to_all(halfway.transpose(1, 0, 2, 3), ('zl', 'zh'), split_axis=0,...  3.59 us
  transfers between devices with their start and end apart: 24, of which 12 were waited for; matrix products, arithmetic and copies ran while one was open for 1% of the time, Pallas kernels for 3%

profile of v6, /device:TPU:16, one launch (start us, length us, event | category | flops | bytes accessed | tf_op | source)
XLA Modules:
  0.0 142.7 jit_solution(15687913442370334664)
XLA Ops:
  0.0 2.6 %shard_map.37 = bf16[8,8,104,128]{3,2,1,0:T(8,128)(2,1)} custom-call(bf16[32,25600]{1,0:T(8,128)(2,1)} %source_ref.1), custom_call_target="tpu_custom_call" | custom-call | tf_op jit(solution)/shard_map/pallas_call | solution.py:87
  2.6 0.0 copy-start.3
  2.6 7.3 %all-to-all-start = ((bf16[8,8,104,128]{3,2,1,0:T(8,128)(2,1)}), bf16[8,8,104,128]{3,2,1,0:T(8,128)(2,1)S(1)}, u32[]{:S(2)}, u32[]{:S(2)}) async-start(bf16[8,8,104,128]{3,2,1,0:T(8,128)(2,1)} %shard_map.37), calls=%async_computation | async-start | bytes 3407872 | tf_op jit(solution)/shard_map/all_to_all | solution.py:304
  9.9 0.0 copy-done.3
  9.9 4.6 %collective-permute-start.2 = (bf16[1,8,2048]{2,1,0:T(8,128)(2,1)S(1)}, bf16[1,8,2048]{2,1,0:T(8,128)(2,1)S(1)}, u32[]{:S(2)}, u32[]{:S(2)}) collective-permute-start(bf16[1,8,2048]{2,1,0:T(8,128)(2,1)S(1)} %bitcast.20), channel_id=1, source_target_pairs={{0,12},{4,8},{8,4},{12,0},{16,28},{20,24},{24,20},{28,16},{1,13},{... | collective-permute-start | bytes 98312 | tf_op jit(solution)/shard_map/ppermute | solution.py:262
  14.5 0.0 collective-permute-start.1
  14.5 0.7 collective-permute-start
  15.1 1.3 collective-permute-done.2
  16.4 2.9 %collective-permute-done.1 = bf16[1,8,2048]{2,1,0:T(8,128)(2,1)S(1)} collective-permute-done((bf16[1,8,2048]{2,1,0:T(8,128)(2,1)S(1)}, bf16[1,8,2048]{2,1,0:T(8,128)(2,1)S(1)}, u32[]{:S(2)}, u32[]{:S(2)}) %collective-permute-start.1) | collective-permute-done | bytes 32800 | tf_op jit(solution)/shard_map/ppermute | solution.py:262
  19.3 0.0 collective-permute-done
  19.3 4.6 %collective-permute-start.4 = (bf16[4,8,896]{2,1,0:T(8,128)(2,1)S(1)}, bf16[4,8,896]{2,1,0:T(8,128)(2,1)S(1)}, u32[]{:S(2)}, u32[]{:S(2)}) collective-permute-start(bf16[4,8,896]{2,1,0:T(8,128)(2,1)S(1)} %pad_maximum_fusion.5), channel_id=1, source_target_pairs={{0,16},{4,20},{8,24},{12,28},{16,0},{20,4},{24,8},{28,12},{1,17},{... | collective-permute-start | bytes 172040 | tf_op jit(solution)/shard_map/ppermute | solution.py:262
  24.0 1.5 %collective-permute-start.3 = (bf16[4,8,1152]{2,1,0:T(8,128)(2,1)S(1)}, bf16[4,8,1152]{2,1,0:T(8,128)(2,1)S(1)}, u32[]{:S(2)}, u32[]{:S(2)}) collective-permute-start(bf16[4,8,1152]{2,1,0:T(8,128)(2,1)S(1)} %slice.24), channel_id=1, source_target_pairs={{0,16},{4,20},{8,24},{12,28},{16,0},{20,4},{24,8},{28,12},{1,17},{... | collective-permute-start | bytes 221192 | tf_op jit(solution)/shard_map/ppermute | solution.py:262
  25.5 2.1 %collective-permute-done.4 = bf16[4,8,896]{2,1,0:T(8,128)(2,1)S(1)} collective-permute-done((bf16[4,8,896]{2,1,0:T(8,128)(2,1)S(1)}, bf16[4,8,896]{2,1,0:T(8,128)(2,1)S(1)}, u32[]{:S(2)}, u32[]{:S(2)}) %collective-permute-start.4) | collective-permute-done | bytes 57376 | tf_op jit(solution)/shard_map/ppermute | solution.py:262
  27.6 5.8 %collective-permute-done.3 = bf16[4,8,1152]{2,1,0:T(8,128)(2,1)S(1)} collective-permute-done((bf16[4,8,1152]{2,1,0:T(8,128)(2,1)S(1)}, bf16[4,8,1152]{2,1,0:T(8,128)(2,1)S(1)}, u32[]{:S(2)}, u32[]{:S(2)}) %collective-permute-start.3) | collective-permute-done | bytes 73760 | tf_op jit(solution)/shard_map/ppermute | solution.py:262
  33.5 3.8 %collective-permute-start.6 = (bf16[8,8,896]{2,1,0:T(8,128)(2,1)S(1)}, bf16[8,8,896]{2,1,0:T(8,128)(2,1)S(1)}, u32[]{:S(2)}, u32[]{:S(2)}) collective-permute-start(bf16[8,8,896]{2,1,0:T(8,128)(2,1)S(1)} %pad_maximum_fusion.4), channel_id=1, source_target_pairs={{128,98},{130,96},{132,102},{134,100},{136,106},{138,104},{140,110... | collective-permute-start | bytes 344072 | tf_op jit(solution)/shard_map/ppermute | solution.py:279
  37.3 2.1 %collective-permute-start.5 = (bf16[8,8,896]{2,1,0:T(8,128)(2,1)S(1)}, bf16[8,8,896]{2,1,0:T(8,128)(2,1)S(1)}, u32[]{:S(2)}, u32[]{:S(2)}) collective-permute-start(bf16[8,8,896]{2,1,0:T(8,128)(2,1)S(1)} %pad_maximum_fusion.4), channel_id=1, source_target_pairs={{128,96},{130,98},{132,100},{134,102},{136,104},{138,106},{140,108... | collective-permute-start | bytes 344072 | tf_op jit(solution)/shard_map/ppermute | solution.py:279
  39.4 1.4 collective-permute-start.7
  40.8 0.0 all-to-all-done
  40.8 1.4 copy.11
  42.2 0.0 collective-permute-done.6
  42.2 0.0 collective-permute-done.5
  42.2 3.6 %all-to-all-start.1 = ((bf16[8,8,104,128]{3,2,1,0:T(8,128)(2,1)}), bf16[8,8,104,128]{3,2,1,0:T(8,128)(2,1)S(1)}, u32[]{:S(2)}, u32[]{:S(2)}) async-start(bf16[8,8,104,128]{3,2,1,0:T(8,128)(2,1)} %bitcast.13), calls=%async_computation.1 | async-start | bytes 3407872 | tf_op jit(solution)/shard_map/all_to_all | solution.py:309
  46.0 0.0 collective-permute-done.7
  46.0 0.1 fusion.1
  46.1 0.1 collective-permute-start.10
  46.2 2.3 %collective-permute-start.9 = (bf16[1,64,1152]{2,1,0:T(8,128)(2,1)S(1)}, bf16[1,64,1152]{2,1,0:T(8,128)(2,1)S(1)}, u32[]{:S(2)}, u32[]{:S(2)}) collective-permute-start(bf16[1,64,1152]{2,1,0:T(8,128)(2,1)S(1)} %bitcast.15), channel_id=1, source_target_pairs={{0,64},{32,96},{64,0},{96,32},{1,65},{33,97},{65,1},{97,33},{2,66}... | collective-permute-start | bytes 442376 | tf_op jit(solution)/shard_map/ppermute | solution.py:262
  48.5 1.8 %collective-permute-start.8 = (bf16[1,64,1152]{2,1,0:T(8,128)(2,1)S(1)}, bf16[1,64,1152]{2,1,0:T(8,128)(2,1)S(1)}, u32[]{:S(2)}, u32[]{:S(2)}) collective-permute-start(bf16[1,64,1152]{2,1,0:T(8,128)(2,1)S(1)} %bitcast.16), channel_id=1, source_target_pairs={{0,32},{32,0},{64,96},{96,64},{1,33},{33,1},{65,97},{97,65},{2,34}... | collective-permute-start | bytes 442376 | tf_op jit(solution)/shard_map/ppermute | solution.py:262
  50.3 3.1 %collective-permute-start.11 = (bf16[1,64,1152]{2,1,0:T(8,128)(2,1)S(1)}, bf16[1,64,1152]{2,1,0:T(8,128)(2,1)S(1)}, u32[]{:S(2)}, u32[]{:S(2)}) collective-permute-start(bf16[1,64,1152]{2,1,0:T(8,128)(2,1)S(1)} %bitcast.18), channel_id=1, source_target_pairs={{0,128},{128,0},{1,129},{129,1},{2,130},{130,2},{3,131},{131,3},{4... | collective-permute-start | bytes 442376 | tf_op jit(solution)/shard_map/ppermute | solution.py:262
  53.5 0.7 collective-permute-done.10
  54.1 0.0 collective-permute-done.9
  54.1 0.9 collective-permute-done.8
  55.0 0.1 pad_maximum_fusion.refs_0_
  55.1 4.1 %collective-permute-start.12 = (bf16[4,64,1152]{2,1,0:T(8,128)(2,1)S(1)}, bf16[4,64,1152]{2,1,0:T(8,128)(2,1)S(1)}, u32[]{:S(2)}, u32[]{:S(2)}) collective-permute-start(bf16[4,64,1152]{2,1,0:T(8,128)(2,1)S(1)} %pad_maximum_fusion.refs_0_), channel_id=1, source_target_pairs={{0,128},{128,0},{1,129},{129,1},{2,130},{130,2},{3,131},{131,3},{4... | collective-permute-start | bytes 1769480 | tf_op jit(solution)/shard_map/ppermute | solution.py:262
  59.2 0.0 collective-permute-done.11
  59.3 2.2 %collective-permute-start.15 = (bf16[2,64,1152]{2,1,0:T(8,128)(2,1)S(1)}, bf16[2,64,1152]{2,1,0:T(8,128)(2,1)S(1)}, u32[]{:S(2)}, u32[]{:S(2)}) collective-permute-start(bf16[2,64,1152]{2,1,0:T(8,128)(2,1)S(1)} %pad_maximum_fusion.1.refs_2_), channel_id=1, source_target_pairs={{0,96},{32,64},{64,32},{96,0},{1,97},{33,65},{65,33},{97,1},{2,98}... | collective-permute-start | bytes 884744 | tf_op jit(solution)/shard_map/ppermute | solution.py:262
  61.5 0.0 collective-permute-start.14
  61.5 2.0 %collective-permute-start.13 = (bf16[2,64,1152]{2,1,0:T(8,128)(2,1)S(1)}, bf16[2,64,1152]{2,1,0:T(8,128)(2,1)}, u32[]{:S(2)}, u32[]{:S(2)}) collective-permute-start(bf16[2,64,1152]{2,1,0:T(8,128)(2,1)S(1)} %pad_maximum_fusion.1.refs_2_), channel_id=1, source_target_pairs={{0,32},{32,0},{64,96},{96,64},{1,33},{33,1},{65,97},{97,65},{2,34}... | collective-permute-start | bytes 884744 | tf_op jit(solution)/shard_map/ppermute | solution.py:262
  63.5 7.0 %collective-permute-done.15.refs_5_ = bf16[2,64,1152]{2,1,0:T(8,128)(2,1)S(1)} collective-permute-done((bf16[2,64,1152]{2,1,0:T(8,128)(2,1)S(1)}, bf16[2,64,1152]{2,1,0:T(8,128)(2,1)S(1)}, u32[]{:S(2)}, u32[]{:S(2)}) %collective-permute-start.15) | collective-permute-done | bytes 294944 | tf_op jit(solution)/shard_map/ppermute | solution.py:262
  70.5 0.0 collective-permute-start.21
  70.5 0.0 collective-permute-done.12.refs_1_
  70.5 0.5 collective-permute-start.16
  71.0 0.0 collective-permute-start.17
  71.0 0.0 collective-permute-done.14.refs_4_
  71.0 0.5 collective-permute-start.20
  71.5 0.0 collective-permute-done.13.refs_3_
  71.5 0.3 collective-permute-start.19
  71.8 0.6 collective-permute-done.21.refs_11_
  72.4 0.0 copy-start
  72.4 0.7 copy-done
  73.1 0.1 collective-permute-start.18
  73.2 0.1 pad_add_fusion.place_ref
  73.3 0.5 collective-permute-done.20.refs_10_
  73.8 0.8 collective-permute-done.19.refs_9_
  74.6 0.5 collective-permute-done.18.refs_8_
  75.1 0.0 collective-permute-done.16.refs_6_
  75.1 0.0 collective-permute-done.17.refs_7_
  75.1 0.0 copy-start.1
  75.1 1.0 copy-done.1
  76.1 4.0 %shard_map.38.source_ref = bf16[64,32,1152]{2,1,0:T(8,128)(2,1)} custom-call(s32[4]{0:T(128)S(1)} %pad_add_fusion.place_ref, bf16[4,64,1152]{2,1,0:T(8,128)(2,1)S(1)} %pad_maximum_fusion.refs_0_, bf16[4,64,1152]{2,1,0:T(8,128)(2,1)S(1)} %collective-permute-done.12.refs_1_, bf16[2,64,1152]{2,1,0:T(8,128)(2,1)S(1)} %pad_maximum_fusion.1.refs_2_, ...), custom_call_target="tpu_custom_call" | custom-call | tf_op jit(solution)/shard_map/pallas_call | solution.py:178
  80.1 2.0 %all-to-all-done.1.in_ref = bf16[8,8,104,128]{3,2,1,0:T(8,128)(2,1)S(1)} async-done(((bf16[8,8,104,128]{3,2,1,0:T(8,128)(2,1)}), bf16[8,8,104,128]{3,2,1,0:T(8,128)(2,1)S(1)}, u32[]{:S(2)}, u32[]{:S(2)}) %all-to-all-start.1) | async-done | bytes 1703968 | tf_op jit(solution)/shard_map/all_to_all | solution.py:309
  82.1 0.0 copy-done.2
  82.1 5.3 %shard_map.39 = bf16[64,104,128]{2,1,0:T(8,128)(2,1)S(1)} custom-call(s32[16]{0:T(128)S(1)} %copy-done.2, bf16[8,8,104,128]{3,2,1,0:T(8,128)(2,1)S(1)} %all-to-all-done.1.in_ref, bf16[64,32,1152]{2,1,0:T(8,128)(2,1)} %shard_map.38.source_ref), custom_call_target="tpu_custom_call" | custom-call | tf_op jit(solution)/shard_map/pallas_call | solution.py:247
  87.4 53.9 %all_to_all.15.in_ref = bf16[64,104,128]{2,1,0:T(8,128)(2,1)S(1)} all-to-all(bf16[64,104,128]{2,1,0:T(8,128)(2,1)S(1)} %shard_map.39), channel_id=1, replica_groups=mesh['yh'=2,'x'=4,'zh'=2,'zl'=4,'yl'=2,'c'=2] {'x','zl','yh','zh'}, dimensions={0} | all-to-all | bytes 3407872 | tf_op jit(solution)/shard_map/all_to_all | solution.py:310
  141.3 1.3 shard_map.40
  (16 shorter events, 0.3 us)
Async XLA Ops:
  2.6 7.3 %copy-start.3 = (bf16[8,2048]{1,0:T(8,128)(2,1)S(1)}, bf16[8,2048]{1,0:T(8,128)(2,1)}, u32[]{:S(2)}) copy-start(bf16[8,2048]{1,0:T(8,128)(2,1)} %param.4) | copy-start | bytes 98308
  2.6 38.2 %all-to-all-start = ((bf16[8,8,104,128]{3,2,1,0:T(8,128)(2,1)}), bf16[8,8,104,128]{3,2,1,0:T(8,128)(2,1)S(1)}, u32[]{:S(2)}, u32[]{:S(2)}) async-start(bf16[8,8,104,128]{3,2,1,0:T(8,128)(2,1)} %shard_map.37), calls=%async_computation | async-start | bytes 3407872 | tf_op jit(solution)/shard_map/all_to_all | solution.py:304
  9.9 6.5 %collective-permute-start.2 = (bf16[1,8,2048]{2,1,0:T(8,128)(2,1)S(1)}, bf16[1,8,2048]{2,1,0:T(8,128)(2,1)S(1)}, u32[]{:S(2)}, u32[]{:S(2)}) collective-permute-start(bf16[1,8,2048]{2,1,0:T(8,128)(2,1)S(1)} %bitcast.20), channel_id=1, source_target_pairs={{0,12},{4,8},{8,4},{12,0},{16,28},{20,24},{24,20},{28,16},{1,13},{... | collective-permute-start | bytes 98312 | tf_op jit(solution)/shard_map/ppermute | solution.py:262
  14.5 4.8 %collective-permute-start.1 = (bf16[1,8,2048]{2,1,0:T(8,128)(2,1)S(1)}, bf16[1,8,2048]{2,1,0:T(8,128)(2,1)S(1)}, u32[]{:S(2)}, u32[]{:S(2)}) collective-permute-start(bf16[1,8,2048]{2,1,0:T(8,128)(2,1)S(1)} %bitcast.21), channel_id=1, source_target_pairs={{0,8},{4,12},{8,0},{12,4},{16,24},{20,28},{24,16},{28,20},{1,9},{5... | collective-permute-start | bytes 98312 | tf_op jit(solution)/shard_map/ppermute | solution.py:262
  14.5 4.8 %collective-permute-start = (bf16[1,8,2048]{2,1,0:T(8,128)(2,1)S(1)}, bf16[1,8,2048]{2,1,0:T(8,128)(2,1)S(1)}, u32[]{:S(2)}, u32[]{:S(2)}) collective-permute-start(bf16[1,8,2048]{2,1,0:T(8,128)(2,1)S(1)} %bitcast.22), channel_id=1, source_target_pairs={{0,4},{4,0},{8,12},{12,8},{16,20},{20,16},{24,28},{28,24},{1,5},{5... | collective-permute-start | bytes 98312 | tf_op jit(solution)/shard_map/ppermute | solution.py:262
  19.3 8.3 %collective-permute-start.4 = (bf16[4,8,896]{2,1,0:T(8,128)(2,1)S(1)}, bf16[4,8,896]{2,1,0:T(8,128)(2,1)S(1)}, u32[]{:S(2)}, u32[]{:S(2)}) collective-permute-start(bf16[4,8,896]{2,1,0:T(8,128)(2,1)S(1)} %pad_maximum_fusion.5), channel_id=1, source_target_pairs={{0,16},{4,20},{8,24},{12,28},{16,0},{20,4},{24,8},{28,12},{1,17},{... | collective-permute-start | bytes 172040 | tf_op jit(solution)/shard_map/ppermute | solution.py:262
  24.0 9.5 %collective-permute-start.3 = (bf16[4,8,1152]{2,1,0:T(8,128)(2,1)S(1)}, bf16[4,8,1152]{2,1,0:T(8,128)(2,1)S(1)}, u32[]{:S(2)}, u32[]{:S(2)}) collective-permute-start(bf16[4,8,1152]{2,1,0:T(8,128)(2,1)S(1)} %slice.24), channel_id=1, source_target_pairs={{0,16},{4,20},{8,24},{12,28},{16,0},{20,4},{24,8},{28,12},{1,17},{... | collective-permute-start | bytes 221192 | tf_op jit(solution)/shard_map/ppermute | solution.py:262
  33.5 8.7 %collective-permute-start.6 = (bf16[8,8,896]{2,1,0:T(8,128)(2,1)S(1)}, bf16[8,8,896]{2,1,0:T(8,128)(2,1)S(1)}, u32[]{:S(2)}, u32[]{:S(2)}) collective-permute-start(bf16[8,8,896]{2,1,0:T(8,128)(2,1)S(1)} %pad_maximum_fusion.4), channel_id=1, source_target_pairs={{128,98},{130,96},{132,102},{134,100},{136,106},{138,104},{140,110... | collective-permute-start | bytes 344072 | tf_op jit(solution)/shard_map/ppermute | solution.py:279
  37.3 4.9 %collective-permute-start.5 = (bf16[8,8,896]{2,1,0:T(8,128)(2,1)S(1)}, bf16[8,8,896]{2,1,0:T(8,128)(2,1)S(1)}, u32[]{:S(2)}, u32[]{:S(2)}) collective-permute-start(bf16[8,8,896]{2,1,0:T(8,128)(2,1)S(1)} %pad_maximum_fusion.4), channel_id=1, source_target_pairs={{128,96},{130,98},{132,100},{134,102},{136,104},{138,106},{140,108... | collective-permute-start | bytes 344072 | tf_op jit(solution)/shard_map/ppermute | solution.py:279
  39.4 6.5 %collective-permute-start.7 = (bf16[8,8,1152]{2,1,0:T(8,128)(2,1)S(1)}, bf16[8,8,1152]{2,1,0:T(8,128)(2,1)S(1)}, u32[]{:S(2)}, u32[]{:S(2)}) collective-permute-start(bf16[8,8,1152]{2,1,0:T(8,128)(2,1)S(1)} %pad_maximum_fusion.2), channel_id=1, source_target_pairs={{0,2},{2,0},{1,3},{3,1},{4,6},{6,4},{5,7},{7,5},{8,10},{10,8},{9,1... | collective-permute-start | bytes 442376 | tf_op jit(solution)/shard_map/ppermute | solution.py:262
  42.2 39.9 %all-to-all-start.1 = ((bf16[8,8,104,128]{3,2,1,0:T(8,128)(2,1)}), bf16[8,8,104,128]{3,2,1,0:T(8,128)(2,1)S(1)}, u32[]{:S(2)}, u32[]{:S(2)}) async-start(bf16[8,8,104,128]{3,2,1,0:T(8,128)(2,1)} %bitcast.13), calls=%async_computation.1 | async-start | bytes 3407872 | tf_op jit(solution)/shard_map/all_to_all | solution.py:309
  46.1 8.0 %collective-permute-start.10 = (bf16[1,64,1152]{2,1,0:T(8,128)(2,1)S(1)}, bf16[1,64,1152]{2,1,0:T(8,128)(2,1)S(1)}, u32[]{:S(2)}, u32[]{:S(2)}) collective-permute-start(bf16[1,64,1152]{2,1,0:T(8,128)(2,1)S(1)} %bitcast.14), channel_id=1, source_target_pairs={{0,96},{32,64},{64,32},{96,0},{1,97},{33,65},{65,33},{97,1},{2,98}... | collective-permute-start | bytes 442376 | tf_op jit(solution)/shard_map/ppermute | solution.py:262
  46.2 7.9 %collective-permute-start.9 = (bf16[1,64,1152]{2,1,0:T(8,128)(2,1)S(1)}, bf16[1,64,1152]{2,1,0:T(8,128)(2,1)S(1)}, u32[]{:S(2)}, u32[]{:S(2)}) collective-permute-start(bf16[1,64,1152]{2,1,0:T(8,128)(2,1)S(1)} %bitcast.15), channel_id=1, source_target_pairs={{0,64},{32,96},{64,0},{96,32},{1,65},{33,97},{65,1},{97,33},{2,66}... | collective-permute-start | bytes 442376 | tf_op jit(solution)/shard_map/ppermute | solution.py:262
  48.5 6.5 %collective-permute-start.8 = (bf16[1,64,1152]{2,1,0:T(8,128)(2,1)S(1)}, bf16[1,64,1152]{2,1,0:T(8,128)(2,1)S(1)}, u32[]{:S(2)}, u32[]{:S(2)}) collective-permute-start(bf16[1,64,1152]{2,1,0:T(8,128)(2,1)S(1)} %bitcast.16), channel_id=1, source_target_pairs={{0,32},{32,0},{64,96},{96,64},{1,33},{33,1},{65,97},{97,65},{2,34}... | collective-permute-start | bytes 442376 | tf_op jit(solution)/shard_map/ppermute | solution.py:262
  50.3 8.9 %collective-permute-start.11 = (bf16[1,64,1152]{2,1,0:T(8,128)(2,1)S(1)}, bf16[1,64,1152]{2,1,0:T(8,128)(2,1)S(1)}, u32[]{:S(2)}, u32[]{:S(2)}) collective-permute-start(bf16[1,64,1152]{2,1,0:T(8,128)(2,1)S(1)} %bitcast.18), channel_id=1, source_target_pairs={{0,128},{128,0},{1,129},{129,1},{2,130},{130,2},{3,131},{131,3},{4... | collective-permute-start | bytes 442376 | tf_op jit(solution)/shard_map/ppermute | solution.py:262
  55.1 15.4 %collective-permute-start.12 = (bf16[4,64,1152]{2,1,0:T(8,128)(2,1)S(1)}, bf16[4,64,1152]{2,1,0:T(8,128)(2,1)S(1)}, u32[]{:S(2)}, u32[]{:S(2)}) collective-permute-start(bf16[4,64,1152]{2,1,0:T(8,128)(2,1)S(1)} %pad_maximum_fusion.refs_0_), channel_id=1, source_target_pairs={{0,128},{128,0},{1,129},{129,1},{2,130},{130,2},{3,131},{131,3},{4... | collective-permute-start | bytes 1769480 | tf_op jit(solution)/shard_map/ppermute | solution.py:262
  59.3 11.2 %collective-permute-start.15 = (bf16[2,64,1152]{2,1,0:T(8,128)(2,1)S(1)}, bf16[2,64,1152]{2,1,0:T(8,128)(2,1)S(1)}, u32[]{:S(2)}, u32[]{:S(2)}) collective-permute-start(bf16[2,64,1152]{2,1,0:T(8,128)(2,1)S(1)} %pad_maximum_fusion.1.refs_2_), channel_id=1, source_target_pairs={{0,96},{32,64},{64,32},{96,0},{1,97},{33,65},{65,33},{97,1},{2,98}... | collective-permute-start | bytes 884744 | tf_op jit(solution)/shard_map/ppermute | solution.py:262
  61.5 9.5 %collective-permute-start.14 = (bf16[2,64,1152]{2,1,0:T(8,128)(2,1)S(1)}, bf16[2,64,1152]{2,1,0:T(8,128)(2,1)}, u32[]{:S(2)}, u32[]{:S(2)}) collective-permute-start(bf16[2,64,1152]{2,1,0:T(8,128)(2,1)S(1)} %pad_maximum_fusion.1.refs_2_), channel_id=1, source_target_pairs={{0,64},{32,96},{64,0},{96,32},{1,65},{33,97},{65,1},{97,33},{2,66}... | collective-permute-start | bytes 884744 | tf_op jit(solution)/shard_map/ppermute | solution.py:262
  61.5 10.0 %collective-permute-start.13 = (bf16[2,64,1152]{2,1,0:T(8,128)(2,1)S(1)}, bf16[2,64,1152]{2,1,0:T(8,128)(2,1)}, u32[]{:S(2)}, u32[]{:S(2)}) collective-permute-start(bf16[2,64,1152]{2,1,0:T(8,128)(2,1)S(1)} %pad_maximum_fusion.1.refs_2_), channel_id=1, source_target_pairs={{0,32},{32,0},{64,96},{96,64},{1,33},{33,1},{65,97},{97,65},{2,34}... | collective-permute-start | bytes 884744 | tf_op jit(solution)/shard_map/ppermute | solution.py:262
  70.5 1.9 %collective-permute-start.21 = (bf16[2,64,1152]{2,1,0:T(8,128)(2,1)S(1)}, bf16[2,64,1152]{2,1,0:T(8,128)(2,1)S(1)}, u32[]{:S(2)}, u32[]{:S(2)}) collective-permute-start(bf16[2,64,1152]{2,1,0:T(8,128)(2,1)S(1)} %collective-permute-done.15.refs_5_), channel_id=1, source_target_pairs={{0,1},{1,0},{2,3},{3,2},{4,5},{5,4},{6,7},{7,6},{8,9},{9,8},{10,11... | collective-permute-start | bytes 884744 | tf_op jit(solution)/shard_map/ppermute | solution.py:262
  70.5 4.7 %collective-permute-start.16 = (bf16[4,64,1152]{2,1,0:T(8,128)(2,1)S(1)}, bf16[4,64,1152]{2,1,0:T(8,128)(2,1)}, u32[]{:S(2)}, u32[]{:S(2)}) collective-permute-start(bf16[4,64,1152]{2,1,0:T(8,128)(2,1)S(1)} %pad_maximum_fusion.refs_0_), channel_id=1, source_target_pairs={{0,1},{1,0},{2,3},{3,2},{4,5},{5,4},{6,7},{7,6},{8,9},{9,8},{10,11... | collective-permute-start | bytes 1769480 | tf_op jit(solution)/shard_map/ppermute | solution.py:262
  71.0 4.2 %collective-permute-start.17 = (bf16[4,64,1152]{2,1,0:T(8,128)(2,1)S(1)}, bf16[4,64,1152]{2,1,0:T(8,128)(2,1)}, u32[]{:S(2)}, u32[]{:S(2)}) collective-permute-start(bf16[4,64,1152]{2,1,0:T(8,128)(2,1)S(1)} %collective-permute-done.12.refs_1_), channel_id=1, source_target_pairs={{0,1},{1,0},{2,3},{3,2},{4,5},{5,4},{6,7},{7,6},{8,9},{9,8},{10,11... | collective-permute-start | bytes 1769480 | tf_op jit(solution)/shard_map/ppermute | solution.py:262
  71.0 2.8 %collective-permute-start.20 = (bf16[2,64,1152]{2,1,0:T(8,128)(2,1)}, bf16[2,64,1152]{2,1,0:T(8,128)(2,1)}, u32[]{:S(2)}, u32[]{:S(2)}) collective-permute-start(bf16[2,64,1152]{2,1,0:T(8,128)(2,1)} %collective-permute-done.14.refs_4_), channel_id=1, source_target_pairs={{0,1},{1,0},{2,3},{3,2},{4,5},{5,4},{6,7},{7,6},{8,9},{9,8},{10,11... | collective-permute-start | bytes 884744 | tf_op jit(solution)/shard_map/ppermute | solution.py:262
  71.5 3.1 %collective-permute-start.19 = (bf16[2,64,1152]{2,1,0:T(8,128)(2,1)}, bf16[2,64,1152]{2,1,0:T(8,128)(2,1)}, u32[]{:S(2)}, u32[]{:S(2)}) collective-permute-start(bf16[2,64,1152]{2,1,0:T(8,128)(2,1)} %collective-permute-done.13.refs_3_), channel_id=1, source_target_pairs={{0,1},{1,0},{2,3},{3,2},{4,5},{5,4},{6,7},{7,6},{8,9},{9,8},{10,11... | collective-permute-start | bytes 884744 | tf_op jit(solution)/shard_map/ppermute | solution.py:262
  72.4 0.7 copy-start
  73.1 2.0 %collective-permute-start.18 = (bf16[2,64,1152]{2,1,0:T(8,128)(2,1)S(1)}, bf16[2,64,1152]{2,1,0:T(8,128)(2,1)}, u32[]{:S(2)}, u32[]{:S(2)}) collective-permute-start(bf16[2,64,1152]{2,1,0:T(8,128)(2,1)S(1)} %pad_maximum_fusion.1.refs_2_), channel_id=1, source_target_pairs={{0,1},{1,0},{2,3},{3,2},{4,5},{5,4},{6,7},{7,6},{8,9},{9,8},{10,11... | collective-permute-start | bytes 884744 | tf_op jit(solution)/shard_map/ppermute | solution.py:262
  73.2 8.9 %copy-start.2 = (s32[16]{0:T(128)S(1)}, s32[16]{0:T(128)}, u32[]{:S(2)}) copy-start(s32[16]{0:T(128)} %locked_ref.1) | copy-start | bytes 196
  75.1 1.0 copy-start.1

commit v7 on v6

--- a/solution.py
+++ b/solution.py
@@ -295,7 +295,7 @@
     a = jnp.concatenate([a] + [exchange(a, "x", 4, dx) for dx in (1, 2, 3)])
     far_a = exchange(a, "yh", 2, 1)
     far_b = [exchange(b, "x", 4, dx) for dx in (1, 2, 3)]
-    a, b, far_a = lax.optimization_barrier((a, b, far_a))
+    a, b, far_b[2] = lax.optimization_barrier((a, b, far_b[2]))
     own = [a, far_a, b] + far_b
     return own + [exchange(panel, "c", 2, 1) for panel in own]
 

time: 143 us -> 144 us (level)
  no operation moved by 1% of the time
where the time goes in v7:
time: 144 us; the launch traced here: 143 us
  blocking collectives  54.7 us (38%)
  starting transfers between devices  46.4 us (32%)
  waiting for transfers between devices  25.3 us (18%)
  Pallas kernels  13.1 us (9%)
  local copies, waits for them, and re-layouts  3.28 us (2%)
    all_to_all x1, blocking collectives, body(): lax.all_to_all(rotate(locked, received, matrix), ('x', 'zl', 'yh', 'zh'),...  54.7 us
    ppermute x20, starting transfers between devices, exchange(): return lax.ppermute(value, axis, [(i, i ^ mask) for i in range(size)])  29.7 us
    ppermute x20, waiting for transfers between devices, exchange(): return lax.ppermute(value, axis, [(i, i ^ mask) for i in range(size)])  23.4 us
    all_to_all x1, starting transfers between devices, body(): lax.all_to_all(pack(vectors), ('yh', 'x'), split_axis=0, concat_axis=0, t...  7.28 us
    ppermute x2, starting transfers between devices, gather_panels(): guests = [lax.ppermute(spare, EIG + ('yl',), pair) for pair in pairs]  5.87 us
    pallas_call x1, Pallas kernels, rotate(): pl.pallas_call(rotate_kernel, in_specs=[pl.BlockSpec(memory_space=pltpu.S...  5.26 us
    pallas_call x1, Pallas kernels, place_panels(): pl.pallas_call(place_kernel, in_specs=[pl.BlockSpec(memory_space=pltpu.SM...  3.96 us
    all_to_all x1, starting transfers between devices, body(): lax.all_to_all(halfway.transpose(1, 0, 2, 3), ('zl', 'zh'), split_axis=0,...  3.59 us
  transfers between devices with their start and end apart: 24, of which 12 were waited for; matrix products, arithmetic and copies ran while one was open for 1% of the time, Pallas kernels for 3%

profile of v7, /device:TPU:16, one launch (start us, length us, event | category | flops | bytes accessed | tf_op | source)
XLA Modules:
  0.0 143.5 jit_solution(12977392245485187492)
XLA Ops:
  0.0 2.6 %shard_map.37 = bf16[8,8,104,128]{3,2,1,0:T(8,128)(2,1)} custom-call(bf16[32,25600]{1,0:T(8,128)(2,1)} %source_ref.1), custom_call_target="tpu_custom_call" | custom-call | tf_op jit(solution)/shard_map/pallas_call | solution.py:87
  2.6 0.0 copy-start.3
  2.6 7.3 %all-to-all-start = ((bf16[8,8,104,128]{3,2,1,0:T(8,128)(2,1)}), bf16[8,8,104,128]{3,2,1,0:T(8,128)(2,1)S(1)}, u32[]{:S(2)}, u32[]{:S(2)}) async-start(bf16[8,8,104,128]{3,2,1,0:T(8,128)(2,1)} %shard_map.37), calls=%async_computation | async-start | bytes 3407872 | tf_op jit(solution)/shard_map/all_to_all | solution.py:304
  9.9 0.0 copy-done.3
  9.9 4.6 %collective-permute-start.2 = (bf16[1,8,2048]{2,1,0:T(8,128)(2,1)S(1)}, bf16[1,8,2048]{2,1,0:T(8,128)(2,1)S(1)}, u32[]{:S(2)}, u32[]{:S(2)}) collective-permute-start(bf16[1,8,2048]{2,1,0:T(8,128)(2,1)S(1)} %bitcast.20), channel_id=1, source_target_pairs={{0,12},{4,8},{8,4},{12,0},{16,28},{20,24},{24,20},{28,16},{1,13},{... | collective-permute-start | bytes 98312 | tf_op jit(solution)/shard_map/ppermute | solution.py:262
  14.5 0.0 collective-permute-start.1
  14.5 0.7 collective-permute-start
  15.1 1.3 collective-permute-done.2
  16.4 2.9 %collective-permute-done.1 = bf16[1,8,2048]{2,1,0:T(8,128)(2,1)S(1)} collective-permute-done((bf16[1,8,2048]{2,1,0:T(8,128)(2,1)S(1)}, bf16[1,8,2048]{2,1,0:T(8,128)(2,1)S(1)}, u32[]{:S(2)}, u32[]{:S(2)}) %collective-permute-start.1) | collective-permute-done | bytes 32800 | tf_op jit(solution)/shard_map/ppermute | solution.py:262
  19.3 0.0 collective-permute-done
  19.3 4.6 %collective-permute-start.4 = (bf16[4,8,896]{2,1,0:T(8,128)(2,1)S(1)}, bf16[4,8,896]{2,1,0:T(8,128)(2,1)S(1)}, u32[]{:S(2)}, u32[]{:S(2)}) collective-permute-start(bf16[4,8,896]{2,1,0:T(8,128)(2,1)S(1)} %pad_maximum_fusion.5), channel_id=1, source_target_pairs={{0,16},{4,20},{8,24},{12,28},{16,0},{20,4},{24,8},{28,12},{1,17},{... | collective-permute-start | bytes 172040 | tf_op jit(solution)/shard_map/ppermute | solution.py:262
  24.0 1.5 %collective-permute-start.3 = (bf16[4,8,1152]{2,1,0:T(8,128)(2,1)S(1)}, bf16[4,8,1152]{2,1,0:T(8,128)(2,1)S(1)}, u32[]{:S(2)}, u32[]{:S(2)}) collective-permute-start(bf16[4,8,1152]{2,1,0:T(8,128)(2,1)S(1)} %slice.24), channel_id=1, source_target_pairs={{0,16},{4,20},{8,24},{12,28},{16,0},{20,4},{24,8},{28,12},{1,17},{... | collective-permute-start | bytes 221192 | tf_op jit(solution)/shard_map/ppermute | solution.py:262
  25.5 2.1 %collective-permute-done.4 = bf16[4,8,896]{2,1,0:T(8,128)(2,1)S(1)} collective-permute-done((bf16[4,8,896]{2,1,0:T(8,128)(2,1)S(1)}, bf16[4,8,896]{2,1,0:T(8,128)(2,1)S(1)}, u32[]{:S(2)}, u32[]{:S(2)}) %collective-permute-start.4) | collective-permute-done | bytes 57376 | tf_op jit(solution)/shard_map/ppermute | solution.py:262
  27.6 5.8 %collective-permute-done.3 = bf16[4,8,1152]{2,1,0:T(8,128)(2,1)S(1)} collective-permute-done((bf16[4,8,1152]{2,1,0:T(8,128)(2,1)S(1)}, bf16[4,8,1152]{2,1,0:T(8,128)(2,1)S(1)}, u32[]{:S(2)}, u32[]{:S(2)}) %collective-permute-start.3) | collective-permute-done | bytes 73760 | tf_op jit(solution)/shard_map/ppermute | solution.py:262
  33.5 3.8 %collective-permute-start.6 = (bf16[8,8,896]{2,1,0:T(8,128)(2,1)S(1)}, bf16[8,8,896]{2,1,0:T(8,128)(2,1)S(1)}, u32[]{:S(2)}, u32[]{:S(2)}) collective-permute-start(bf16[8,8,896]{2,1,0:T(8,128)(2,1)S(1)} %pad_maximum_fusion.4), channel_id=1, source_target_pairs={{128,98},{130,96},{132,102},{134,100},{136,106},{138,104},{140,110... | collective-permute-start | bytes 344072 | tf_op jit(solution)/shard_map/ppermute | solution.py:279
  37.3 2.1 %collective-permute-start.5 = (bf16[8,8,896]{2,1,0:T(8,128)(2,1)S(1)}, bf16[8,8,896]{2,1,0:T(8,128)(2,1)S(1)}, u32[]{:S(2)}, u32[]{:S(2)}) collective-permute-start(bf16[8,8,896]{2,1,0:T(8,128)(2,1)S(1)} %pad_maximum_fusion.4), channel_id=1, source_target_pairs={{128,96},{130,98},{132,100},{134,102},{136,104},{138,106},{140,108... | collective-permute-start | bytes 344072 | tf_op jit(solution)/shard_map/ppermute | solution.py:279
  39.4 1.4 collective-permute-start.7
  40.8 0.0 all-to-all-done
  40.8 1.4 copy.11
  42.2 0.0 collective-permute-done.6
  42.2 0.0 collective-permute-done.5
  42.2 3.6 %all-to-all-start.1 = ((bf16[8,8,104,128]{3,2,1,0:T(8,128)(2,1)}), bf16[8,8,104,128]{3,2,1,0:T(8,128)(2,1)S(1)}, u32[]{:S(2)}, u32[]{:S(2)}) async-start(bf16[8,8,104,128]{3,2,1,0:T(8,128)(2,1)} %bitcast.13), calls=%async_computation.1 | async-start | bytes 3407872 | tf_op jit(solution)/shard_map/all_to_all | solution.py:309
  46.0 0.0 collective-permute-done.7
  46.0 0.1 fusion.1
  46.1 0.1 collective-permute-start.10
  46.2 2.3 %collective-permute-start.9 = (bf16[1,64,1152]{2,1,0:T(8,128)(2,1)S(1)}, bf16[1,64,1152]{2,1,0:T(8,128)(2,1)S(1)}, u32[]{:S(2)}, u32[]{:S(2)}) collective-permute-start(bf16[1,64,1152]{2,1,0:T(8,128)(2,1)S(1)} %bitcast.15), channel_id=1, source_target_pairs={{0,64},{32,96},{64,0},{96,32},{1,65},{33,97},{65,1},{97,33},{2,66}... | collective-permute-start | bytes 442376 | tf_op jit(solution)/shard_map/ppermute | solution.py:262
  48.5 1.8 %collective-permute-start.8 = (bf16[1,64,1152]{2,1,0:T(8,128)(2,1)S(1)}, bf16[1,64,1152]{2,1,0:T(8,128)(2,1)S(1)}, u32[]{:S(2)}, u32[]{:S(2)}) collective-permute-start(bf16[1,64,1152]{2,1,0:T(8,128)(2,1)S(1)} %bitcast.16), channel_id=1, source_target_pairs={{0,32},{32,0},{64,96},{96,64},{1,33},{33,1},{65,97},{97,65},{2,34}... | collective-permute-start | bytes 442376 | tf_op jit(solution)/shard_map/ppermute | solution.py:262
  50.3 3.1 %collective-permute-start.11 = (bf16[1,64,1152]{2,1,0:T(8,128)(2,1)S(1)}, bf16[1,64,1152]{2,1,0:T(8,128)(2,1)S(1)}, u32[]{:S(2)}, u32[]{:S(2)}) collective-permute-start(bf16[1,64,1152]{2,1,0:T(8,128)(2,1)S(1)} %bitcast.18), channel_id=1, source_target_pairs={{0,128},{128,0},{1,129},{129,1},{2,130},{130,2},{3,131},{131,3},{4... | collective-permute-start | bytes 442376 | tf_op jit(solution)/shard_map/ppermute | solution.py:262
  53.5 0.7 collective-permute-done.10
  54.1 0.0 collective-permute-done.9
  54.1 0.9 collective-permute-done.8
  55.0 0.1 pad_maximum_fusion.refs_0_
  55.1 4.1 %collective-permute-start.13 = (bf16[4,64,1152]{2,1,0:T(8,128)(2,1)S(1)}, bf16[4,64,1152]{2,1,0:T(8,128)(2,1)S(1)}, u32[]{:S(2)}, u32[]{:S(2)}) collective-permute-start(bf16[4,64,1152]{2,1,0:T(8,128)(2,1)S(1)} %pad_maximum_fusion.refs_0_), channel_id=1, source_target_pairs={{0,128},{128,0},{1,129},{129,1},{2,130},{130,2},{3,131},{131,3},{4... | collective-permute-start | bytes 1769480 | tf_op jit(solution)/shard_map/ppermute | solution.py:262
  59.2 0.0 collective-permute-done.11
  59.3 2.6 %collective-permute-start.15 = (bf16[2,64,1152]{2,1,0:T(8,128)(2,1)S(1)}, bf16[2,64,1152]{2,1,0:T(8,128)(2,1)S(1)}, u32[]{:S(2)}, u32[]{:S(2)}) collective-permute-start(bf16[2,64,1152]{2,1,0:T(8,128)(2,1)S(1)} %pad_maximum_fusion.1.refs_2_), channel_id=1, source_target_pairs={{0,64},{32,96},{64,0},{96,32},{1,65},{33,97},{65,1},{97,33},{2,66}... | collective-permute-start | bytes 884744 | tf_op jit(solution)/shard_map/ppermute | solution.py:262
  61.9 1.1 collective-permute-start.12
  63.0 0.8 collective-permute-start.14
  63.7 3.9 %collective-permute-done.15.refs_4_ = bf16[2,64,1152]{2,1,0:T(8,128)(2,1)S(1)} collective-permute-done((bf16[2,64,1152]{2,1,0:T(8,128)(2,1)S(1)}, bf16[2,64,1152]{2,1,0:T(8,128)(2,1)S(1)}, u32[]{:S(2)}, u32[]{:S(2)}) %collective-permute-start.15) | collective-permute-done | bytes 294944 | tf_op jit(solution)/shard_map/ppermute | solution.py:262
  67.7 0.0 collective-permute-start.20
  67.7 3.2 %collective-permute-done.12.refs_5_ = bf16[2,64,1152]{2,1,0:T(8,128)(2,1)} collective-permute-done((bf16[2,64,1152]{2,1,0:T(8,128)(2,1)S(1)}, bf16[2,64,1152]{2,1,0:T(8,128)(2,1)}, u32[]{:S(2)}, u32[]{:S(2)}) %collective-permute-start.12) | collective-permute-done | bytes 294944 | tf_op jit(solution)/shard_map/ppermute | solution.py:262
  70.8 0.0 collective-permute-start.16
  70.8 0.0 collective-permute-done.13.refs_1_
  70.8 0.5 collective-permute-start.17
  71.4 0.0 collective-permute-start.18
  71.4 0.4 collective-permute-done.14.refs_3_
  71.7 0.1 collective-permute-start.19
  71.9 0.0 collective-permute-done.20.refs_10_
  71.9 0.0 copy-start
  71.9 0.7 copy-done
  72.6 0.4 collective-permute-start.21
  73.0 0.0 copy-start.2
  73.0 0.1 pad_add_fusion.place_ref
  73.1 1.8 %collective-permute-done.19.refs_9_ = bf16[2,64,1152]{2,1,0:T(8,128)(2,1)} collective-permute-done((bf16[2,64,1152]{2,1,0:T(8,128)(2,1)}, bf16[2,64,1152]{2,1,0:T(8,128)(2,1)}, u32[]{:S(2)}, u32[]{:S(2)}) %collective-permute-start.19) | collective-permute-done | bytes 294944 | tf_op jit(solution)/shard_map/ppermute | solution.py:262
  74.9 0.0 collective-permute-done.18.refs_8_
  74.9 0.4 collective-permute-done.21.refs_11_
  75.3 0.0 collective-permute-done.16.refs_6_
  75.3 0.0 collective-permute-done.17.refs_7_
  75.3 1.0 copy-done.1
  76.3 4.0 %shard_map.38.source_ref = bf16[64,32,1152]{2,1,0:T(8,128)(2,1)} custom-call(s32[4]{0:T(128)S(1)} %pad_add_fusion.place_ref, bf16[4,64,1152]{2,1,0:T(8,128)(2,1)S(1)} %pad_maximum_fusion.refs_0_, bf16[4,64,1152]{2,1,0:T(8,128)(2,1)S(1)} %collective-permute-done.13.refs_1_, bf16[2,64,1152]{2,1,0:T(8,128)(2,1)S(1)} %pad_maximum_fusion.1.refs_2_, ...), custom_call_target="tpu_custom_call" | custom-call | tf_op jit(solution)/shard_map/pallas_call | solution.py:178
  80.2 1.9 %all-to-all-done.1.in_ref = bf16[8,8,104,128]{3,2,1,0:T(8,128)(2,1)S(1)} async-done(((bf16[8,8,104,128]{3,2,1,0:T(8,128)(2,1)}), bf16[8,8,104,128]{3,2,1,0:T(8,128)(2,1)S(1)}, u32[]{:S(2)}, u32[]{:S(2)}) %all-to-all-start.1) | async-done | bytes 1703968 | tf_op jit(solution)/shard_map/all_to_all | solution.py:309
  82.1 0.0 copy-done.2
  82.1 5.3 %shard_map.39 = bf16[64,104,128]{2,1,0:T(8,128)(2,1)S(1)} custom-call(s32[16]{0:T(128)S(1)} %copy-done.2, bf16[8,8,104,128]{3,2,1,0:T(8,128)(2,1)S(1)} %all-to-all-done.1.in_ref, bf16[64,32,1152]{2,1,0:T(8,128)(2,1)} %shard_map.38.source_ref), custom_call_target="tpu_custom_call" | custom-call | tf_op jit(solution)/shard_map/pallas_call | solution.py:247
  87.4 54.7 %all_to_all.15.in_ref = bf16[64,104,128]{2,1,0:T(8,128)(2,1)S(1)} all-to-all(bf16[64,104,128]{2,1,0:T(8,128)(2,1)S(1)} %shard_map.39), channel_id=1, replica_groups=mesh['yh'=2,'x'=4,'zh'=2,'zl'=4,'yl'=2,'c'=2] {'x','zl','yh','zh'}, dimensions={0} | all-to-all | bytes 3407872 | tf_op jit(solution)/shard_map/all_to_all | solution.py:310
  142.0 1.3 shard_map.40
  (16 shorter events, 0.3 us)
Async XLA Ops:
  2.6 7.3 %copy-start.3 = (bf16[8,2048]{1,0:T(8,128)(2,1)S(1)}, bf16[8,2048]{1,0:T(8,128)(2,1)}, u32[]{:S(2)}) copy-start(bf16[8,2048]{1,0:T(8,128)(2,1)} %param.4) | copy-start | bytes 98308
  2.6 38.2 %all-to-all-start = ((bf16[8,8,104,128]{3,2,1,0:T(8,128)(2,1)}), bf16[8,8,104,128]{3,2,1,0:T(8,128)(2,1)S(1)}, u32[]{:S(2)}, u32[]{:S(2)}) async-start(bf16[8,8,104,128]{3,2,1,0:T(8,128)(2,1)} %shard_map.37), calls=%async_computation | async-start | bytes 3407872 | tf_op jit(solution)/shard_map/all_to_all | solution.py:304
  9.9 6.5 %collective-permute-start.2 = (bf16[1,8,2048]{2,1,0:T(8,128)(2,1)S(1)}, bf16[1,8,2048]{2,1,0:T(8,128)(2,1)S(1)}, u32[]{:S(2)}, u32[]{:S(2)}) collective-permute-start(bf16[1,8,2048]{2,1,0:T(8,128)(2,1)S(1)} %bitcast.20), channel_id=1, source_target_pairs={{0,12},{4,8},{8,4},{12,0},{16,28},{20,24},{24,20},{28,16},{1,13},{... | collective-permute-start | bytes 98312 | tf_op jit(solution)/shard_map/ppermute | solution.py:262
  14.5 4.8 %collective-permute-start.1 = (bf16[1,8,2048]{2,1,0:T(8,128)(2,1)S(1)}, bf16[1,8,2048]{2,1,0:T(8,128)(2,1)S(1)}, u32[]{:S(2)}, u32[]{:S(2)}) collective-permute-start(bf16[1,8,2048]{2,1,0:T(8,128)(2,1)S(1)} %bitcast.21), channel_id=1, source_target_pairs={{0,8},{4,12},{8,0},{12,4},{16,24},{20,28},{24,16},{28,20},{1,9},{5... | collective-permute-start | bytes 98312 | tf_op jit(solution)/shard_map/ppermute | solution.py:262
  14.5 4.8 %collective-permute-start = (bf16[1,8,2048]{2,1,0:T(8,128)(2,1)S(1)}, bf16[1,8,2048]{2,1,0:T(8,128)(2,1)S(1)}, u32[]{:S(2)}, u32[]{:S(2)}) collective-permute-start(bf16[1,8,2048]{2,1,0:T(8,128)(2,1)S(1)} %bitcast.22), channel_id=1, source_target_pairs={{0,4},{4,0},{8,12},{12,8},{16,20},{20,16},{24,28},{28,24},{1,5},{5... | collective-permute-start | bytes 98312 | tf_op jit(solution)/shard_map/ppermute | solution.py:262
  19.3 8.3 %collective-permute-start.4 = (bf16[4,8,896]{2,1,0:T(8,128)(2,1)S(1)}, bf16[4,8,896]{2,1,0:T(8,128)(2,1)S(1)}, u32[]{:S(2)}, u32[]{:S(2)}) collective-permute-start(bf16[4,8,896]{2,1,0:T(8,128)(2,1)S(1)} %pad_maximum_fusion.5), channel_id=1, source_target_pairs={{0,16},{4,20},{8,24},{12,28},{16,0},{20,4},{24,8},{28,12},{1,17},{... | collective-permute-start | bytes 172040 | tf_op jit(solution)/shard_map/ppermute | solution.py:262
  24.0 9.5 %collective-permute-start.3 = (bf16[4,8,1152]{2,1,0:T(8,128)(2,1)S(1)}, bf16[4,8,1152]{2,1,0:T(8,128)(2,1)S(1)}, u32[]{:S(2)}, u32[]{:S(2)}) collective-permute-start(bf16[4,8,1152]{2,1,0:T(8,128)(2,1)S(1)} %slice.24), channel_id=1, source_target_pairs={{0,16},{4,20},{8,24},{12,28},{16,0},{20,4},{24,8},{28,12},{1,17},{... | collective-permute-start | bytes 221192 | tf_op jit(solution)/shard_map/ppermute | solution.py:262
  33.5 8.7 %collective-permute-start.6 = (bf16[8,8,896]{2,1,0:T(8,128)(2,1)S(1)}, bf16[8,8,896]{2,1,0:T(8,128)(2,1)S(1)}, u32[]{:S(2)}, u32[]{:S(2)}) collective-permute-start(bf16[8,8,896]{2,1,0:T(8,128)(2,1)S(1)} %pad_maximum_fusion.4), channel_id=1, source_target_pairs={{128,98},{130,96},{132,102},{134,100},{136,106},{138,104},{140,110... | collective-permute-start | bytes 344072 | tf_op jit(solution)/shard_map/ppermute | solution.py:279
  37.3 4.9 %collective-permute-start.5 = (bf16[8,8,896]{2,1,0:T(8,128)(2,1)S(1)}, bf16[8,8,896]{2,1,0:T(8,128)(2,1)S(1)}, u32[]{:S(2)}, u32[]{:S(2)}) collective-permute-start(bf16[8,8,896]{2,1,0:T(8,128)(2,1)S(1)} %pad_maximum_fusion.4), channel_id=1, source_target_pairs={{128,96},{130,98},{132,100},{134,102},{136,104},{138,106},{140,108... | collective-permute-start | bytes 344072 | tf_op jit(solution)/shard_map/ppermute | solution.py:279
  39.4 6.5 %collective-permute-start.7 = (bf16[8,8,1152]{2,1,0:T(8,128)(2,1)S(1)}, bf16[8,8,1152]{2,1,0:T(8,128)(2,1)S(1)}, u32[]{:S(2)}, u32[]{:S(2)}) collective-permute-start(bf16[8,8,1152]{2,1,0:T(8,128)(2,1)S(1)} %pad_maximum_fusion.2), channel_id=1, source_target_pairs={{0,2},{2,0},{1,3},{3,1},{4,6},{6,4},{5,7},{7,5},{8,10},{10,8},{9,1... | collective-permute-start | bytes 442376 | tf_op jit(solution)/shard_map/ppermute | solution.py:262
  42.2 39.9 %all-to-all-start.1 = ((bf16[8,8,104,128]{3,2,1,0:T(8,128)(2,1)}), bf16[8,8,104,128]{3,2,1,0:T(8,128)(2,1)S(1)}, u32[]{:S(2)}, u32[]{:S(2)}) async-start(bf16[8,8,104,128]{3,2,1,0:T(8,128)(2,1)} %bitcast.13), calls=%async_computation.1 | async-start | bytes 3407872 | tf_op jit(solution)/shard_map/all_to_all | solution.py:309
  46.1 8.0 %collective-permute-start.10 = (bf16[1,64,1152]{2,1,0:T(8,128)(2,1)S(1)}, bf16[1,64,1152]{2,1,0:T(8,128)(2,1)S(1)}, u32[]{:S(2)}, u32[]{:S(2)}) collective-permute-start(bf16[1,64,1152]{2,1,0:T(8,128)(2,1)S(1)} %bitcast.14), channel_id=1, source_target_pairs={{0,96},{32,64},{64,32},{96,0},{1,97},{33,65},{65,33},{97,1},{2,98}... | collective-permute-start | bytes 442376 | tf_op jit(solution)/shard_map/ppermute | solution.py:262
  46.2 7.9 %collective-permute-start.9 = (bf16[1,64,1152]{2,1,0:T(8,128)(2,1)S(1)}, bf16[1,64,1152]{2,1,0:T(8,128)(2,1)S(1)}, u32[]{:S(2)}, u32[]{:S(2)}) collective-permute-start(bf16[1,64,1152]{2,1,0:T(8,128)(2,1)S(1)} %bitcast.15), channel_id=1, source_target_pairs={{0,64},{32,96},{64,0},{96,32},{1,65},{33,97},{65,1},{97,33},{2,66}... | collective-permute-start | bytes 442376 | tf_op jit(solution)/shard_map/ppermute | solution.py:262
  48.5 6.5 %collective-permute-start.8 = (bf16[1,64,1152]{2,1,0:T(8,128)(2,1)S(1)}, bf16[1,64,1152]{2,1,0:T(8,128)(2,1)S(1)}, u32[]{:S(2)}, u32[]{:S(2)}) collective-permute-start(bf16[1,64,1152]{2,1,0:T(8,128)(2,1)S(1)} %bitcast.16), channel_id=1, source_target_pairs={{0,32},{32,0},{64,96},{96,64},{1,33},{33,1},{65,97},{97,65},{2,34}... | collective-permute-start | bytes 442376 | tf_op jit(solution)/shard_map/ppermute | solution.py:262
  50.3 8.9 %collective-permute-start.11 = (bf16[1,64,1152]{2,1,0:T(8,128)(2,1)S(1)}, bf16[1,64,1152]{2,1,0:T(8,128)(2,1)S(1)}, u32[]{:S(2)}, u32[]{:S(2)}) collective-permute-start(bf16[1,64,1152]{2,1,0:T(8,128)(2,1)S(1)} %bitcast.18), channel_id=1, source_target_pairs={{0,128},{128,0},{1,129},{129,1},{2,130},{130,2},{3,131},{131,3},{4... | collective-permute-start | bytes 442376 | tf_op jit(solution)/shard_map/ppermute | solution.py:262
  55.1 15.8 %collective-permute-start.13 = (bf16[4,64,1152]{2,1,0:T(8,128)(2,1)S(1)}, bf16[4,64,1152]{2,1,0:T(8,128)(2,1)S(1)}, u32[]{:S(2)}, u32[]{:S(2)}) collective-permute-start(bf16[4,64,1152]{2,1,0:T(8,128)(2,1)S(1)} %pad_maximum_fusion.refs_0_), channel_id=1, source_target_pairs={{0,128},{128,0},{1,129},{129,1},{2,130},{130,2},{3,131},{131,3},{4... | collective-permute-start | bytes 1769480 | tf_op jit(solution)/shard_map/ppermute | solution.py:262
  59.3 8.4 %collective-permute-start.15 = (bf16[2,64,1152]{2,1,0:T(8,128)(2,1)S(1)}, bf16[2,64,1152]{2,1,0:T(8,128)(2,1)S(1)}, u32[]{:S(2)}, u32[]{:S(2)}) collective-permute-start(bf16[2,64,1152]{2,1,0:T(8,128)(2,1)S(1)} %pad_maximum_fusion.1.refs_2_), channel_id=1, source_target_pairs={{0,64},{32,96},{64,0},{96,32},{1,65},{33,97},{65,1},{97,33},{2,66}... | collective-permute-start | bytes 884744 | tf_op jit(solution)/shard_map/ppermute | solution.py:262
  61.9 9.0 %collective-permute-start.12 = (bf16[2,64,1152]{2,1,0:T(8,128)(2,1)S(1)}, bf16[2,64,1152]{2,1,0:T(8,128)(2,1)}, u32[]{:S(2)}, u32[]{:S(2)}) collective-permute-start(bf16[2,64,1152]{2,1,0:T(8,128)(2,1)S(1)} %pad_maximum_fusion.1.refs_2_), channel_id=1, source_target_pairs={{0,96},{32,64},{64,32},{96,0},{1,97},{33,65},{65,33},{97,1},{2,98}... | collective-permute-start | bytes 884744 | tf_op jit(solution)/shard_map/ppermute | solution.py:262
  63.0 8.8 %collective-permute-start.14 = (bf16[2,64,1152]{2,1,0:T(8,128)(2,1)S(1)}, bf16[2,64,1152]{2,1,0:T(8,128)(2,1)}, u32[]{:S(2)}, u32[]{:S(2)}) collective-permute-start(bf16[2,64,1152]{2,1,0:T(8,128)(2,1)S(1)} %pad_maximum_fusion.1.refs_2_), channel_id=1, source_target_pairs={{0,32},{32,0},{64,96},{96,64},{1,33},{33,1},{65,97},{97,65},{2,34}... | collective-permute-start | bytes 884744 | tf_op jit(solution)/shard_map/ppermute | solution.py:262
  67.7 4.2 %collective-permute-start.20 = (bf16[2,64,1152]{2,1,0:T(8,128)(2,1)S(1)}, bf16[2,64,1152]{2,1,0:T(8,128)(2,1)S(1)}, u32[]{:S(2)}, u32[]{:S(2)}) collective-permute-start(bf16[2,64,1152]{2,1,0:T(8,128)(2,1)S(1)} %collective-permute-done.15.refs_4_), channel_id=1, source_target_pairs={{0,1},{1,0},{2,3},{3,2},{4,5},{5,4},{6,7},{7,6},{8,9},{9,8},{10,11... | collective-permute-start | bytes 884744 | tf_op jit(solution)/shard_map/ppermute | solution.py:262
  70.8 4.5 %collective-permute-start.16 = (bf16[4,64,1152]{2,1,0:T(8,128)(2,1)S(1)}, bf16[4,64,1152]{2,1,0:T(8,128)(2,1)}, u32[]{:S(2)}, u32[]{:S(2)}) collective-permute-start(bf16[4,64,1152]{2,1,0:T(8,128)(2,1)S(1)} %pad_maximum_fusion.refs_0_), channel_id=1, source_target_pairs={{0,1},{1,0},{2,3},{3,2},{4,5},{5,4},{6,7},{7,6},{8,9},{9,8},{10,11... | collective-permute-start | bytes 1769480 | tf_op jit(solution)/shard_map/ppermute | solution.py:262
  70.8 4.5 %collective-permute-start.17 = (bf16[4,64,1152]{2,1,0:T(8,128)(2,1)S(1)}, bf16[4,64,1152]{2,1,0:T(8,128)(2,1)}, u32[]{:S(2)}, u32[]{:S(2)}) collective-permute-start(bf16[4,64,1152]{2,1,0:T(8,128)(2,1)S(1)} %collective-permute-done.13.refs_1_), channel_id=1, source_target_pairs={{0,1},{1,0},{2,3},{3,2},{4,5},{5,4},{6,7},{7,6},{8,9},{9,8},{10,11... | collective-permute-start | bytes 1769480 | tf_op jit(solution)/shard_map/ppermute | solution.py:262
  71.4 3.5 %collective-permute-start.18 = (bf16[2,64,1152]{2,1,0:T(8,128)(2,1)S(1)}, bf16[2,64,1152]{2,1,0:T(8,128)(2,1)}, u32[]{:S(2)}, u32[]{:S(2)}) collective-permute-start(bf16[2,64,1152]{2,1,0:T(8,128)(2,1)S(1)} %pad_maximum_fusion.1.refs_2_), channel_id=1, source_target_pairs={{0,1},{1,0},{2,3},{3,2},{4,5},{5,4},{6,7},{7,6},{8,9},{9,8},{10,11... | collective-permute-start | bytes 884744 | tf_op jit(solution)/shard_map/ppermute | solution.py:262
  71.7 3.1 %collective-permute-start.19 = (bf16[2,64,1152]{2,1,0:T(8,128)(2,1)}, bf16[2,64,1152]{2,1,0:T(8,128)(2,1)}, u32[]{:S(2)}, u32[]{:S(2)}) collective-permute-start(bf16[2,64,1152]{2,1,0:T(8,128)(2,1)} %collective-permute-done.14.refs_3_), channel_id=1, source_target_pairs={{0,1},{1,0},{2,3},{3,2},{4,5},{5,4},{6,7},{7,6},{8,9},{9,8},{10,11... | collective-permute-start | bytes 884744 | tf_op jit(solution)/shard_map/ppermute | solution.py:262
  71.9 0.7 copy-start
  72.6 2.7 %collective-permute-start.21 = (bf16[2,64,1152]{2,1,0:T(8,128)(2,1)}, bf16[2,64,1152]{2,1,0:T(8,128)(2,1)}, u32[]{:S(2)}, u32[]{:S(2)}) collective-permute-start(bf16[2,64,1152]{2,1,0:T(8,128)(2,1)} %collective-permute-done.12.refs_5_), channel_id=1, source_target_pairs={{0,1},{1,0},{2,3},{3,2},{4,5},{5,4},{6,7},{7,6},{8,9},{9,8},{10,11... | collective-permute-start | bytes 884744 | tf_op jit(solution)/shard_map/ppermute | solution.py:262
  73.0 9.1 %copy-start.2 = (s32[16]{0:T(128)S(1)}, s32[16]{0:T(128)}, u32[]{:S(2)}) copy-start(s32[16]{0:T(128)} %locked_ref.1) | copy-start | bytes 196
  75.3 1.0 copy-start.1
